TPU v7x, 512 devices: a whole 4x8x8 slice. The times are simulated.
512 devices in a mesh: chan: 16 (over y, core), tm: 32 (over z, x).
Axes of the slice: x: 4, y: 8, z: 8, core: 2. Of those that a mesh axis runs over, the one named last changes fastest.
Arguments:
- strain: bfloat16 [32, 64, 128, 1024], P('tm', 'chan'), may hold values from -60 to 60, as said below
- pair_slots: int32 [192, 2], P('chan'), may hold values from -1 to 63, as said below
Outputs:
- coherence: float32 [128, 192, 256], P('tm', 'chan')
Inputs may be any that keep to these rules, and one draw needn't show every extreme that they name: `strain`: samples of one channel share a scale; values stay within the range. `pair_slots`: row s belongs to owner s // 12; a live slot holds blocks a <= b with b - a <= 8, both within 8 blocks of the owner's own blocks (owner o holds blocks o * 4 to o * 4 + 3); an empty slot holds -1, -1. Each owner's live slots come first and number 2 to 12; in every draw one owner fills all 12 slots and another holds 2.
All inputs are finite; a program needn't handle non-finite values.
Results may differ from a plain program's by a relative error of at most 0.00061.
Values may be sent and summed in bfloat16 or wider, within the bound.
No kernel may reach another device: no remote copies, remote signals or barrier semaphores. Data moves between devices by JAX's collectives and lax.ppermute only.
A program may use at most 128 MiB of HBM per device.

v0:
```python
import math

import jax
import jax.numpy as jnp
from jax import lax
from jax.sharding import PartitionSpec as P

DEPTH = 2


def shifted(value, axis, by):
    count = lax.axis_size(axis)
    pairs = [(i, i + by) for i in range(count) if 0 <= i + by < count]
    return lax.ppermute(value, axis, pairs)


def spectral_table(samples, bins):
    sample_axis = lax.iota(jnp.int32, samples)
    bin_axis = lax.iota(jnp.int32, bins) + 1
    phases = sample_axis[:, None] * bin_axis[None, :] % (2 * samples)
    angles = phases.astype(jnp.float32) * (math.pi / samples)
    tapers = 0.5 - 0.5 * jnp.cos(sample_axis.astype(jnp.float32) * (2.0 * math.pi / samples))
    whole = jnp.concatenate([jnp.cos(angles), -jnp.sin(angles)], axis=1) * tapers[:, None]
    return whole.astype(jnp.bfloat16)


def whiten(blocks, table_bf):
    block_count, channels, samples = blocks.shape
    bins = table_bf.shape[1] // 2
    spectra = jnp.dot(
        blocks.reshape(block_count * channels, samples),
        table_bf,
        preferred_element_type=jnp.float32,
    )
    spectra = spectra.reshape(block_count, channels, 2 * bins)
    powers = (
        spectra[:, :, :bins] * spectra[:, :, :bins] + spectra[:, :, bins:] * spectra[:, :, bins:]
    )
    levels = jnp.sqrt(jnp.mean(powers, axis=1) + 1e-05)
    both_levels = jnp.concatenate([levels, levels], axis=1)
    return (spectra / both_levels[:, None, :]).astype(jnp.bfloat16)


def on_device(strain, pair_slots):
    own_blocks = strain[0]
    block_count, channels, samples = own_blocks.shape
    table_bf = spectral_table(samples, samples)
    moving = whiten(own_blocks, table_bf)
    owner_index = lax.axis_index("chan")
    lower_parts = []
    upper_parts = []
    for distance in range(DEPTH, 0, -1):
        lower_parts.append(shifted(moving, "chan", distance))
    for distance in range(1, DEPTH + 1):
        upper_parts.append(shifted(moving, "chan", -distance))
    window = jnp.concatenate(lower_parts + [moving] + upper_parts, axis=0)
    first_in_window = (owner_index - DEPTH) * block_count
    first_block = pair_slots[:, 0]
    second_block = pair_slots[:, 1]
    active = first_block >= 0
    index_a = jnp.where(active, first_block - first_in_window, 0)
    index_b = jnp.where(active, second_block - first_in_window, 0)
    active_f = active.astype(jnp.float32)
    slot_count = pair_slots.shape[0]

    def one_slot(slot_index):
        source_block = lax.dynamic_index_in_dim(window, index_a[slot_index], 0, keepdims=False)
        partner = lax.dynamic_index_in_dim(window, index_b[slot_index], 0, keepdims=False)
        turned = jnp.concatenate([-partner[:, samples:], partner[:, :samples]], axis=1)
        stacked_partner = jnp.concatenate([partner, turned], axis=0)
        product = lax.dot_general(
            source_block,
            stacked_partner,
            (((1,), (1,)), ((), ())),
            preferred_element_type=jnp.float32,
        )
        return product * active_f[slot_index]

    per_slot = lax.map(one_slot, jnp.arange(slot_count, dtype=jnp.int32))
    stacked = lax.psum_scatter(
        jnp.transpose(per_slot, (1, 0, 2)), "tm", scatter_dimension=0, tiled=True
    )
    return stacked / (samples * lax.axis_size("tm"))


def solution(mesh):
    return jax.shard_map(
        on_device,
        mesh=mesh,
        in_specs=(P("tm", "chan", None, None), P("chan", None)),
        out_specs=P("tm", "chan", None),
        check_vma=False,
    )
```

profile of v0, /device:TPU:56, one launch (start us, length us, event | category | flops | bytes accessed | tf_op | source)
XLA Modules:
  0.0 522.8 jit_solution(1290439433048474165)
XLA Ops:
  6.6 16.5 %fusion.22 = (f32[1024,1024]{1,0:T(8,128)S(1)}, f32[1024,1024]{1,0:T(8,128)S(1)}) fusion(s32[1024]{0:T(1024)S(1)} %iota_add_fusion), kind=kLoop, calls=%fused_computation.32 | loop fusion | flops 15728640 | bytes 8392704 | tf_op jit(solution)/shard_map/cos | solution.py:23
  23.1 2.5 fusion.14
  30.8 3.7 collective-permute-start.2
  34.5 5.8 %collective-permute-start.3 = (bf16[4,128,2048]{2,1,0:T(8,128)(2,1)S(1)}, bf16[4,128,2048]{2,1,0:T(8,128)(2,1)}, u32[]{:S(2)}, u32[]{:S(2)}) collective-permute-start(bf16[4,128,2048]{2,1,0:T(8,128)(2,1)S(1)} %divide_convert_fusion), channel_id=1, source_target_pairs={{64,0},{96,32},{128,64},{160,96},{192,128},{224,160},{256,192},{28... | collective-permute-start | bytes 6291464 | tf_op jit(solution)/shard_map/ppermute | solution.py:14
  40.4 37.7 %collective-permute-done = bf16[4,128,2048]{2,1,0:T(8,128)(2,1)} collective-permute-done((bf16[4,128,2048]{2,1,0:T(8,128)(2,1)S(1)}, bf16[4,128,2048]{2,1,0:T(8,128)(2,1)}, u32[]{:S(2)}, u32[]{:S(2)}) %collective-permute-start) | collective-permute-done | bytes 2097184 | tf_op jit(solution)/shard_map/ppermute | solution.py:14
  79.8 19.6 %collective-permute-done.1 = bf16[4,128,2048]{2,1,0:T(8,128)(2,1)} collective-permute-done((bf16[4,128,2048]{2,1,0:T(8,128)(2,1)S(1)}, bf16[4,128,2048]{2,1,0:T(8,128)(2,1)}, u32[]{:S(2)}, u32[]{:S(2)}) %collective-permute-start.1) | collective-permute-done | bytes 2097184 | tf_op jit(solution)/shard_map/ppermute | solution.py:14
  105.2 4.0 copy-done.3
  109.1 175.6 %while.10 = (s32[]{:T(128)}, f32[12,128,256]{2,0,1:T(8,128)}, s32[12]{0:T(128)S(1)}, s32[12]{0:T(128)S(1)}, bf16[20,128,2048]{2,1,0:T(8,128)(2,1)}, /*index=5*/s...) while((s32[]{:T(128)}, f32[12,128,256]{2,0,1:T(8,128)}, ...), condition=%wide.region_2.3_spmd, body=%wide.region_1.2_spmd.sunk | while | flops 137527312 | bytes 4326159 | solution.py:79
  119.7 4.1 dynamic_update_slice.5
  132.1 2.1 fusion.30
  134.3 4.1 dynamic_update_slice.5
  148.9 4.1 dynamic_update_slice.5
  161.3 2.1 fusion.30
  163.6 4.1 dynamic_update_slice.5
  178.2 4.1 dynamic_update_slice.5
  192.8 4.1 dynamic_update_slice.5
  207.5 4.1 dynamic_update_slice.5
  222.1 4.1 dynamic_update_slice.5
  236.7 4.1 dynamic_update_slice.5
  251.4 4.1 dynamic_update_slice.5
  263.8 2.1 fusion.30
  266.0 4.1 dynamic_update_slice.5
  280.6 4.1 dynamic_update_slice.5
  284.7 229.7 %reduce-scatter.2.cloned.1.call-done = f32[4,12,256]{2,1,0:T(8,128)} async-done(((f32[128,12,256]{2,1,0:T(8,128)}), f32[4,12,256]{2,1,0:T(8,128)}) %reduce-scatter.2.cloned.1.call-update) | async-done | bytes 49168 | tf_op jit(solution)/shard_map/reduce_scatter | solution.py:80
  (125 shorter events, 74.7 us)
Async XLA Ops:
  6.5 16.6 %copy-start = (bf16[1,4,128,1024]{3,2,1,0:T(8,128)(2,1)S(1)}, bf16[1,4,128,1024]{3,2,1,0:T(8,128)(2,1)}, u32[]{:S(2)}) copy-start(bf16[1,4,128,1024]{3,2,1,0:T(8,128)(2,1)} %param.4) | copy-start | bytes 3145732
  6.5 507.9 %reduce-scatter.2.cloned.1.call-start = ((), (), s32[]{:S(2)}) async-start(), calls=%async_computation.1 | async-start | bytes 2162688 | tf_op jit(solution)/shard_map/reduce_scatter | solution.py:80
  25.6 2.0 copy-start.1
  26.2 14.2 %copy-start.4 = (s32[12,2]{0,1:T(2,128)S(1)}, s32[12,2]{0,1:T(2,128)}, u32[]{:S(2)}) copy-start(s32[12,2]{0,1:T(2,128)} %param.5) | copy-start | bytes 292
  27.6 50.5 %collective-permute-start = (bf16[4,128,2048]{2,1,0:T(8,128)(2,1)S(1)}, bf16[4,128,2048]{2,1,0:T(8,128)(2,1)}, u32[]{:S(2)}, u32[]{:S(2)}) collective-permute-start(bf16[4,128,2048]{2,1,0:T(8,128)(2,1)S(1)} %divide_convert_fusion), channel_id=1, source_target_pairs={{0,64},{32,96},{64,128},{96,160},{128,192},{160,224},{192,256},{22... | collective-permute-start | bytes 6291464 | tf_op jit(solution)/shard_map/ppermute | solution.py:14
  28.9 70.5 %collective-permute-start.1 = (bf16[4,128,2048]{2,1,0:T(8,128)(2,1)S(1)}, bf16[4,128,2048]{2,1,0:T(8,128)(2,1)}, u32[]{:S(2)}, u32[]{:S(2)}) collective-permute-start(bf16[4,128,2048]{2,1,0:T(8,128)(2,1)S(1)} %divide_convert_fusion), channel_id=1, source_target_pairs={{0,32},{32,64},{64,96},{96,128},{128,160},{160,192},{192,224},{224... | collective-permute-start | bytes 6291464 | tf_op jit(solution)/shard_map/ppermute | solution.py:14
  30.8 70.9 %collective-permute-start.2 = (bf16[4,128,2048]{2,1,0:T(8,128)(2,1)S(1)}, bf16[4,128,2048]{2,1,0:T(8,128)(2,1)}, u32[]{:S(2)}, u32[]{:S(2)}) collective-permute-start(bf16[4,128,2048]{2,1,0:T(8,128)(2,1)S(1)} %divide_convert_fusion), channel_id=1, source_target_pairs={{32,0},{64,32},{96,64},{128,96},{160,128},{192,160},{224,192},{256... | collective-permute-start | bytes 6291464 | tf_op jit(solution)/shard_map/ppermute | solution.py:14
  34.5 68.9 %collective-permute-start.3 = (bf16[4,128,2048]{2,1,0:T(8,128)(2,1)S(1)}, bf16[4,128,2048]{2,1,0:T(8,128)(2,1)}, u32[]{:S(2)}, u32[]{:S(2)}) collective-permute-start(bf16[4,128,2048]{2,1,0:T(8,128)(2,1)S(1)} %divide_convert_fusion), channel_id=1, source_target_pairs={{64,0},{96,32},{128,64},{160,96},{192,128},{224,160},{256,192},{28... | collective-permute-start | bytes 6291464 | tf_op jit(solution)/shard_map/ppermute | solution.py:14
  40.4 60.8 %copy-start.2 = (f32[2048,512]{0,1:T(8,128)S(1)}, f32[2048,512]{0,1:T(8,128)}, u32[]{:S(2)}) copy-start(f32[2048,512]{0,1:T(8,128)} %copy-done.1) | copy-start | bytes 12582916
  105.1 4.0 copy-start.3
Sparse Core Ops, SparseCore 0:
  284.9 229.5 reduce-scatter.1
where the time goes:
time: 526 us; the launch traced here: 523 us
  waiting for transfers between devices  287 us (55%)
  local copies, waits for them, and re-layouts  103 us (20%)
  loops' own time  59.9 us (11%)
  matrix products  27.4 us (5%)
  other arithmetic  19.5 us (4%)
  between operations  13.6 us (3%)
  starting transfers between devices  12.7 us (2%)
    reduce_scatter x1, waiting for transfers between devices, on_device(): lax.psum_scatter(jnp.transpose(per_slot, (1, 0, 2)), 'tm', scatter_dimens...  230 us
    another operation x1, loops' own time, on_device(): per_slot = lax.map(one_slot, jnp.arange(slot_count, dtype=jnp.int32))  59.9 us
    ppermute x4, waiting for transfers between devices, shifted(): return lax.ppermute(value, axis, pairs)  57.3 us
    dynamic_update_slice x24, local copies, waits for them, and re-layouts, on_device(): per_slot = lax.map(one_slot, jnp.arange(slot_count, dtype=jnp.int32))  50.6 us
    dot_general x12, matrix products, one_slot(): lax.dot_general(source_block, stacked_partner, (((1,), (1,)), ((), ())),...  24.9 us
    cos x1, other arithmetic, spectral_table(): jnp.cos(angles)  16.5 us
    squeeze x12, local copies, waits for them, and re-layouts, one_slot(): lax.dynamic_index_in_dim(window, index_b[slot_index], 0, keepdims=False)  13 us
    ppermute x4, starting transfers between devices, shifted(): return lax.ppermute(value, axis, pairs)  12.7 us
  transfers between devices with their start and end apart: 5, of which 3 were waited for; matrix products, arithmetic and copies ran while one was open for 1% of the time, Pallas kernels for 0%

commit v1 on v0

v1 whole, which is shorter than its diff:
```python
import functools
import math

import jax
import jax.numpy as jnp
from jax import lax
from jax.experimental import pallas as pl
from jax.experimental.pallas import tpu as pltpu
from jax.sharding import PartitionSpec as P

LANES = 128
CHUNK = 256
ROWS_PERIOD = 16
GROUPS = 5
VMEM = 24 * 1024 * 1024


def table_parts(samples):
    sample = lax.broadcasted_iota(jnp.int32, (samples, LANES), 0)
    low = lax.broadcasted_iota(jnp.int32, (samples, LANES), 1) + 1
    angles = (sample * low % (2 * samples)).astype(jnp.float32) * (math.pi / samples)
    tapers = 0.5 - 0.5 * jnp.cos(sample.astype(jnp.float32) * (2.0 * math.pi / samples))
    steps = samples // LANES
    period = 2 * samples // LANES
    shape = (steps, period, LANES)
    step = lax.broadcasted_iota(jnp.int32, shape, 0)
    row = lax.broadcasted_iota(jnp.int32, shape, 1)
    turns = (step * row % period).astype(jnp.float32) * (2.0 * math.pi / period)
    return tapers * jnp.cos(angles), tapers * jnp.sin(angles), jnp.cos(turns), jnp.sin(turns)


def whiten_chunk(x, table, out_ref):
    blocks, channels, samples = x.shape
    spectra = jnp.dot(x.reshape(blocks * channels, samples), table, preferred_element_type=jnp.float32)
    for block in range(blocks):
        part = spectra[block * channels : (block + 1) * channels]
        real, imag = part[:, :CHUNK], part[:, CHUNK:]
        power = jnp.sum(real * real + imag * imag, axis=0, keepdims=True) * (1.0 / channels)
        scale = 1.0 / jnp.sqrt(power + 1e-05)
        out_ref[block, :channels, :] = (real * scale).astype(jnp.bfloat16)
        out_ref[block, channels:, :] = (imag * scale).astype(jnp.bfloat16)


def first_kernel(cos_ref, sin_ref, step_cos_ref, step_sin_ref, x_ref, table_ref, out_ref):
    chunk = pl.program_id(0)
    samples = x_ref.shape[2]
    period = step_cos_ref.shape[1]
    shape = (samples // period, period, LANES)
    low_cos = cos_ref[...].reshape(shape)
    low_sin = sin_ref[...].reshape(shape)
    per_chunk = CHUNK // LANES
    for part in range(per_chunk):
        step_cos = step_cos_ref[chunk * per_chunk + part][None]
        step_sin = step_sin_ref[chunk * per_chunk + part][None]
        real = low_cos * step_cos - low_sin * step_sin
        imag = -(low_sin * step_cos + low_cos * step_sin)
        columns = slice(part * LANES, (part + 1) * LANES)
        table_ref[:, columns] = real.reshape(samples, LANES).astype(jnp.bfloat16)
        columns = slice(CHUNK + part * LANES, CHUNK + (part + 1) * LANES)
        table_ref[:, columns] = imag.reshape(samples, LANES).astype(jnp.bfloat16)
    whiten_chunk(x_ref[...], table_ref[...], out_ref)


def whiten_first(x, parts):
    blocks, channels, samples = x.shape
    cos, sin, step_cos, step_sin = parts
    whole = lambda a: pl.BlockSpec(a.shape, lambda j: (0,) * a.ndim)
    return pl.pallas_call(
        first_kernel,
        grid=(samples // CHUNK,),
        in_specs=[whole(cos), whole(sin), whole(step_cos), whole(step_sin), whole(x)],
        out_specs=[
            pl.BlockSpec((samples, 2 * CHUNK), lambda j: (0, j)),
            pl.BlockSpec((blocks, 2 * channels, CHUNK), lambda j: (0, 0, j)),
        ],
        out_shape=[
            jax.ShapeDtypeStruct((samples, 2 * samples), jnp.bfloat16),
            jax.ShapeDtypeStruct((GROUPS * blocks, 2 * channels, samples), jnp.bfloat16),
        ],
        compiler_params=pltpu.CompilerParams(vmem_limit_bytes=VMEM),
        cost_estimate=pl.CostEstimate(
            flops=4 * blocks * channels * samples * samples, bytes_accessed=8 << 20, transcendentals=0
        ),
        name="table_and_own",
    )(cos, sin, step_cos, step_sin, x)


def next_kernel(x_ref, table_ref, window_ref, out_ref):
    del window_ref
    whiten_chunk(x_ref[...], table_ref[...], out_ref)


def whiten_into(window, place, x, table, name):
    blocks, channels, samples = x.shape
    return pl.pallas_call(
        next_kernel,
        grid=(samples // CHUNK,),
        in_specs=[
            pl.BlockSpec(x.shape, lambda j: (0, 0, 0)),
            pl.BlockSpec((samples, 2 * CHUNK), lambda j: (0, j)),
            pl.BlockSpec(memory_space=pl.ANY),
        ],
        out_specs=pl.BlockSpec((blocks, 2 * channels, CHUNK), lambda j: (place, 0, j)),
        out_shape=jax.ShapeDtypeStruct(window.shape, window.dtype),
        input_output_aliases={2: 0},
        compiler_params=pltpu.CompilerParams(vmem_limit_bytes=VMEM),
        cost_estimate=pl.CostEstimate(
            flops=4 * blocks * channels * samples * samples, bytes_accessed=8 << 20, transcendentals=0
        ),
        name=name,
    )(x, table, window)


def pair_kernel(owner_ref, slots_ref, a0_ref, b0_ref, a1_ref, b1_ref, out_ref):
    del owner_ref
    step = pl.program_id(0)
    channels = a0_ref.shape[1] // 2
    found = []
    for a_ref, b_ref, slot in ((a0_ref, b0_ref, 2 * step), (a1_ref, b1_ref, 2 * step + 1)):
        product = lax.dot_general(
            a_ref[0], b_ref[0], (((1,), (1,)), ((), ())), preferred_element_type=jnp.float32
        )
        real = product[:channels, :channels] + product[channels:, channels:]
        imag = product[channels:, :channels] - product[:channels, channels:]
        live = jnp.where(slots_ref[2 * slot] >= 0, 0.25, 0.0)
        both = jnp.concatenate([real, imag], axis=1) * live
        found.append(both.reshape(channels // 8, 8, 2 * channels))
    first, second = found
    row = lax.broadcasted_iota(jnp.int32, first.shape, 1)
    out_ref[:, 0] = jnp.where(row < 4, first, pltpu.roll(second, 4, 1))
    out_ref[:, 1] = jnp.where(row < 4, pltpu.roll(first, 4, 1), second)


def pair_products(window, slots, owner, own_blocks):
    _, stacked, samples = window.shape
    channels = stacked // 2
    slot_count = slots.shape[0]

    def place(owner_ref, slots_ref, entry):
        owner = owner_ref[0]
        block = slots_ref[entry]
        block = jnp.where(block >= 0, block, owner * own_blocks)
        side = 1 - 2 * lax.rem(owner, 2)
        away = (lax.div(block, own_blocks) - owner) * side
        return lax.rem(away + GROUPS, GROUPS) * own_blocks + lax.rem(block, own_blocks)

    def spec(which):
        return pl.BlockSpec(
            (1, stacked, samples),
            lambda i, owner_ref, slots_ref: (place(owner_ref, slots_ref, 4 * i + which), 0, 0),
        )

    return pl.pallas_call(
        pair_kernel,
        grid_spec=pltpu.PrefetchScalarGridSpec(
            num_scalar_prefetch=2,
            grid=(slot_count // 2,),
            in_specs=[spec(0), spec(1), spec(2), spec(3)],
            out_specs=pl.BlockSpec((channels // 8, 2, 8, 2 * channels), lambda i, *_: (0, 0, i, 0)),
        ),
        out_shape=jax.ShapeDtypeStruct((channels // 8, 2, slot_count * 4, 2 * channels), jnp.float32),
        compiler_params=pltpu.CompilerParams(vmem_limit_bytes=VMEM),
        cost_estimate=pl.CostEstimate(
            flops=slot_count * 8 * channels * channels * samples, bytes_accessed=14 << 20, transcendentals=0
        ),
        name="pair_products",
    )(owner, slots.reshape(-1), window, window, window, window)


def on_device(strain, pair_slots):
    x = strain[0]
    blocks, channels, samples = x.shape
    owners = lax.axis_size("chan")
    windows = lax.axis_size("tm")
    slot_count = pair_slots.shape[0]
    owner = lax.axis_index("chan")
    even = range(0, owners, 2)
    odd = range(1, owners, 2)
    sibling_pairs = [(i, i ^ 1) for i in range(owners)]
    near_pairs = [((i + 2) % owners, i) for i in even] + [((i - 2) % owners, i) for i in odd]
    far_pairs = [((i - 2) % owners, i) for i in even] + [((i + 2) % owners, i) for i in odd]

    passed_on = lax.ppermute(x, "chan", near_pairs)
    sibling = lax.ppermute(x, "chan", sibling_pairs)
    far = lax.ppermute(x, "chan", far_pairs)
    table, window = whiten_first(x, table_parts(samples))
    window = whiten_into(window, 1, sibling, table, "sibling")
    from_sibling = lax.ppermute(passed_on, "chan", sibling_pairs)
    window = whiten_into(window, 2, passed_on, table, "near")
    window = whiten_into(window, 4, from_sibling, table, "passed")
    window = whiten_into(window, 3, far, table, "far")

    products = pair_products(window, pair_slots, owner.reshape(1), blocks)
    rows = channels // windows
    products = products.reshape(windows, slot_count * rows, 2 * channels).astype(jnp.float16)
    arrived = lax.all_to_all(products, "tm", 0, 0, tiled=True)
    total = jnp.sum(arrived.astype(jnp.float32), axis=0) * (4.0 / (samples * windows))
    return jnp.transpose(total.reshape(slot_count, rows, 2 * channels), (1, 0, 2))


def solution(mesh):
    return jax.shard_map(
        on_device,
        mesh=mesh,
        in_specs=(P("tm", "chan", None, None), P("chan", None)),
        out_specs=P("tm", "chan", None),
        check_vma=False,
    )
```

time: 526 us -> 90.7 us (0.17)
  waiting for transfers between devices: 287 us -> 15.7 us
  local copies, waits for them, and re-layouts: 103 us -> 2.71 us
  loops' own time: 59.9 us -> 0 us
  blocking collectives: 0 us -> 33.2 us
  matrix products: 27.4 us -> 0 us
  Pallas kernels: 0 us -> 23 us
  other arithmetic: 19.5 us -> 2.68 us
  between operations: 13.6 us -> 0.15 us
    reduce_scatter x1 -> x0, waiting for transfers between devices: 230 us -> none  [on_device(): lax.psum_scatter(jnp.transpose(per_slot, (1, 0, 2)), 'tm', scatter_dimens...]
    another operation x1 -> x0, loops' own time: 59.9 us -> none  [on_device(): per_slot = lax.map(one_slot, jnp.arange(slot_count, dtype=jnp.int32))]
    dynamic_update_slice x24 -> x0, local copies, waits for them, and re-layouts: 50.6 us -> none  [on_device(): per_slot = lax.map(one_slot, jnp.arange(slot_count, dtype=jnp.int32))]
    ppermute x4, waiting for transfers between devices: 57.3 us -> 15.7 us  [the longest x1 15.7 us: on_device(): passed_on = lax.ppermute(x, 'chan', near_pairs)]
    all_to_all x0 -> x1, blocking collectives: none -> 33.2 us  [on_device(): arrived = lax.all_to_all(products, 'tm', 0, 0, tiled=True)]
    dot_general x13 -> x0, matrix products: 27.4 us -> none  [the longest x12 24.9 us: one_slot(): lax.dot_general(source_block, stacked_partner, (((1,), (1,)), ((), ())),...]
    dynamic_slice x48 -> x0, local copies, waits for them, and re-layouts: 26.8 us -> none  [the longest x12 6.73 us: one_slot(): index_a[slot_index]]
    pallas_call x0 -> x6, Pallas kernels: none -> 23 us  [the longest x4 15 us: whiten_into(): pl.pallas_call(next_kernel, grid=(samples // CHUNK,), in_specs=[pl.BlockS...]
  transfers between devices with their start and end apart: 5 -> 4, of which waited for: 3 -> 1; matrix products, arithmetic and copies ran while one was open for 1% -> 4% of each run, Pallas kernels for 0% -> 17%
where the time goes in v1:
time: 90.7 us; the launch traced here: 90.2 us
  blocking collectives  33.2 us (37%)
  Pallas kernels  23 us (25%)
  waiting for transfers between devices  15.7 us (17%)
  starting transfers between devices  12.8 us (14%)
  local copies, waits for them, and re-layouts  2.71 us (3%)
  other arithmetic  2.68 us (3%)
    all_to_all x1, blocking collectives, on_device(): arrived = lax.all_to_all(products, 'tm', 0, 0, tiled=True)  33.2 us
    ppermute x1, waiting for transfers between devices, on_device(): passed_on = lax.ppermute(x, 'chan', near_pairs)  15.7 us
    pallas_call x4, Pallas kernels, whiten_into(): pl.pallas_call(next_kernel, grid=(samples // CHUNK,), in_specs=[pl.BlockS...  15 us
    ppermute x1, starting transfers between devices, on_device(): far = lax.ppermute(x, 'chan', far_pairs)  5.72 us
    pallas_call x1, Pallas kernels, whiten_first(): pl.pallas_call(first_kernel, grid=(samples // CHUNK,), in_specs=[whole(co...  4.31 us
    pallas_call x1, Pallas kernels, pair_products(): pl.pallas_call(pair_kernel, grid_spec=pltpu.PrefetchScalarGridSpec(num_sc...  3.7 us
    ppermute x1, starting transfers between devices, on_device(): passed_on = lax.ppermute(x, 'chan', near_pairs)  3.25 us
    mul x1, other arithmetic, table_parts(): tapers * jnp.sin(angles)  2.1 us
  transfers between devices with their start and end apart: 4, of which 1 were waited for; matrix products, arithmetic and copies ran while one was open for 4% of the time, Pallas kernels for 17%

profile of v1, /device:TPU:56, one launch (start us, length us, event | category | flops | bytes accessed | tf_op | source)
XLA Modules:
  0.0 90.2 jit_solution(18201884569868529664)
XLA Ops:
  0.0 3.2 %collective-permute-start.1 = (bf16[4,128,1024]{2,1,0:T(8,128)(2,1)}, bf16[4,128,1024]{2,1,0:T(8,128)(2,1)S(1)}, u32[]{:S(2)}, u32[]{:S(2)}) collective-permute-start(bf16[4,128,1024]{2,1,0:T(8,128)(2,1)} %bitcast.4), channel_id=1, source_target_pairs={{64,0},{128,64},{192,128},{256,192},{320,256},{384,320},{448,384},... | collective-permute-start | bytes 3145736 | tf_op jit(solution)/shard_map/ppermute | solution.py:183
  3.3 1.9 %collective-permute-start.3 = (bf16[4,128,1024]{2,1,0:T(8,128)(2,1)}, bf16[4,128,1024]{2,1,0:T(8,128)(2,1)S(1)}, u32[]{:S(2)}, u32[]{:S(2)}) collective-permute-start(bf16[4,128,1024]{2,1,0:T(8,128)(2,1)} %bitcast.5), channel_id=1, source_target_pairs={{0,32},{32,0},{64,96},{96,64},{128,160},{160,128},{192,224},{224,1... | collective-permute-start | bytes 3145736 | tf_op jit(solution)/shard_map/ppermute | solution.py:184
  5.2 5.7 %collective-permute-start = (bf16[4,128,1024]{2,1,0:T(8,128)(2,1)}, bf16[4,128,1024]{2,1,0:T(8,128)(2,1)S(1)}, u32[]{:S(2)}, u32[]{:S(2)}) collective-permute-start(bf16[4,128,1024]{2,1,0:T(8,128)(2,1)} %bitcast.6), channel_id=1, source_target_pairs={{448,0},{0,64},{64,128},{128,192},{192,256},{256,320},{320,384},{3... | collective-permute-start | bytes 3145736 | tf_op jit(solution)/shard_map/ppermute | solution.py:185
  10.9 0.8 copy.8
  11.7 0.1 reshape.13.slots_ref
  11.8 15.7 %collective-permute-done.1.x_ref = bf16[4,128,1024]{2,1,0:T(8,128)(2,1)S(1)} collective-permute-done((bf16[4,128,1024]{2,1,0:T(8,128)(2,1)}, bf16[4,128,1024]{2,1,0:T(8,128)(2,1)S(1)}, u32[]{:S(2)}, u32[]{:S(2)}) %collective-permute-start.1) | collective-permute-done | bytes 1048608 | tf_op jit(solution)/shard_map/ppermute | solution.py:183
  27.5 1.9 %collective-permute-start.2 = (bf16[4,128,1024]{2,1,0:T(8,128)(2,1)S(1)}, bf16[4,128,1024]{2,1,0:T(8,128)(2,1)S(1)}, u32[]{:S(2)}, u32[]{:S(2)}) collective-permute-start(bf16[4,128,1024]{2,1,0:T(8,128)(2,1)S(1)} %collective-permute-done.1.x_ref), channel_id=1, source_target_pairs={{0,32},{32,0},{64,96},{96,64},{128,160},{160,128},{192,224},{224,1... | collective-permute-start | bytes 3145736 | tf_op jit(solution)/shard_map/ppermute | solution.py:188
  29.4 0.2 fusion.12
  29.7 2.1 %sine_multiply_fusion = (f32[1024,128]{1,0:T(8,128)S(1)}, f32[1024,128]{1,0:T(8,128)S(1)}) fusion(s32[128]{0:T(128)S(1)} %iota_add_fusion, f32[1024]{0:T(1024)S(1)} %multiply_subtract_fusion), kind=kLoop, calls=%fused_computation.7 | loop fusion | flops 2097152 | bytes 1053184 | tf_op jit(solution)/shard_map/mul | solution.py:29
  31.8 0.0 copy-start
  31.8 1.2 %copy-done = bf16[1,4,128,1024]{3,2,1,0:T(8,128)(2,1)S(1)} copy-done((bf16[1,4,128,1024]{3,2,1,0:T(8,128)(2,1)S(1)}, bf16[1,4,128,1024]{3,2,1,0:T(8,128)(2,1)}, u32[]{:S(2)}) %copy-start) | copy-done | bytes 1048600
  33.0 4.3 %table_and_own.1 = (bf16[1024,2048]{1,0:T(8,128)(2,1)S(1)}, bf16[20,256,1024]{2,1,0:T(8,128)(2,1)S(1)}) custom-call(f32[1024,128]{1,0:T(8,128)S(1)} %get-tuple-element.10.cos_ref, f32[1024,128]{1,0:T(8,128)S(1)} %get-tuple-element.9.sin_ref, f32[8,16,128]{2,1,0:T(8,128)S(1)} %get-tuple-element.12.step_cos_ref, ...), custom_call_target="tpu_custom_call" | custom-call | flops 2147483648 | bytes 8388608 | tf_op jit(solution)/shard_map/table_and_own/pallas_call | solution.py:68
  37.3 0.0 collective-permute-done.3.x_ref
  37.4 3.7 %sibling.1.window_ref = bf16[20,256,1024]{2,1,0:T(8,128)(2,1)S(1)} custom-call(bf16[4,128,1024]{2,1,0:T(8,128)(2,1)S(1)} %collective-permute-done.3.x_ref, bf16[1024,2048]{1,0:T(8,128)(2,1)S(1)} %get-tuple-element.7.table_ref, bf16[20,256,1024]{2,1,0:T(8,128)(2,1)S(1)} %get-tuple-element.8.window_ref), custom_call_target="tpu_custom_call", output_to_operand_aliasing={{}: (2, {})} | custom-call | flops 2147483648 | bytes 8388608 | tf_op jit(solution)/shard_map/sibling/pallas_call | solution.py:95
  41.1 3.7 %near.1.window_ref = bf16[20,256,1024]{2,1,0:T(8,128)(2,1)S(1)} custom-call(bf16[4,128,1024]{2,1,0:T(8,128)(2,1)S(1)} %collective-permute-done.1.x_ref, bf16[1024,2048]{1,0:T(8,128)(2,1)S(1)} %get-tuple-element.7.table_ref, bf16[20,256,1024]{2,1,0:T(8,128)(2,1)S(1)} %sibling.1.window_ref), custom_call_target="tpu_custom_call", output_to_operand_aliasing={{}: (2, {})} | custom-call | flops 2147483648 | bytes 8388608 | tf_op jit(solution)/shard_map/near/pallas_call | solution.py:95
  44.8 0.0 collective-permute-done.2.x_ref
  44.9 3.7 %passed.1.window_ref = bf16[20,256,1024]{2,1,0:T(8,128)(2,1)S(1)} custom-call(bf16[4,128,1024]{2,1,0:T(8,128)(2,1)S(1)} %collective-permute-done.2.x_ref, bf16[1024,2048]{1,0:T(8,128)(2,1)S(1)} %get-tuple-element.7.table_ref, bf16[20,256,1024]{2,1,0:T(8,128)(2,1)S(1)} %near.1.window_ref), custom_call_target="tpu_custom_call", output_to_operand_aliasing={{}: (2, {})} | custom-call | flops 2147483648 | bytes 8388608 | tf_op jit(solution)/shard_map/passed/pallas_call | solution.py:95
  48.6 0.0 collective-permute-done.x_ref
  48.6 3.7 %far.1.a0_ref.b0_ref.a1_ref.b1_ref = bf16[20,256,1024]{2,1,0:T(8,128)(2,1)S(1)} custom-call(bf16[4,128,1024]{2,1,0:T(8,128)(2,1)S(1)} %collective-permute-done.x_ref, bf16[1024,2048]{1,0:T(8,128)(2,1)S(1)} %get-tuple-element.7.table_ref, bf16[20,256,1024]{2,1,0:T(8,128)(2,1)S(1)} %passed.1.window_ref), custom_call_target="tpu_custom_call", output_to_operand_aliasing={{}: (2, {})} | custom-call | flops 2147483648 | bytes 8388608 | tf_op jit(solution)/shard_map/far/pallas_call | solution.py:95
  52.4 3.7 %pair_products.1 = f32[16,2,48,256]{3,2,1,0:T(8,128)S(1)} custom-call(s32[1]{0:T(128)} %bitcast.owner_ref, s32[24]{0:T(128)S(1)} %reshape.13.slots_ref, bf16[20,256,1024]{2,1,0:T(8,128)(2,1)S(1)} %far.1.a0_ref.b0_ref.a1_ref.b1_ref, bf16[20,256,1024]{2,1,0:T(8,128)(2,1)S(1)} %far.1.a0_ref.b0_ref.a1_ref.b1_ref, ...), custom_call_target="tpu_custom_call" | custom-call | flops 1610612736 | bytes 14680064 | tf_op jit(solution)/shard_map/pair_products/pallas_call | solution.py:153
  56.1 0.2 convert_element_type.28
  56.3 33.2 %all_to_all.5 = f16[32,48,256]{2,1,0:T(8,128)(2,1)S(1)} all-to-all(f16[32,48,256]{2,1,0:T(8,128)(2,1)S(1)} %bitcast.8), channel_id=1, replica_groups=mesh['chan'=16,'tm'=32] {'tm'}, dimensions={0} | all-to-all | bytes 1572864 | tf_op jit(solution)/shard_map/all_to_all | solution.py:196
  89.4 0.1 convert_reduce_fusion
  89.6 0.6 mul.70
  (3 shorter events, 0.1 us)
Async XLA Ops:
  0.0 27.5 %collective-permute-start.1 = (bf16[4,128,1024]{2,1,0:T(8,128)(2,1)}, bf16[4,128,1024]{2,1,0:T(8,128)(2,1)S(1)}, u32[]{:S(2)}, u32[]{:S(2)}) collective-permute-start(bf16[4,128,1024]{2,1,0:T(8,128)(2,1)} %bitcast.4), channel_id=1, source_target_pairs={{64,0},{128,64},{192,128},{256,192},{320,256},{384,320},{448,384},... | collective-permute-start | bytes 3145736 | tf_op jit(solution)/shard_map/ppermute | solution.py:183
  3.3 34.1 %collective-permute-start.3 = (bf16[4,128,1024]{2,1,0:T(8,128)(2,1)}, bf16[4,128,1024]{2,1,0:T(8,128)(2,1)S(1)}, u32[]{:S(2)}, u32[]{:S(2)}) collective-permute-start(bf16[4,128,1024]{2,1,0:T(8,128)(2,1)} %bitcast.5), channel_id=1, source_target_pairs={{0,32},{32,0},{64,96},{96,64},{128,160},{160,128},{192,224},{224,1... | collective-permute-start | bytes 3145736 | tf_op jit(solution)/shard_map/ppermute | solution.py:184
  5.2 43.4 %collective-permute-start = (bf16[4,128,1024]{2,1,0:T(8,128)(2,1)}, bf16[4,128,1024]{2,1,0:T(8,128)(2,1)S(1)}, u32[]{:S(2)}, u32[]{:S(2)}) collective-permute-start(bf16[4,128,1024]{2,1,0:T(8,128)(2,1)} %bitcast.6), channel_id=1, source_target_pairs={{448,0},{0,64},{64,128},{128,192},{192,256},{256,320},{320,384},{3... | collective-permute-start | bytes 3145736 | tf_op jit(solution)/shard_map/ppermute | solution.py:185
  27.5 17.3 %collective-permute-start.2 = (bf16[4,128,1024]{2,1,0:T(8,128)(2,1)S(1)}, bf16[4,128,1024]{2,1,0:T(8,128)(2,1)S(1)}, u32[]{:S(2)}, u32[]{:S(2)}) collective-permute-start(bf16[4,128,1024]{2,1,0:T(8,128)(2,1)S(1)} %collective-permute-done.1.x_ref), channel_id=1, source_target_pairs={{0,32},{32,0},{64,96},{96,64},{128,160},{160,128},{192,224},{224,1... | collective-permute-start | bytes 3145736 | tf_op jit(solution)/shard_map/ppermute | solution.py:188
  31.8 1.2 %copy-start = (bf16[1,4,128,1024]{3,2,1,0:T(8,128)(2,1)S(1)}, bf16[1,4,128,1024]{3,2,1,0:T(8,128)(2,1)}, u32[]{:S(2)}) copy-start(bf16[1,4,128,1024]{3,2,1,0:T(8,128)(2,1)} %param.2) | copy-start | bytes 3145732

commit v2 on v1

--- a/solution.py
+++ b/solution.py
@@ -11,22 +11,33 @@
 LANES = 128
 CHUNK = 256
 ROWS_PERIOD = 16
+SPLIT = 32
 GROUPS = 5
 VMEM = 24 * 1024 * 1024
 
 
 def table_parts(samples):
-    sample = lax.broadcasted_iota(jnp.int32, (samples, LANES), 0)
-    low = lax.broadcasted_iota(jnp.int32, (samples, LANES), 1) + 1
-    angles = (sample * low % (2 * samples)).astype(jnp.float32) * (math.pi / samples)
-    tapers = 0.5 - 0.5 * jnp.cos(sample.astype(jnp.float32) * (2.0 * math.pi / samples))
-    steps = samples // LANES
-    period = 2 * samples // LANES
-    shape = (steps, period, LANES)
-    step = lax.broadcasted_iota(jnp.int32, shape, 0)
-    row = lax.broadcasted_iota(jnp.int32, shape, 1)
-    turns = (step * row % period).astype(jnp.float32) * (2.0 * math.pi / period)
-    return tapers * jnp.cos(angles), tapers * jnp.sin(angles), jnp.cos(turns), jnp.sin(turns)
+    shape = (4 * SPLIT + samples // LANES * ROWS_PERIOD, LANES)
+    row = lax.broadcasted_iota(jnp.int32, shape, 0)
+    bin_low = lax.broadcasted_iota(jnp.int32, shape, 1) + 1
+    part = row // SPLIT
+    at = row % SPLIT
+    step_row = row - 4 * SPLIT
+    phases = jnp.where(
+        part == 0,
+        bin_low * at * SPLIT,
+        jnp.where(
+            part == 1,
+            bin_low * at,
+            jnp.where(
+                part == 2,
+                2 * SPLIT * at,
+                jnp.where(part == 3, 2 * at, (step_row // ROWS_PERIOD) * (step_row % ROWS_PERIOD) * LANES),
+            ),
+        ),
+    )
+    angles = (phases % (2 * samples)).astype(jnp.float32) * (math.pi / samples)
+    return jnp.cos(angles), jnp.sin(angles)
 
 
 def whiten_chunk(x, table, out_ref):
@@ -41,17 +52,32 @@
         out_ref[block, channels:, :] = (imag * scale).astype(jnp.bfloat16)
 
 
-def first_kernel(cos_ref, sin_ref, step_cos_ref, step_sin_ref, x_ref, table_ref, out_ref):
+def first_kernel(cos_ref, sin_ref, x_ref, table_ref, out_ref, low_cos_ref, low_sin_ref):
     chunk = pl.program_id(0)
     samples = x_ref.shape[2]
-    period = step_cos_ref.shape[1]
-    shape = (samples // period, period, LANES)
-    low_cos = cos_ref[...].reshape(shape)
-    low_sin = sin_ref[...].reshape(shape)
+
+    @pl.when(chunk == 0)
+    def _():
+        rows = lambda ref, part: ref[part * SPLIT : (part + 1) * SPLIT, :]
+        for at in range(samples // SPLIT):
+            high = lambda ref, part: ref[part * SPLIT + at : part * SPLIT + at + 1, :]
+            taper = 0.5 - 0.5 * (
+                high(cos_ref, 2) * rows(cos_ref, 3) - high(sin_ref, 2) * rows(sin_ref, 3)
+            )
+            cos = high(cos_ref, 0) * rows(cos_ref, 1) - high(sin_ref, 0) * rows(sin_ref, 1)
+            sin = high(sin_ref, 0) * rows(cos_ref, 1) + high(cos_ref, 0) * rows(sin_ref, 1)
+            low_cos_ref[at * SPLIT : (at + 1) * SPLIT, :] = taper * cos
+            low_sin_ref[at * SPLIT : (at + 1) * SPLIT, :] = taper * sin
+
+    shape = (samples // ROWS_PERIOD, ROWS_PERIOD, LANES)
+    low_cos = low_cos_ref[...].reshape(shape)
+    low_sin = low_sin_ref[...].reshape(shape)
     per_chunk = CHUNK // LANES
     for part in range(per_chunk):
-        step_cos = step_cos_ref[chunk * per_chunk + part][None]
-        step_sin = step_sin_ref[chunk * per_chunk + part][None]
+        first_row = 4 * SPLIT + (chunk * per_chunk + part) * ROWS_PERIOD
+        step_rows = pl.ds(pl.multiple_of(first_row, ROWS_PERIOD), ROWS_PERIOD)
+        step_cos = cos_ref[step_rows, :][None]
+        step_sin = sin_ref[step_rows, :][None]
         real = low_cos * step_cos - low_sin * step_sin
         imag = -(low_sin * step_cos + low_cos * step_sin)
         columns = slice(part * LANES, (part + 1) * LANES)
@@ -63,12 +89,12 @@
 
 def whiten_first(x, parts):
     blocks, channels, samples = x.shape
-    cos, sin, step_cos, step_sin = parts
+    cos, sin = parts
     whole = lambda a: pl.BlockSpec(a.shape, lambda j: (0,) * a.ndim)
     return pl.pallas_call(
         first_kernel,
         grid=(samples // CHUNK,),
-        in_specs=[whole(cos), whole(sin), whole(step_cos), whole(step_sin), whole(x)],
+        in_specs=[whole(cos), whole(sin), whole(x)],
         out_specs=[
             pl.BlockSpec((samples, 2 * CHUNK), lambda j: (0, j)),
             pl.BlockSpec((blocks, 2 * channels, CHUNK), lambda j: (0, 0, j)),
@@ -77,12 +103,13 @@
             jax.ShapeDtypeStruct((samples, 2 * samples), jnp.bfloat16),
             jax.ShapeDtypeStruct((GROUPS * blocks, 2 * channels, samples), jnp.bfloat16),
         ],
+        scratch_shapes=[pltpu.VMEM((samples, LANES), jnp.float32)] * 2,
         compiler_params=pltpu.CompilerParams(vmem_limit_bytes=VMEM),
         cost_estimate=pl.CostEstimate(
-            flops=4 * blocks * channels * samples * samples, bytes_accessed=8 << 20, transcendentals=0
+            flops=blocks * channels * samples, bytes_accessed=1 << 16, transcendentals=0
         ),
         name="table_and_own",
-    )(cos, sin, step_cos, step_sin, x)
+    )(cos, sin, x)
 
 
 def next_kernel(x_ref, table_ref, window_ref, out_ref):
@@ -105,7 +132,7 @@
         input_output_aliases={2: 0},
         compiler_params=pltpu.CompilerParams(vmem_limit_bytes=VMEM),
         cost_estimate=pl.CostEstimate(
-            flops=4 * blocks * channels * samples * samples, bytes_accessed=8 << 20, transcendentals=0
+            flops=blocks * channels * samples, bytes_accessed=1 << 16, transcendentals=0
         ),
         name=name,
     )(x, table, window)
@@ -122,7 +149,7 @@
         )
         real = product[:channels, :channels] + product[channels:, channels:]
         imag = product[channels:, :channels] - product[:channels, channels:]
-        live = jnp.where(slots_ref[2 * slot] >= 0, 0.25, 0.0)
+        live = jnp.where(slots_ref[0, slot] >= 0, 0.25, 0.0)
         both = jnp.concatenate([real, imag], axis=1) * live
         found.append(both.reshape(channels // 8, 8, 2 * channels))
     first, second = found
@@ -136,18 +163,18 @@
     channels = stacked // 2
     slot_count = slots.shape[0]
 
-    def place(owner_ref, slots_ref, entry):
+    def place(owner_ref, slots_ref, which, slot):
         owner = owner_ref[0]
-        block = slots_ref[entry]
+        block = slots_ref[which, slot]
         block = jnp.where(block >= 0, block, owner * own_blocks)
         side = 1 - 2 * lax.rem(owner, 2)
         away = (lax.div(block, own_blocks) - owner) * side
         return lax.rem(away + GROUPS, GROUPS) * own_blocks + lax.rem(block, own_blocks)
 
-    def spec(which):
+    def spec(which, of_two):
         return pl.BlockSpec(
             (1, stacked, samples),
-            lambda i, owner_ref, slots_ref: (place(owner_ref, slots_ref, 4 * i + which), 0, 0),
+            lambda i, owner_ref, slots_ref: (place(owner_ref, slots_ref, which, 2 * i + of_two), 0, 0),
         )
 
     return pl.pallas_call(
@@ -155,16 +182,16 @@
         grid_spec=pltpu.PrefetchScalarGridSpec(
             num_scalar_prefetch=2,
             grid=(slot_count // 2,),
-            in_specs=[spec(0), spec(1), spec(2), spec(3)],
+            in_specs=[spec(0, 0), spec(1, 0), spec(0, 1), spec(1, 1)],
             out_specs=pl.BlockSpec((channels // 8, 2, 8, 2 * channels), lambda i, *_: (0, 0, i, 0)),
         ),
         out_shape=jax.ShapeDtypeStruct((channels // 8, 2, slot_count * 4, 2 * channels), jnp.float32),
         compiler_params=pltpu.CompilerParams(vmem_limit_bytes=VMEM),
         cost_estimate=pl.CostEstimate(
-            flops=slot_count * 8 * channels * channels * samples, bytes_accessed=14 << 20, transcendentals=0
+            flops=slot_count * channels * samples, bytes_accessed=1 << 16, transcendentals=0
         ),
         name="pair_products",
-    )(owner, slots.reshape(-1), window, window, window, window)
+    )(owner, slots.T, window, window, window, window)
 
 
 def on_device(strain, pair_slots):
@@ -180,14 +207,18 @@
     near_pairs = [((i + 2) % owners, i) for i in even] + [((i - 2) % owners, i) for i in odd]
     far_pairs = [((i - 2) % owners, i) for i in even] + [((i + 2) % owners, i) for i in odd]
 
-    passed_on = lax.ppermute(x, "chan", near_pairs)
+    near = lax.ppermute(x, "chan", near_pairs)
     sibling = lax.ppermute(x, "chan", sibling_pairs)
+    table, window = whiten_first(x, table_parts(samples))
+    x, window, table = lax.optimization_barrier((x, window, table))
     far = lax.ppermute(x, "chan", far_pairs)
-    table, window = whiten_first(x, table_parts(samples))
     window = whiten_into(window, 1, sibling, table, "sibling")
-    from_sibling = lax.ppermute(passed_on, "chan", sibling_pairs)
-    window = whiten_into(window, 2, passed_on, table, "near")
-    window = whiten_into(window, 4, from_sibling, table, "passed")
+    near, window = lax.optimization_barrier((near, window))
+    passed = lax.ppermute(near, "chan", sibling_pairs)
+    window = whiten_into(window, 2, near, table, "near")
+    passed, window = lax.optimization_barrier((passed, window))
+    window = whiten_into(window, 4, passed, table, "passed")
+    far, window = lax.optimization_barrier((far, window))
     window = whiten_into(window, 3, far, table, "far")
 
     products = pair_products(window, pair_slots, owner.reshape(1), blocks)

time: 90.7 us -> 93.9 us (1.035)
  the two profiles are of different devices: /device:TPU:56 before, /device:TPU:2 now
where the time goes in v2:
time: 93.9 us; the launch traced here: 93.5 us
  blocking collectives  35.4 us (38%)
  Pallas kernels  24.4 us (26%)
  local copies, waits for them, and re-layouts  18.7 us (20%)
  starting transfers between devices  11.1 us (12%)
  waiting for transfers between devices  2.51 us (3%)
  other arithmetic  1.08 us (1%)
    all_to_all x1, blocking collectives, on_device(): arrived = lax.all_to_all(products, 'tm', 0, 0, tiled=True)  35.4 us
    unnamed x14, local copies, waits for them, and re-layouts  18.1 us
    pallas_call x4, Pallas kernels, whiten_into(): pl.pallas_call(next_kernel, grid=(samples // CHUNK,), in_specs=[pl.BlockS...  14.9 us
    pallas_call x1, Pallas kernels, whiten_first(): pl.pallas_call(first_kernel, grid=(samples // CHUNK,), in_specs=[whole(co...  5.79 us
    ppermute x1, starting transfers between devices, on_device(): near = lax.ppermute(x, 'chan', near_pairs)  5.38 us
    pallas_call x1, Pallas kernels, pair_products(): pl.pallas_call(pair_kernel, grid_spec=pltpu.PrefetchScalarGridSpec(num_sc...  3.7 us
    ppermute x1, waiting for transfers between devices, on_device(): far = lax.ppermute(x, 'chan', far_pairs)  2.5 us
    ppermute x1, starting transfers between devices, on_device(): far = lax.ppermute(x, 'chan', far_pairs)  1.92 us
  transfers between devices with their start and end apart: 4, of which 1 were waited for; matrix products, arithmetic and copies ran while one was open for 1% of the time, Pallas kernels for 18%

profile of v2, /device:TPU:2, one launch (start us, length us, event | category | flops | bytes accessed | tf_op | source)
XLA Modules:
  0.0 93.5 jit_solution(600696628369965761)
XLA Ops:
  0.0 1.9 %collective-permute-start.2 = (bf16[4,128,1024]{2,1,0:T(8,128)(2,1)}, bf16[4,128,1024]{2,1,0:T(8,128)(2,1)S(1)}, u32[]{:S(2)}, u32[]{:S(2)}) collective-permute-start(bf16[4,128,1024]{2,1,0:T(8,128)(2,1)} %bitcast.2.x_ref), channel_id=1, source_target_pairs={{0,32},{32,0},{64,96},{96,64},{128,160},{160,128},{192,224},{224,1... | collective-permute-start | bytes 3145736 | tf_op jit(solution)/shard_map/ppermute | solution.py:211
  1.9 5.4 %collective-permute-start.1 = (bf16[4,128,1024]{2,1,0:T(8,128)(2,1)}, bf16[4,128,1024]{2,1,0:T(8,128)(2,1)S(1)}, u32[]{:S(2)}, u32[]{:S(2)}) collective-permute-start(bf16[4,128,1024]{2,1,0:T(8,128)(2,1)} %bitcast.2.x_ref), channel_id=1, source_target_pairs={{64,0},{128,64},{192,128},{256,192},{320,256},{384,320},{448,384},... | collective-permute-start | bytes 3145736 | tf_op jit(solution)/shard_map/ppermute | solution.py:210
  7.4 0.7 fusion.8
  8.1 5.8 %table_and_own.1 = (bf16[1024,2048]{1,0:T(8,128)(2,1)S(1)}, bf16[20,256,1024]{2,1,0:T(8,128)(2,1)S(1)}) custom-call(f32[256,128]{1,0:T(8,128)S(1)} %get-tuple-element.28.cos_ref, f32[256,128]{1,0:T(8,128)S(1)} %get-tuple-element.27.sin_ref, bf16[4,128,1024]{2,1,0:T(8,128)(2,1)} %bitcast.2.x_ref), custom_call_target="tpu_custom_call" | custom-call | flops 524288 | bytes 65536 | tf_op jit(solution)/shard_map/table_and_own/pallas_call | solution.py:94
  13.9 0.0 collective-permute-done.2.x_ref
  14.0 3.7 %sibling.1.window_ref = bf16[20,256,1024]{2,1,0:T(8,128)(2,1)S(1)} custom-call(bf16[4,128,1024]{2,1,0:T(8,128)(2,1)S(1)} %collective-permute-done.2.x_ref, bf16[1024,2048]{1,0:T(8,128)(2,1)S(1)} %get-tuple-element.19.table_ref, bf16[20,256,1024]{2,1,0:T(8,128)(2,1)S(1)} %get-tuple-element.20.window_ref), custom_call_target="tpu_custom_call", output_to_operand_aliasing={{}: (2, {})} | custom-call | flops 524288 | bytes 65536 | tf_op jit(solution)/shard_map/sibling/pallas_call | solution.py:122
  17.7 4.0 %copy-done = bf16[20,256,1024]{2,1,0:T(8,128)(2,1)} copy-done((bf16[20,256,1024]{2,1,0:T(8,128)(2,1)}, bf16[20,256,1024]{2,1,0:T(8,128)(2,1)S(1)}, u32[]{:S(2)}) %copy-start) | copy-done | bytes 10485784
  21.7 0.0 collective-permute-done.1.x_ref
  21.7 1.9 %collective-permute-start.3 = (bf16[4,128,1024]{2,1,0:T(8,128)(2,1)S(1)}, bf16[4,128,1024]{2,1,0:T(8,128)(2,1)S(1)}, u32[]{:S(2)}, u32[]{:S(2)}) collective-permute-start(bf16[4,128,1024]{2,1,0:T(8,128)(2,1)S(1)} %collective-permute-done.1.x_ref), channel_id=1, source_target_pairs={{0,32},{32,0},{64,96},{96,64},{128,160},{160,128},{192,224},{224,1... | collective-permute-start | bytes 3145736 | tf_op jit(solution)/shard_map/ppermute | solution.py:217
  23.6 1.9 %collective-permute-start = (bf16[4,128,1024]{2,1,0:T(8,128)(2,1)}, bf16[4,128,1024]{2,1,0:T(8,128)(2,1)S(1)}, u32[]{:S(2)}, u32[]{:S(2)}) collective-permute-start(bf16[4,128,1024]{2,1,0:T(8,128)(2,1)} %bitcast.2.x_ref), channel_id=1, source_target_pairs={{448,0},{0,64},{64,128},{128,192},{192,256},{256,320},{320,384},{3... | collective-permute-start | bytes 3145736 | tf_op jit(solution)/shard_map/ppermute | solution.py:214
  25.6 4.0 %copy-done.1 = bf16[20,256,1024]{2,1,0:T(8,128)(2,1)S(1)} copy-done((bf16[20,256,1024]{2,1,0:T(8,128)(2,1)S(1)}, bf16[20,256,1024]{2,1,0:T(8,128)(2,1)}, u32[]{:S(2)}) %copy-start.1) | copy-done | bytes 10485784
  29.5 2.2 %copy-done.5 = bf16[1024,2048]{1,0:T(8,128)(2,1)S(1)} copy-done((bf16[1024,2048]{1,0:T(8,128)(2,1)S(1)}, bf16[1024,2048]{1,0:T(8,128)(2,1)}, u32[]{:S(2)}) %copy-start.5) | copy-done | bytes 4194328
  31.7 3.7 %near.1.window_ref = bf16[20,256,1024]{2,1,0:T(8,128)(2,1)S(1)} custom-call(bf16[4,128,1024]{2,1,0:T(8,128)(2,1)S(1)} %collective-permute-done.1.x_ref, bf16[1024,2048]{1,0:T(8,128)(2,1)S(1)} %copy-done.5, bf16[20,256,1024]{2,1,0:T(8,128)(2,1)S(1)} %copy-done.1), custom_call_target="tpu_custom_call", output_to_operand_aliasing={{}: (2, {})} | custom-call | flops 524288 | bytes 65536 | tf_op jit(solution)/shard_map/near/pallas_call | solution.py:122
  35.5 3.7 %passed.1.window_ref = bf16[20,256,1024]{2,1,0:T(8,128)(2,1)S(1)} custom-call(bf16[4,128,1024]{2,1,0:T(8,128)(2,1)S(1)} %collective-permute-done.3.x_ref, bf16[1024,2048]{1,0:T(8,128)(2,1)S(1)} %copy-done.5, bf16[20,256,1024]{2,1,0:T(8,128)(2,1)S(1)} %near.1.window_ref), custom_call_target="tpu_custom_call", output_to_operand_aliasing={{}: (2, {})} | custom-call | flops 524288 | bytes 65536 | tf_op jit(solution)/shard_map/passed/pallas_call | solution.py:122
  39.2 0.0 copy-start.6
  39.2 2.5 %collective-permute-done.x_ref = bf16[4,128,1024]{2,1,0:T(8,128)(2,1)S(1)} collective-permute-done((bf16[4,128,1024]{2,1,0:T(8,128)(2,1)}, bf16[4,128,1024]{2,1,0:T(8,128)(2,1)S(1)}, u32[]{:S(2)}, u32[]{:S(2)}) %collective-permute-start) | collective-permute-done | bytes 1048608 | tf_op jit(solution)/shard_map/ppermute | solution.py:214
  41.7 3.7 %far.1.a0_ref.b0_ref.a1_ref.b1_ref = bf16[20,256,1024]{2,1,0:T(8,128)(2,1)S(1)} custom-call(bf16[4,128,1024]{2,1,0:T(8,128)(2,1)S(1)} %collective-permute-done.x_ref, bf16[1024,2048]{1,0:T(8,128)(2,1)S(1)} %copy-done.5, bf16[20,256,1024]{2,1,0:T(8,128)(2,1)S(1)} %passed.1.window_ref), custom_call_target="tpu_custom_call", output_to_operand_aliasing={{}: (2, {})} | custom-call | flops 524288 | bytes 65536 | tf_op jit(solution)/shard_map/far/pallas_call | solution.py:122
  45.5 4.0 %copy-done.2 = bf16[20,256,1024]{2,1,0:T(8,128)(2,1)} copy-done((bf16[20,256,1024]{2,1,0:T(8,128)(2,1)}, bf16[20,256,1024]{2,1,0:T(8,128)(2,1)S(1)}, u32[]{:S(2)}) %copy-start.2) | copy-done | bytes 10485784
  49.5 4.0 %copy-done.3 = bf16[20,256,1024]{2,1,0:T(8,128)(2,1)S(1)} copy-done((bf16[20,256,1024]{2,1,0:T(8,128)(2,1)S(1)}, bf16[20,256,1024]{2,1,0:T(8,128)(2,1)}, u32[]{:S(2)}) %copy-start.3) | copy-done | bytes 10485784
  53.4 3.7 %pair_products.1 = f32[16,2,48,256]{3,2,1,0:T(8,128)S(1)} custom-call(s32[1]{0:T(128)} %bitcast.owner_ref, s32[2,12]{1,0:T(2,128)S(1)} %bitcast.5, bf16[20,256,1024]{2,1,0:T(8,128)(2,1)S(1)} %copy-done.3, bf16[20,256,1024]{2,1,0:T(8,128)(2,1)S(1)} %copy-done.3, bf16[20,256,1024]{2,1,0:T(8,128)(2,1)S(1)} %copy-done.3, bf16[20,256,1024]{2,1,0:T(8,128)(2,1)S(1)} %copy-done.3), custom_call_target="tpu_custom_call" | custom-call | flops 1572864 | bytes 65536 | tf_op jit(solution)/shard_map/pair_products/pallas_call | solution.py:180
  57.1 0.2 convert_element_type.15
  57.3 35.4 %all_to_all.5 = f16[32,48,256]{2,1,0:T(8,128)(2,1)S(1)} all-to-all(f16[32,48,256]{2,1,0:T(8,128)(2,1)S(1)} %bitcast.6), channel_id=1, replica_groups=mesh['chan'=16,'tm'=32] {'tm'}, dimensions={0} | all-to-all | bytes 1572864 | tf_op jit(solution)/shard_map/all_to_all | solution.py:227
  92.7 0.1 convert_reduce_fusion
  92.9 0.6 mul.64
  (17 shorter events, 0.1 us)
Async XLA Ops:
  0.0 14.0 %collective-permute-start.2 = (bf16[4,128,1024]{2,1,0:T(8,128)(2,1)}, bf16[4,128,1024]{2,1,0:T(8,128)(2,1)S(1)}, u32[]{:S(2)}, u32[]{:S(2)}) collective-permute-start(bf16[4,128,1024]{2,1,0:T(8,128)(2,1)} %bitcast.2.x_ref), channel_id=1, source_target_pairs={{0,32},{32,0},{64,96},{96,64},{128,160},{160,128},{192,224},{224,1... | collective-permute-start | bytes 3145736 | tf_op jit(solution)/shard_map/ppermute | solution.py:211
  1.9 19.8 %collective-permute-start.1 = (bf16[4,128,1024]{2,1,0:T(8,128)(2,1)}, bf16[4,128,1024]{2,1,0:T(8,128)(2,1)S(1)}, u32[]{:S(2)}, u32[]{:S(2)}) collective-permute-start(bf16[4,128,1024]{2,1,0:T(8,128)(2,1)} %bitcast.2.x_ref), channel_id=1, source_target_pairs={{64,0},{128,64},{192,128},{256,192},{320,256},{384,320},{448,384},... | collective-permute-start | bytes 3145736 | tf_op jit(solution)/shard_map/ppermute | solution.py:210
  13.9 3.8 %copy-start.4 = (bf16[1024,2048]{1,0:T(8,128)(2,1)}, bf16[1024,2048]{1,0:T(8,128)(2,1)S(1)}, u32[]{:S(2)}) copy-start(bf16[1024,2048]{1,0:T(8,128)(2,1)S(1)} %get-tuple-element.19.table_ref) | copy-start | bytes 12582916
  17.7 4.0 %copy-start = (bf16[20,256,1024]{2,1,0:T(8,128)(2,1)}, bf16[20,256,1024]{2,1,0:T(8,128)(2,1)S(1)}, u32[]{:S(2)}) copy-start(bf16[20,256,1024]{2,1,0:T(8,128)(2,1)S(1)} %sibling.1.window_ref) | copy-start | bytes 31457284
  21.7 13.8 %collective-permute-start.3 = (bf16[4,128,1024]{2,1,0:T(8,128)(2,1)S(1)}, bf16[4,128,1024]{2,1,0:T(8,128)(2,1)S(1)}, u32[]{:S(2)}, u32[]{:S(2)}) collective-permute-start(bf16[4,128,1024]{2,1,0:T(8,128)(2,1)S(1)} %collective-permute-done.1.x_ref), channel_id=1, source_target_pairs={{0,32},{32,0},{64,96},{96,64},{128,160},{160,128},{192,224},{224,1... | collective-permute-start | bytes 3145736 | tf_op jit(solution)/shard_map/ppermute | solution.py:217
  23.6 18.1 %collective-permute-start = (bf16[4,128,1024]{2,1,0:T(8,128)(2,1)}, bf16[4,128,1024]{2,1,0:T(8,128)(2,1)S(1)}, u32[]{:S(2)}, u32[]{:S(2)}) collective-permute-start(bf16[4,128,1024]{2,1,0:T(8,128)(2,1)} %bitcast.2.x_ref), channel_id=1, source_target_pairs={{448,0},{0,64},{64,128},{128,192},{192,256},{256,320},{320,384},{3... | collective-permute-start | bytes 3145736 | tf_op jit(solution)/shard_map/ppermute | solution.py:214
  25.6 4.0 %copy-start.1 = (bf16[20,256,1024]{2,1,0:T(8,128)(2,1)S(1)}, bf16[20,256,1024]{2,1,0:T(8,128)(2,1)}, u32[]{:S(2)}) copy-start(bf16[20,256,1024]{2,1,0:T(8,128)(2,1)} %copy-done) | copy-start | bytes 31457284
  29.5 2.2 %copy-start.5 = (bf16[1024,2048]{1,0:T(8,128)(2,1)S(1)}, bf16[1024,2048]{1,0:T(8,128)(2,1)}, u32[]{:S(2)}) copy-start(bf16[1024,2048]{1,0:T(8,128)(2,1)} %copy-done.4) | copy-start | bytes 12582916
  39.2 10.2 %copy-start.6 = (s32[12,2]{0,1:T(2,128)S(1)}, s32[12,2]{0,1:T(2,128)}, u32[]{:S(2)}) copy-start(s32[12,2]{0,1:T(2,128)} %param.3) | copy-start | bytes 292
  45.5 4.0 %copy-start.2 = (bf16[20,256,1024]{2,1,0:T(8,128)(2,1)}, bf16[20,256,1024]{2,1,0:T(8,128)(2,1)S(1)}, u32[]{:S(2)}) copy-start(bf16[20,256,1024]{2,1,0:T(8,128)(2,1)S(1)} %far.1.a0_ref.b0_ref.a1_ref.b1_ref) | copy-start | bytes 31457284
  49.5 4.0 %copy-start.3 = (bf16[20,256,1024]{2,1,0:T(8,128)(2,1)S(1)}, bf16[20,256,1024]{2,1,0:T(8,128)(2,1)}, u32[]{:S(2)}) copy-start(bf16[20,256,1024]{2,1,0:T(8,128)(2,1)} %copy-done.2) | copy-start | bytes 31457284

commit v3 on v2

v3 whole, which is shorter than its diff:
```python
import math

import jax
import jax.numpy as jnp
from jax import lax
from jax.experimental import pallas as pl
from jax.experimental.pallas import tpu as pltpu
from jax.sharding import PartitionSpec as P

LANES = 128
CHUNK = 256
ROWS_PERIOD = 16
SPLIT = 32
GROUPS = 5
VMEM = 28 * 1024 * 1024


def table_parts(samples):
    shape = (4 * SPLIT + samples // LANES * ROWS_PERIOD, LANES)
    row = lax.broadcasted_iota(jnp.int32, shape, 0)
    bin_low = lax.broadcasted_iota(jnp.int32, shape, 1) + 1
    part = row // SPLIT
    at = row % SPLIT
    step_row = row - 4 * SPLIT
    phases = jnp.where(
        part == 0,
        bin_low * at * SPLIT,
        jnp.where(
            part == 1,
            bin_low * at,
            jnp.where(
                part == 2,
                2 * SPLIT * at,
                jnp.where(part == 3, 2 * at, (step_row // ROWS_PERIOD) * (step_row % ROWS_PERIOD) * LANES),
            ),
        ),
    )
    angles = (phases % (2 * samples)).astype(jnp.float32) * (math.pi / samples)
    return jnp.cos(angles), jnp.sin(angles)


def whiten_chunk(x, table, out_ref):
    blocks, channels, samples = x.shape
    spectra = jnp.dot(x.reshape(blocks * channels, samples), table, preferred_element_type=jnp.float32)
    for block in range(blocks):
        part = spectra[block * channels : (block + 1) * channels]
        real, imag = part[:, :CHUNK], part[:, CHUNK:]
        power = jnp.sum(real * real + imag * imag, axis=0, keepdims=True) * (1.0 / channels)
        scale = 1.0 / jnp.sqrt(power + 1e-05)
        out_ref[block, :channels, :] = (real * scale).astype(jnp.bfloat16)
        out_ref[block, channels:, :] = (imag * scale).astype(jnp.bfloat16)


def first_kernel(cos_ref, sin_ref, x_ref, table_ref, out_ref, again_ref, low_cos_ref, low_sin_ref):
    chunk = pl.program_id(0)
    samples = x_ref.shape[2]

    @pl.when(chunk == 0)
    def _():
        again_ref[...] = x_ref[...]
        rows = lambda ref, part: ref[part * SPLIT : (part + 1) * SPLIT, :]
        for at in range(samples // SPLIT):
            high = lambda ref, part: ref[part * SPLIT + at : part * SPLIT + at + 1, :]
            taper = 0.5 - 0.5 * (
                high(cos_ref, 2) * rows(cos_ref, 3) - high(sin_ref, 2) * rows(sin_ref, 3)
            )
            cos = high(cos_ref, 0) * rows(cos_ref, 1) - high(sin_ref, 0) * rows(sin_ref, 1)
            sin = high(sin_ref, 0) * rows(cos_ref, 1) + high(cos_ref, 0) * rows(sin_ref, 1)
            low_cos_ref[at * SPLIT : (at + 1) * SPLIT, :] = taper * cos
            low_sin_ref[at * SPLIT : (at + 1) * SPLIT, :] = taper * sin

    shape = (samples // ROWS_PERIOD, ROWS_PERIOD, LANES)
    low_cos = low_cos_ref[...].reshape(shape)
    low_sin = low_sin_ref[...].reshape(shape)
    per_chunk = CHUNK // LANES
    for part in range(per_chunk):
        first_row = 4 * SPLIT + (chunk * per_chunk + part) * ROWS_PERIOD
        step_rows = pl.ds(pl.multiple_of(first_row, ROWS_PERIOD), ROWS_PERIOD)
        step_cos = cos_ref[step_rows, :][None]
        step_sin = sin_ref[step_rows, :][None]
        real = low_cos * step_cos - low_sin * step_sin
        imag = -(low_sin * step_cos + low_cos * step_sin)
        columns = slice(part * LANES, (part + 1) * LANES)
        table_ref[:, columns] = real.reshape(samples, LANES).astype(jnp.bfloat16)
        columns = slice(CHUNK + part * LANES, CHUNK + (part + 1) * LANES)
        table_ref[:, columns] = imag.reshape(samples, LANES).astype(jnp.bfloat16)
    whiten_chunk(x_ref[...], table_ref[...], out_ref)


def hint(work):
    return pl.CostEstimate(flops=work, bytes_accessed=1 << 16, transcendentals=0)


def whiten_first(x, parts):
    blocks, channels, samples = x.shape
    cos, sin = parts
    whole = lambda a: pl.BlockSpec(a.shape, lambda j: (0,) * a.ndim)
    return pl.pallas_call(
        first_kernel,
        grid=(samples // CHUNK,),
        in_specs=[whole(cos), whole(sin), whole(x)],
        out_specs=[
            pl.BlockSpec((samples, 2 * CHUNK), lambda j: (0, j)),
            pl.BlockSpec((blocks, 2 * channels, CHUNK), lambda j: (0, 0, j)),
            whole(x),
        ],
        out_shape=[
            jax.ShapeDtypeStruct((samples, 2 * samples), jnp.bfloat16),
            jax.ShapeDtypeStruct((blocks, 2 * channels, samples), jnp.bfloat16),
            jax.ShapeDtypeStruct(x.shape, x.dtype),
        ],
        scratch_shapes=[pltpu.VMEM((samples, LANES), jnp.float32)] * 2,
        compiler_params=pltpu.CompilerParams(vmem_limit_bytes=VMEM),
        cost_estimate=hint(blocks * channels * samples),
        name="table_and_own",
    )(cos, sin, x)


def next_kernel(x_ref, table_ref, out_ref):
    whiten_chunk(x_ref[...], table_ref[...], out_ref)


def whiten_next(x, table, name):
    blocks, channels, samples = x.shape
    return pl.pallas_call(
        next_kernel,
        grid=(samples // CHUNK,),
        in_specs=[
            pl.BlockSpec(x.shape, lambda j: (0, 0, 0)),
            pl.BlockSpec((samples, 2 * CHUNK), lambda j: (0, j)),
        ],
        out_specs=pl.BlockSpec((blocks, 2 * channels, CHUNK), lambda j: (0, 0, j)),
        out_shape=jax.ShapeDtypeStruct((blocks, 2 * channels, samples), jnp.bfloat16),
        compiler_params=pltpu.CompilerParams(vmem_limit_bytes=VMEM),
        cost_estimate=hint(blocks * channels * samples),
        name=name,
    )(x, table)


def last_kernel(
    owner_ref, slots_ref, x_ref, table_ref, own_ref, sibling_ref, near_ref, passed_ref, out_ref, window_ref, sems
):
    step = pl.program_id(0)
    blocks, channels, samples = x_ref.shape
    chunks = samples // CHUNK
    parts = ((own_ref, 0), (sibling_ref, 1), (near_ref, 2), (passed_ref, 4))
    copies = [
        pltpu.make_async_copy(ref, window_ref.at[pl.ds(place * blocks, blocks)], sems.at[at])
        for at, (ref, place) in enumerate(parts)
    ]

    @pl.when(step == 0)
    def _():
        for copy in copies:
            copy.start()

    for chunk in range(chunks):

        @pl.when(step == chunk)
        def _():
            columns = pl.ds(chunk * CHUNK, CHUNK)
            far = window_ref.at[pl.ds(3 * blocks, blocks), :, columns]
            whiten_chunk(x_ref[...], table_ref[...], far)

    @pl.when(step == chunks - 1)
    def _():
        for copy in copies:
            copy.wait()

    @pl.when(step >= chunks)
    def _():
        owner = owner_ref[0]

        def place(block):
            block = jnp.where(block >= 0, block, owner * blocks)
            away = (lax.div(block, blocks) - owner) * (1 - 2 * lax.rem(owner, 2))
            return lax.rem(away + GROUPS, GROUPS) * blocks + lax.rem(block, blocks)

        found = []
        for slot in (2 * (step - chunks), 2 * (step - chunks) + 1):
            first, second = slots_ref[0, slot], slots_ref[1, slot]
            product = lax.dot_general(
                window_ref[place(first)],
                window_ref[place(second)],
                (((1,), (1,)), ((), ())),
                preferred_element_type=jnp.float32,
            )
            real = product[:channels, :channels] + product[channels:, channels:]
            imag = product[channels:, :channels] - product[:channels, channels:]
            live = jnp.where(first >= 0, 0.25, 0.0)
            both = jnp.concatenate([real, imag], axis=1) * live
            found.append(both.reshape(channels // 8, 8, 2 * channels))
        first, second = found
        row = lax.broadcasted_iota(jnp.int32, first.shape, 1)
        out_ref[:, 0] = jnp.where(row < 4, first, pltpu.roll(second, 4, 1))
        out_ref[:, 1] = jnp.where(row < 4, pltpu.roll(first, 4, 1), second)


def far_and_pairs(owner, slots, x, table, own, sibling, near, passed):
    blocks, channels, samples = x.shape
    slot_count = slots.shape[0]
    chunks = samples // CHUNK
    anywhere = pl.BlockSpec(memory_space=pl.ANY)
    return pl.pallas_call(
        last_kernel,
        grid_spec=pltpu.PrefetchScalarGridSpec(
            num_scalar_prefetch=2,
            grid=(chunks + slot_count // 2,),
            in_specs=[
                pl.BlockSpec(x.shape, lambda i, *_: (0, 0, 0)),
                pl.BlockSpec((samples, 2 * CHUNK), lambda i, *_: (0, jnp.minimum(i, chunks - 1))),
                anywhere,
                anywhere,
                anywhere,
                anywhere,
            ],
            out_specs=pl.BlockSpec(
                (channels // 8, 2, 8, 2 * channels), lambda i, *_: (0, 0, jnp.maximum(i - chunks, 0), 0)
            ),
            scratch_shapes=[
                pltpu.VMEM((GROUPS * blocks, 2 * channels, samples), jnp.bfloat16),
                pltpu.SemaphoreType.DMA((4,)),
            ],
        ),
        out_shape=jax.ShapeDtypeStruct((channels // 8, 2, slot_count * 4, 2 * channels), jnp.float32),
        compiler_params=pltpu.CompilerParams(vmem_limit_bytes=VMEM),
        cost_estimate=hint(slot_count * channels * samples),
        name="far_and_pairs",
    )(owner, slots.T, x, table, own, sibling, near, passed)


def after_transfer(x, work):
    anywhere = pl.BlockSpec(memory_space=pl.ANY)
    return pl.pallas_call(
        lambda x_ref, out_ref: None,
        in_specs=[anywhere],
        out_specs=anywhere,
        out_shape=jax.ShapeDtypeStruct(x.shape, x.dtype),
        input_output_aliases={0: 0},
        cost_estimate=hint(work),
        name="far_arrived",
    )(x)


def on_device(strain, pair_slots):
    x = strain[0]
    blocks, channels, samples = x.shape
    owners = lax.axis_size("chan")
    windows = lax.axis_size("tm")
    slot_count = pair_slots.shape[0]
    owner = lax.axis_index("chan")
    even = range(0, owners, 2)
    odd = range(1, owners, 2)
    sibling_pairs = [(i, i ^ 1) for i in range(owners)]
    near_pairs = [((i + 2) % owners, i) for i in even] + [((i - 2) % owners, i) for i in odd]
    far_pairs = [((i - 2) % owners, i) for i in even] + [((i + 2) % owners, i) for i in odd]

    near = lax.ppermute(x, "chan", near_pairs)
    table, own, again = whiten_first(x, table_parts(samples))
    sibling = lax.ppermute(own, "chan", sibling_pairs)
    far = lax.ppermute(again, "chan", far_pairs)
    far = after_transfer(far, 100 * 10**9)
    near = whiten_next(near, table, "near")
    passed = lax.ppermute(near, "chan", sibling_pairs)
    products = far_and_pairs(owner.reshape(1), pair_slots, far, table, own, sibling, near, passed)

    rows = channels // windows
    products = products.reshape(windows, slot_count * rows, 2 * channels).astype(jnp.float16)
    arrived = lax.all_to_all(products, "tm", 0, 0, tiled=True)
    total = jnp.sum(arrived.astype(jnp.float32), axis=0) * (4.0 / (samples * windows))
    return jnp.transpose(total.reshape(slot_count, rows, 2 * channels), (1, 0, 2))


def solution(mesh):
    return jax.shard_map(
        on_device,
        mesh=mesh,
        in_specs=(P("tm", "chan", None, None), P("chan", None)),
        out_specs=P("tm", "chan", None),
        check_vma=False,
    )
```

time: 93.9 us -> 79.9 us (0.85)
  the two profiles are of different devices: /device:TPU:2 before, /device:TPU:56 now
where the time goes in v3:
time: 79.9 us; the launch traced here: 79.5 us
  blocking collectives  32.6 us (41%)
  Pallas kernels  18.2 us (23%)
  starting transfers between devices  12.8 us (16%)
  local copies, waits for them, and re-layouts  8.19 us (10%)
  waiting for transfers between devices  6.57 us (8%)
  other arithmetic  1.07 us (1%)
    all_to_all x1, blocking collectives, on_device(): arrived = lax.all_to_all(products, 'tm', 0, 0, tiled=True)  32.6 us
    pallas_call x1, Pallas kernels, far_and_pairs(): pl.pallas_call(last_kernel, grid_spec=pltpu.PrefetchScalarGridSpec(num_sc...  8.95 us
    unnamed x10, local copies, waits for them, and re-layouts  7.55 us
    ppermute x1, starting transfers between devices, on_device(): far = lax.ppermute(again, 'chan', far_pairs)  5.7 us
    pallas_call x1, Pallas kernels, whiten_first(): pl.pallas_call(first_kernel, grid=(samples // CHUNK,), in_specs=[whole(co...  5.55 us
    ppermute x1, waiting for transfers between devices, on_device(): passed = lax.ppermute(near, 'chan', sibling_pairs)  3.76 us
    pallas_call x1, Pallas kernels, whiten_next(): pl.pallas_call(next_kernel, grid=(samples // CHUNK,), in_specs=[pl.BlockS...  3.73 us
    ppermute x1, starting transfers between devices, on_device(): near = lax.ppermute(x, 'chan', near_pairs)  3.25 us
  transfers between devices with their start and end apart: 4, of which 3 were waited for; matrix products, arithmetic and copies ran while one was open for 1% of the time, Pallas kernels for 12%

profile of v3, /device:TPU:56, one launch (start us, length us, event | category | flops | bytes accessed | tf_op | source)
XLA Modules:
  0.0 79.5 jit_solution(15147351864818600909)
XLA Ops:
  0.0 3.2 %collective-permute-start.2 = (bf16[4,128,1024]{2,1,0:T(8,128)(2,1)}, bf16[4,128,1024]{2,1,0:T(8,128)(2,1)S(1)}, u32[]{:S(2)}, u32[]{:S(2)}) collective-permute-start(bf16[4,128,1024]{2,1,0:T(8,128)(2,1)} %bitcast.5), channel_id=1, source_target_pairs={{64,0},{128,64},{192,128},{256,192},{320,256},{384,320},{448,384},... | collective-permute-start | bytes 3145736 | tf_op jit(solution)/shard_map/ppermute | solution.py:258
  3.3 0.7 fusion.8
  4.1 0.0 copy-start.3
  4.1 1.2 %copy-done.3 = bf16[1,4,128,1024]{3,2,1,0:T(8,128)(2,1)S(1)} copy-done((bf16[1,4,128,1024]{3,2,1,0:T(8,128)(2,1)S(1)}, bf16[1,4,128,1024]{3,2,1,0:T(8,128)(2,1)}, u32[]{:S(2)}) %copy-start.3) | copy-done | bytes 1048600
  5.3 5.5 %table_and_own.1 = (bf16[1024,2048]{1,0:T(8,128)(2,1)S(1)}, bf16[4,256,1024]{2,1,0:T(8,128)(2,1)}, bf16[4,128,1024]{2,1,0:T(8,128)(2,1)}) custom-call(f32[256,128]{1,0:T(8,128)S(1)} %get-tuple-element.12.cos_ref, f32[256,128]{1,0:T(8,128)S(1)} %get-tuple-element.11.sin_ref, bf16[4,128,1024]{2,1,0:T(8,128)(2,1)S(1)} %bitcast.6), custom_call_target="tpu_custom_call" | custom-call | flops 524288 | bytes 65536 | tf_op jit(solution)/shard_map/table_and_own/pallas_call | solution.py:98
  10.9 0.0 copy-start
  10.9 1.9 %copy-done = bf16[1024,2048]{1,0:T(8,128)(2,1)} copy-done((bf16[1024,2048]{1,0:T(8,128)(2,1)}, bf16[1024,2048]{1,0:T(8,128)(2,1)S(1)}, u32[]{:S(2)}) %copy-start) | copy-done | bytes 4194328
  12.8 5.7 %collective-permute-start = (bf16[4,128,1024]{2,1,0:T(8,128)(2,1)}, bf16[4,128,1024]{2,1,0:T(8,128)(2,1)}, u32[]{:S(2)}, u32[]{:S(2)}) collective-permute-start(bf16[4,128,1024]{2,1,0:T(8,128)(2,1)} %get-tuple-element.8), channel_id=1, source_target_pairs={{448,0},{0,64},{64,128},{128,192},{192,256},{256,320},{320,384},{3... | collective-permute-start | bytes 3145736 | tf_op jit(solution)/shard_map/ppermute | solution.py:261
  18.5 1.9 %collective-permute-start.1 = (bf16[4,256,1024]{2,1,0:T(8,128)(2,1)}, bf16[4,256,1024]{2,1,0:T(8,128)(2,1)}, u32[]{:S(2)}, u32[]{:S(2)}) collective-permute-start(bf16[4,256,1024]{2,1,0:T(8,128)(2,1)} %get-tuple-element.10.own_ref), channel_id=1, source_target_pairs={{0,32},{32,0},{64,96},{96,64},{128,160},{160,128},{192,224},{224,1... | collective-permute-start | bytes 6291464 | tf_op jit(solution)/shard_map/ppermute | solution.py:260
  20.5 2.3 %collective-permute-done.2.x_ref = bf16[4,128,1024]{2,1,0:T(8,128)(2,1)S(1)} collective-permute-done((bf16[4,128,1024]{2,1,0:T(8,128)(2,1)}, bf16[4,128,1024]{2,1,0:T(8,128)(2,1)S(1)}, u32[]{:S(2)}, u32[]{:S(2)}) %collective-permute-start.2) | collective-permute-done | bytes 1048608 | tf_op jit(solution)/shard_map/ppermute | solution.py:258
  22.8 2.2 %copy-done.1 = bf16[1024,2048]{1,0:T(8,128)(2,1)S(1)} copy-done((bf16[1024,2048]{1,0:T(8,128)(2,1)S(1)}, bf16[1024,2048]{1,0:T(8,128)(2,1)}, u32[]{:S(2)}) %copy-start.1) | copy-done | bytes 4194328
  25.0 3.7 %near.1.near_ref = bf16[4,256,1024]{2,1,0:T(8,128)(2,1)S(1)} custom-call(bf16[4,128,1024]{2,1,0:T(8,128)(2,1)S(1)} %collective-permute-done.2.x_ref, bf16[1024,2048]{1,0:T(8,128)(2,1)S(1)} %copy-done.1), custom_call_target="tpu_custom_call" | custom-call | flops 524288 | bytes 65536 | tf_op jit(solution)/shard_map/near/pallas_call | solution.py:125
  28.7 0.0 copy-start.4
  28.7 1.9 %collective-permute-start.3 = (bf16[4,256,1024]{2,1,0:T(8,128)(2,1)S(1)}, bf16[4,256,1024]{2,1,0:T(8,128)(2,1)}, u32[]{:S(2)}, u32[]{:S(2)}) collective-permute-start(bf16[4,256,1024]{2,1,0:T(8,128)(2,1)S(1)} %near.1.near_ref), channel_id=1, source_target_pairs={{0,32},{32,0},{64,96},{96,64},{128,160},{160,128},{192,224},{224,1... | collective-permute-start | bytes 6291464 | tf_op jit(solution)/shard_map/ppermute | solution.py:264
  30.6 0.5 collective-permute-done.x_ref
  31.1 0.0 collective-permute-done.1.sibling_ref
  31.1 3.8 %collective-permute-done.3.passed_ref = bf16[4,256,1024]{2,1,0:T(8,128)(2,1)} collective-permute-done((bf16[4,256,1024]{2,1,0:T(8,128)(2,1)S(1)}, bf16[4,256,1024]{2,1,0:T(8,128)(2,1)}, u32[]{:S(2)}, u32[]{:S(2)}) %collective-permute-start.3) | collective-permute-done | bytes 2097184 | tf_op jit(solution)/shard_map/ppermute | solution.py:264
  34.9 0.0 copy-done.4
  34.9 2.2 %copy-done.2 = bf16[1024,2048]{1,0:T(8,128)(2,1)S(1)} copy-done((bf16[1024,2048]{1,0:T(8,128)(2,1)S(1)}, bf16[1024,2048]{1,0:T(8,128)(2,1)}, u32[]{:S(2)}) %copy-start.2) | copy-done | bytes 4194328
  37.1 8.9 %far_and_pairs.1 = f32[16,2,48,256]{3,2,1,0:T(8,128)S(1)} custom-call(s32[1]{0:T(128)} %bitcast.owner_ref, s32[2,12]{1,0:T(2,128)S(1)} %bitcast.7, bf16[4,128,1024]{2,1,0:T(8,128)(2,1)} %far_arrived.1.x_ref, bf16[1024,2048]{1,0:T(8,128)(2,1)S(1)} %copy-done.2, bf16[4,256,1024]{2,1,0:T(8,128)(2,1)} %get-tuple-element.10.own_ref, ...), custom_call_target="tpu_custom_call" | custom-call | flops 1572864 | bytes 65536 | tf_op jit(solution)/shard_map/far_and_pairs/pallas_call | solution.py:204
  46.0 0.2 convert_element_type.15
  46.2 32.6 %all_to_all.5 = f16[32,48,256]{2,1,0:T(8,128)(2,1)S(1)} all-to-all(f16[32,48,256]{2,1,0:T(8,128)(2,1)S(1)} %bitcast.8), channel_id=1, replica_groups=mesh['chan'=16,'tm'=32] {'tm'}, dimensions={0} | all-to-all | bytes 1572864 | tf_op jit(solution)/shard_map/all_to_all | solution.py:269
  78.8 0.1 convert_reduce_fusion
  78.9 0.6 mul.64
  (11 shorter events, 0.1 us)
Async XLA Ops:
  0.0 22.8 %collective-permute-start.2 = (bf16[4,128,1024]{2,1,0:T(8,128)(2,1)}, bf16[4,128,1024]{2,1,0:T(8,128)(2,1)S(1)}, u32[]{:S(2)}, u32[]{:S(2)}) collective-permute-start(bf16[4,128,1024]{2,1,0:T(8,128)(2,1)} %bitcast.5), channel_id=1, source_target_pairs={{64,0},{128,64},{192,128},{256,192},{320,256},{384,320},{448,384},... | collective-permute-start | bytes 3145736 | tf_op jit(solution)/shard_map/ppermute | solution.py:258
  4.1 1.2 %copy-start.3 = (bf16[1,4,128,1024]{3,2,1,0:T(8,128)(2,1)S(1)}, bf16[1,4,128,1024]{3,2,1,0:T(8,128)(2,1)}, u32[]{:S(2)}) copy-start(bf16[1,4,128,1024]{3,2,1,0:T(8,128)(2,1)} %param.2) | copy-start | bytes 3145732
  10.9 1.9 %copy-start = (bf16[1024,2048]{1,0:T(8,128)(2,1)}, bf16[1024,2048]{1,0:T(8,128)(2,1)S(1)}, u32[]{:S(2)}) copy-start(bf16[1024,2048]{1,0:T(8,128)(2,1)S(1)} %get-tuple-element.9.table_ref) | copy-start | bytes 12582916
  12.8 18.3 %collective-permute-start = (bf16[4,128,1024]{2,1,0:T(8,128)(2,1)}, bf16[4,128,1024]{2,1,0:T(8,128)(2,1)}, u32[]{:S(2)}, u32[]{:S(2)}) collective-permute-start(bf16[4,128,1024]{2,1,0:T(8,128)(2,1)} %get-tuple-element.8), channel_id=1, source_target_pairs={{448,0},{0,64},{64,128},{128,192},{192,256},{256,320},{320,384},{3... | collective-permute-start | bytes 3145736 | tf_op jit(solution)/shard_map/ppermute | solution.py:261
  18.5 12.6 %collective-permute-start.1 = (bf16[4,256,1024]{2,1,0:T(8,128)(2,1)}, bf16[4,256,1024]{2,1,0:T(8,128)(2,1)}, u32[]{:S(2)}, u32[]{:S(2)}) collective-permute-start(bf16[4,256,1024]{2,1,0:T(8,128)(2,1)} %get-tuple-element.10.own_ref), channel_id=1, source_target_pairs={{0,32},{32,0},{64,96},{96,64},{128,160},{160,128},{192,224},{224,1... | collective-permute-start | bytes 6291464 | tf_op jit(solution)/shard_map/ppermute | solution.py:260
  22.8 2.2 %copy-start.1 = (bf16[1024,2048]{1,0:T(8,128)(2,1)S(1)}, bf16[1024,2048]{1,0:T(8,128)(2,1)}, u32[]{:S(2)}) copy-start(bf16[1024,2048]{1,0:T(8,128)(2,1)} %copy-done) | copy-start | bytes 12582916
  28.7 6.2 %copy-start.4 = (s32[12,2]{0,1:T(2,128)S(1)}, s32[12,2]{0,1:T(2,128)}, u32[]{:S(2)}) copy-start(s32[12,2]{0,1:T(2,128)} %param.3) | copy-start | bytes 292
  28.7 6.2 %collective-permute-start.3 = (bf16[4,256,1024]{2,1,0:T(8,128)(2,1)S(1)}, bf16[4,256,1024]{2,1,0:T(8,128)(2,1)}, u32[]{:S(2)}, u32[]{:S(2)}) collective-permute-start(bf16[4,256,1024]{2,1,0:T(8,128)(2,1)S(1)} %near.1.near_ref), channel_id=1, source_target_pairs={{0,32},{32,0},{64,96},{96,64},{128,160},{160,128},{192,224},{224,1... | collective-permute-start | bytes 6291464 | tf_op jit(solution)/shard_map/ppermute | solution.py:264
  34.9 2.2 %copy-start.2 = (bf16[1024,2048]{1,0:T(8,128)(2,1)S(1)}, bf16[1024,2048]{1,0:T(8,128)(2,1)}, u32[]{:S(2)}) copy-start(bf16[1024,2048]{1,0:T(8,128)(2,1)} %copy-done) | copy-start | bytes 12582916

commit v4 on v3

v4 whole, which is shorter than its diff:
```python
import math

import jax
import jax.numpy as jnp
from jax import lax
from jax.experimental import pallas as pl
from jax.experimental.pallas import tpu as pltpu
from jax.sharding import PartitionSpec as P

LANES = 128
ROWS_PERIOD = 16
SPLIT = 32
GROUPS = 5
SLOTS_PER_STEP = 6
MIB = 1024 * 1024


def table_parts(samples):
    shape = (4 * SPLIT + samples // LANES * ROWS_PERIOD, LANES)
    row = lax.broadcasted_iota(jnp.int32, shape, 0)
    bin_low = lax.broadcasted_iota(jnp.int32, shape, 1) + 1
    part = row // SPLIT
    at = row % SPLIT
    step_row = row - 4 * SPLIT
    phases = jnp.where(
        part == 0,
        bin_low * at * SPLIT,
        jnp.where(
            part == 1,
            bin_low * at,
            jnp.where(
                part == 2,
                2 * SPLIT * at,
                jnp.where(part == 3, 2 * at, (step_row // ROWS_PERIOD) * (step_row % ROWS_PERIOD) * LANES),
            ),
        ),
    )
    angles = (phases % (2 * samples)).astype(jnp.float32) * (math.pi / samples)
    return jnp.cos(angles), jnp.sin(angles)


def whiten_bins(x, table, out_ref, bins):
    blocks, channels, samples = x.shape
    spectra = jnp.dot(x.reshape(blocks * channels, samples), table, preferred_element_type=jnp.float32)
    for block in range(blocks):
        part = spectra[block * channels : (block + 1) * channels]
        real, imag = part[:, :LANES], part[:, LANES:]
        power = jnp.sum(real * real + imag * imag, axis=0, keepdims=True) * (1.0 / channels)
        scale = 1.0 / jnp.sqrt(power + 1e-05)
        out_ref[block, :channels, bins] = (real * scale).astype(jnp.bfloat16)
        out_ref[block, channels:, bins] = (imag * scale).astype(jnp.bfloat16)


def first_kernel(cos_ref, sin_ref, x_ref, table_ref, out_ref, again_ref, low_cos_ref, low_sin_ref):
    samples = x_ref.shape[2]
    again_ref[...] = x_ref[...]
    rows = lambda ref, part: ref[part * SPLIT : (part + 1) * SPLIT, :]
    for at in range(samples // SPLIT):
        high = lambda ref, part: ref[part * SPLIT + at : part * SPLIT + at + 1, :]
        taper = 0.5 - 0.5 * (high(cos_ref, 2) * rows(cos_ref, 3) - high(sin_ref, 2) * rows(sin_ref, 3))
        cos = high(cos_ref, 0) * rows(cos_ref, 1) - high(sin_ref, 0) * rows(sin_ref, 1)
        sin = high(sin_ref, 0) * rows(cos_ref, 1) + high(cos_ref, 0) * rows(sin_ref, 1)
        low_cos_ref[at * SPLIT : (at + 1) * SPLIT, :] = taper * cos
        low_sin_ref[at * SPLIT : (at + 1) * SPLIT, :] = taper * sin

    shape = (samples // ROWS_PERIOD, ROWS_PERIOD, LANES)
    for step in range(samples // LANES):
        low_cos = low_cos_ref[...].reshape(shape)
        low_sin = low_sin_ref[...].reshape(shape)
        step_rows = slice(4 * SPLIT + step * ROWS_PERIOD, 4 * SPLIT + (step + 1) * ROWS_PERIOD)
        step_cos = cos_ref[step_rows, :][None]
        step_sin = sin_ref[step_rows, :][None]
        real = low_cos * step_cos - low_sin * step_sin
        imag = -(low_sin * step_cos + low_cos * step_sin)
        columns = slice(2 * step * LANES, (2 * step + 1) * LANES)
        table_ref[:, columns] = real.reshape(samples, LANES).astype(jnp.bfloat16)
        columns = slice((2 * step + 1) * LANES, (2 * step + 2) * LANES)
        table_ref[:, columns] = imag.reshape(samples, LANES).astype(jnp.bfloat16)
    whiten_all(x_ref, table_ref, out_ref)


def whiten_all(x_ref, table_ref, out_ref):
    x = x_ref[...]
    for step in range(x.shape[2] // LANES):
        table = table_ref[:, 2 * step * LANES : 2 * (step + 1) * LANES]
        whiten_bins(x, table, out_ref, slice(step * LANES, (step + 1) * LANES))


def hint(work):
    return pl.CostEstimate(flops=work, bytes_accessed=1 << 16, transcendentals=0)


def pinned(*arrays):
    return tuple(pltpu.with_memory_space_constraint(array, pltpu.VMEM) for array in arrays)


HERE = pl.BlockSpec(memory_space=pltpu.VMEM)


def whiten_first(x, parts):
    blocks, channels, samples = x.shape
    return pl.pallas_call(
        first_kernel,
        in_specs=[HERE] * 3,
        out_specs=[HERE] * 3,
        out_shape=[
            pltpu.VMEM((samples, 2 * samples), jnp.bfloat16),
            pltpu.VMEM((blocks, 2 * channels, samples), jnp.bfloat16),
            pltpu.VMEM(x.shape, x.dtype),
        ],
        scratch_shapes=[pltpu.VMEM((samples, LANES), jnp.float32)] * 2,
        compiler_params=pltpu.CompilerParams(vmem_limit_bytes=12 * MIB),
        cost_estimate=hint(blocks * channels * samples),
        name="table_and_own",
    )(*pinned(*parts, x))


def whiten_next(x, table, name):
    blocks, channels, samples = x.shape
    return pl.pallas_call(
        whiten_all,
        in_specs=[HERE] * 2,
        out_specs=HERE,
        out_shape=pltpu.VMEM((blocks, 2 * channels, samples), jnp.bfloat16),
        compiler_params=pltpu.CompilerParams(vmem_limit_bytes=12 * MIB),
        cost_estimate=hint(blocks * channels * samples),
        name=name,
    )(*pinned(x, table))


def last_kernel(
    owner_ref, slots_ref, x_ref, table_ref, own_ref, sibling_ref, near_ref, passed_ref, out_ref, window_ref, sems
):
    step = pl.program_id(0)
    blocks, channels, samples = x_ref.shape

    @pl.when(step == 0)
    def _():
        parts = ((own_ref, 0), (sibling_ref, 1), (near_ref, 2), (passed_ref, 4))
        copies = [
            pltpu.make_async_copy(ref, window_ref.at[pl.ds(place * blocks, blocks)], sems.at[at])
            for at, (ref, place) in enumerate(parts)
        ]
        for copy in copies:
            copy.start()
        whiten_all(x_ref, table_ref, window_ref.at[pl.ds(3 * blocks, blocks)])
        for copy in copies:
            copy.wait()

    @pl.when(step > 0)
    def _():
        owner = owner_ref[0]

        def place(block):
            block = jnp.where(block >= 0, block, owner * blocks)
            away = (lax.div(block, blocks) - owner) * (1 - 2 * lax.rem(owner, 2))
            return lax.rem(away + GROUPS, GROUPS) * blocks + lax.rem(block, blocks)

        found = []
        for at in range(SLOTS_PER_STEP):
            slot = (step - 1) * SLOTS_PER_STEP + at
            first, second = slots_ref[0, slot], slots_ref[1, slot]
            product = lax.dot_general(
                window_ref[place(first)],
                window_ref[place(second)],
                (((1,), (1,)), ((), ())),
                preferred_element_type=jnp.float32,
            )
            real = product[:channels, :channels] + product[channels:, channels:]
            imag = product[channels:, :channels] - product[:channels, channels:]
            live = jnp.where(first >= 0, 0.25, 0.0)
            both = jnp.concatenate([real, imag], axis=1) * live
            found.append(both.reshape(channels // 8, 8, 2 * channels))
        for pair in range(SLOTS_PER_STEP // 2):
            first, second = found[2 * pair], found[2 * pair + 1]
            row = lax.broadcasted_iota(jnp.int32, first.shape, 1)
            rows = slice(8 * pair, 8 * (pair + 1))
            out_ref[:, 0, rows] = jnp.where(row < 4, first, pltpu.roll(second, 4, 1))
            out_ref[:, 1, rows] = jnp.where(row < 4, pltpu.roll(first, 4, 1), second)


def far_and_pairs(owner, slots, x, table, own, sibling, near, passed):
    blocks, channels, samples = x.shape
    slot_count = slots.shape[0]
    return pl.pallas_call(
        last_kernel,
        grid_spec=pltpu.PrefetchScalarGridSpec(
            num_scalar_prefetch=2,
            grid=(1 + slot_count // SLOTS_PER_STEP,),
            in_specs=[HERE] * 6,
            out_specs=pl.BlockSpec(
                (channels // 8, 2, 4 * SLOTS_PER_STEP, 2 * channels), lambda i, *_: (0, 0, jnp.maximum(i - 1, 0), 0)
            ),
            scratch_shapes=[
                pltpu.VMEM((GROUPS * blocks, 2 * channels, samples), jnp.bfloat16),
                pltpu.SemaphoreType.DMA((4,)),
            ],
        ),
        out_shape=pltpu.VMEM((channels // 8, 2, slot_count * 4, 2 * channels), jnp.float32),
        compiler_params=pltpu.CompilerParams(vmem_limit_bytes=20 * MIB),
        cost_estimate=hint(slot_count * channels * samples),
        name="far_and_pairs",
    )(owner, slots.T, *pinned(x, table, own, sibling, near, passed))


def after_transfer(x, work):
    anywhere = pl.BlockSpec(memory_space=pl.ANY)
    return pl.pallas_call(
        lambda x_ref, out_ref: None,
        in_specs=[anywhere],
        out_specs=anywhere,
        out_shape=jax.ShapeDtypeStruct(x.shape, x.dtype),
        input_output_aliases={0: 0},
        cost_estimate=hint(work),
        name="far_arrived",
    )(x)


def on_device(strain, pair_slots):
    x = strain[0]
    blocks, channels, samples = x.shape
    owners = lax.axis_size("chan")
    windows = lax.axis_size("tm")
    slot_count = pair_slots.shape[0]
    owner = lax.axis_index("chan")
    even = range(0, owners, 2)
    odd = range(1, owners, 2)
    sibling_pairs = [(i, i ^ 1) for i in range(owners)]
    near_pairs = [((i + 2) % owners, i) for i in even] + [((i - 2) % owners, i) for i in odd]
    far_pairs = [((i - 2) % owners, i) for i in even] + [((i + 2) % owners, i) for i in odd]

    near = lax.ppermute(x, "chan", near_pairs)
    table, own, again = whiten_first(x, table_parts(samples))
    sibling = lax.ppermute(own, "chan", sibling_pairs)
    far = lax.ppermute(again, "chan", far_pairs)
    far = after_transfer(far, 100 * 10**9)
    near = whiten_next(near, table, "near")
    passed = lax.ppermute(near, "chan", sibling_pairs)
    products = far_and_pairs(owner.reshape(1), pair_slots, far, table, own, sibling, near, passed)

    rows = channels // windows
    products = products.reshape(windows, slot_count * rows, 2 * channels).astype(jnp.float16)
    arrived = lax.all_to_all(products, "tm", 0, 0, tiled=True)
    total = jnp.sum(arrived.astype(jnp.float32), axis=0) * (4.0 / (samples * windows))
    return jnp.transpose(total.reshape(slot_count, rows, 2 * channels), (1, 0, 2))


def solution(mesh):
    return jax.shard_map(
        on_device,
        mesh=mesh,
        in_specs=(P("tm", "chan", None, None), P("chan", None)),
        out_specs=P("tm", "chan", None),
        check_vma=False,
    )
```

time: 79.9 us -> 79.8 us (level)
    pallas_call x2, Pallas kernels: 9.28 us -> 8.15 us  [the longest x1 5.36 us: whiten_first(): pl.pallas_call(first_kernel, in_specs=[HERE] * 3, out_specs=[HERE] * 3, o...]
  transfers between devices with their start and end apart: 4 -> 4, of which waited for: 3 -> 3; matrix products, arithmetic and copies ran while one was open for 1% -> 1% of each run, Pallas kernels for 12% -> 10%
where the time goes in v4:
time: 79.8 us; the launch traced here: 79.3 us
  blocking collectives  32.6 us (41%)
  Pallas kernels  17.6 us (22%)
  starting transfers between devices  12.8 us (16%)
  local copies, waits for them, and re-layouts  8.19 us (10%)
  waiting for transfers between devices  6.94 us (9%)
  other arithmetic  1.07 us (1%)
    all_to_all x1, blocking collectives, on_device(): arrived = lax.all_to_all(products, 'tm', 0, 0, tiled=True)  32.6 us
    pallas_call x1, Pallas kernels, far_and_pairs(): pl.pallas_call(last_kernel, grid_spec=pltpu.PrefetchScalarGridSpec(num_sc...  9.44 us
    unnamed x10, local copies, waits for them, and re-layouts  7.55 us
    ppermute x1, starting transfers between devices, on_device(): far = lax.ppermute(again, 'chan', far_pairs)  5.7 us
    pallas_call x1, Pallas kernels, whiten_first(): pl.pallas_call(first_kernel, in_specs=[HERE] * 3, out_specs=[HERE] * 3, o...  5.36 us
    ppermute x1, starting transfers between devices, on_device(): near = lax.ppermute(x, 'chan', near_pairs)  3.25 us
    ppermute x1, waiting for transfers between devices, on_device(): passed = lax.ppermute(near, 'chan', sibling_pairs)  3.19 us
    pallas_call x1, Pallas kernels, whiten_next(): pl.pallas_call(whiten_all, in_specs=[HERE] * 2, out_specs=HERE, out_shape...  2.79 us
  transfers between devices with their start and end apart: 4, of which 3 were waited for; matrix products, arithmetic and copies ran while one was open for 1% of the time, Pallas kernels for 10%

profile of v4, /device:TPU:56, one launch (start us, length us, event | category | flops | bytes accessed | tf_op | source)
XLA Modules:
  0.0 79.3 jit_solution(10123095625698852928)
XLA Ops:
  0.0 3.2 %collective-permute-start.2 = (bf16[4,128,1024]{2,1,0:T(8,128)(2,1)}, bf16[4,128,1024]{2,1,0:T(8,128)(2,1)S(1)}, u32[]{:S(2)}, u32[]{:S(2)}) collective-permute-start(bf16[4,128,1024]{2,1,0:T(8,128)(2,1)} %bitcast.5), channel_id=1, source_target_pairs={{64,0},{128,64},{192,128},{256,192},{320,256},{384,320},{448,384},... | collective-permute-start | bytes 3145736 | tf_op jit(solution)/shard_map/ppermute | solution.py:232
  3.3 0.7 fusion.8
  4.1 0.0 copy-start.3
  4.1 1.2 %copy-done.3 = bf16[1,4,128,1024]{3,2,1,0:T(8,128)(2,1)S(1)} copy-done((bf16[1,4,128,1024]{3,2,1,0:T(8,128)(2,1)S(1)}, bf16[1,4,128,1024]{3,2,1,0:T(8,128)(2,1)}, u32[]{:S(2)}) %copy-start.3) | copy-done | bytes 1048600
  5.3 5.4 %table_and_own.1 = (bf16[1024,2048]{1,0:T(8,128)(2,1)S(1)}, bf16[4,256,1024]{2,1,0:T(8,128)(2,1)}, bf16[4,128,1024]{2,1,0:T(8,128)(2,1)}) custom-call(f32[256,128]{1,0:T(8,128)S(1)} %get-tuple-element.12.cos_ref, f32[256,128]{1,0:T(8,128)S(1)} %get-tuple-element.11.sin_ref, bf16[4,128,1024]{2,1,0:T(8,128)(2,1)S(1)} %bitcast.6), custom_call_target="tpu_custom_call" | custom-call | flops 524288 | bytes 65536 | tf_op jit(solution)/shard_map/table_and_own/pallas_call | solution.py:102
  10.7 0.0 copy-start
  10.7 1.9 %copy-done = bf16[1024,2048]{1,0:T(8,128)(2,1)} copy-done((bf16[1024,2048]{1,0:T(8,128)(2,1)}, bf16[1024,2048]{1,0:T(8,128)(2,1)S(1)}, u32[]{:S(2)}) %copy-start) | copy-done | bytes 4194328
  12.6 5.7 %collective-permute-start = (bf16[4,128,1024]{2,1,0:T(8,128)(2,1)}, bf16[4,128,1024]{2,1,0:T(8,128)(2,1)}, u32[]{:S(2)}, u32[]{:S(2)}) collective-permute-start(bf16[4,128,1024]{2,1,0:T(8,128)(2,1)} %get-tuple-element.8), channel_id=1, source_target_pairs={{448,0},{0,64},{64,128},{128,192},{192,256},{256,320},{320,384},{3... | collective-permute-start | bytes 3145736 | tf_op jit(solution)/shard_map/ppermute | solution.py:235
  18.3 1.9 %collective-permute-start.1 = (bf16[4,256,1024]{2,1,0:T(8,128)(2,1)}, bf16[4,256,1024]{2,1,0:T(8,128)(2,1)}, u32[]{:S(2)}, u32[]{:S(2)}) collective-permute-start(bf16[4,256,1024]{2,1,0:T(8,128)(2,1)} %get-tuple-element.10.own_ref), channel_id=1, source_target_pairs={{0,32},{32,0},{64,96},{96,64},{128,160},{160,128},{192,224},{224,1... | collective-permute-start | bytes 6291464 | tf_op jit(solution)/shard_map/ppermute | solution.py:234
  20.3 2.7 %collective-permute-done.2.x_ref = bf16[4,128,1024]{2,1,0:T(8,128)(2,1)S(1)} collective-permute-done((bf16[4,128,1024]{2,1,0:T(8,128)(2,1)}, bf16[4,128,1024]{2,1,0:T(8,128)(2,1)S(1)}, u32[]{:S(2)}, u32[]{:S(2)}) %collective-permute-start.2) | collective-permute-done | bytes 1048608 | tf_op jit(solution)/shard_map/ppermute | solution.py:232
  23.0 2.2 %copy-done.1 = bf16[1024,2048]{1,0:T(8,128)(2,1)S(1)} copy-done((bf16[1024,2048]{1,0:T(8,128)(2,1)S(1)}, bf16[1024,2048]{1,0:T(8,128)(2,1)}, u32[]{:S(2)}) %copy-start.1) | copy-done | bytes 4194328
  25.1 2.8 %near.1.near_ref = bf16[4,256,1024]{2,1,0:T(8,128)(2,1)S(1)} custom-call(bf16[4,128,1024]{2,1,0:T(8,128)(2,1)S(1)} %collective-permute-done.2.x_ref, bf16[1024,2048]{1,0:T(8,128)(2,1)S(1)} %copy-done.1), custom_call_target="tpu_custom_call" | custom-call | flops 524288 | bytes 65536 | tf_op jit(solution)/shard_map/near/pallas_call | solution.py:120
  27.9 0.0 copy-start.4
  28.0 1.9 %collective-permute-start.3 = (bf16[4,256,1024]{2,1,0:T(8,128)(2,1)S(1)}, bf16[4,256,1024]{2,1,0:T(8,128)(2,1)}, u32[]{:S(2)}, u32[]{:S(2)}) collective-permute-start(bf16[4,256,1024]{2,1,0:T(8,128)(2,1)S(1)} %near.1.near_ref), channel_id=1, source_target_pairs={{0,32},{32,0},{64,96},{96,64},{128,160},{160,128},{192,224},{224,1... | collective-permute-start | bytes 6291464 | tf_op jit(solution)/shard_map/ppermute | solution.py:238
  29.9 1.1 %collective-permute-done.x_ref = bf16[4,128,1024]{2,1,0:T(8,128)(2,1)} collective-permute-done((bf16[4,128,1024]{2,1,0:T(8,128)(2,1)}, bf16[4,128,1024]{2,1,0:T(8,128)(2,1)}, u32[]{:S(2)}, u32[]{:S(2)}) %collective-permute-start) | collective-permute-done | bytes 1048608 | tf_op jit(solution)/shard_map/ppermute | solution.py:235
  30.9 0.0 collective-permute-done.1.sibling_ref
  30.9 3.2 %collective-permute-done.3.passed_ref = bf16[4,256,1024]{2,1,0:T(8,128)(2,1)} collective-permute-done((bf16[4,256,1024]{2,1,0:T(8,128)(2,1)S(1)}, bf16[4,256,1024]{2,1,0:T(8,128)(2,1)}, u32[]{:S(2)}, u32[]{:S(2)}) %collective-permute-start.3) | collective-permute-done | bytes 2097184 | tf_op jit(solution)/shard_map/ppermute | solution.py:238
  34.1 0.0 copy-done.4
  34.1 2.2 %copy-done.2 = bf16[1024,2048]{1,0:T(8,128)(2,1)S(1)} copy-done((bf16[1024,2048]{1,0:T(8,128)(2,1)S(1)}, bf16[1024,2048]{1,0:T(8,128)(2,1)}, u32[]{:S(2)}) %copy-start.2) | copy-done | bytes 4194328
  36.3 9.4 %far_and_pairs.1 = f32[16,2,48,256]{3,2,1,0:T(8,128)S(1)} custom-call(s32[1]{0:T(128)} %bitcast.owner_ref, s32[2,12]{1,0:T(2,128)S(1)} %bitcast.7, bf16[4,128,1024]{2,1,0:T(8,128)(2,1)} %far_arrived.1.x_ref, bf16[1024,2048]{1,0:T(8,128)(2,1)S(1)} %copy-done.2, bf16[4,256,1024]{2,1,0:T(8,128)(2,1)} %get-tuple-element.10.own_ref, ...), custom_call_target="tpu_custom_call" | custom-call | flops 1572864 | bytes 65536 | tf_op jit(solution)/shard_map/far_and_pairs/pallas_call | solution.py:185
  45.8 0.2 convert_element_type.15
  45.9 32.6 %all_to_all.5 = f16[32,48,256]{2,1,0:T(8,128)(2,1)S(1)} all-to-all(f16[32,48,256]{2,1,0:T(8,128)(2,1)S(1)} %bitcast.8), channel_id=1, replica_groups=mesh['chan'=16,'tm'=32] {'tm'}, dimensions={0} | all-to-all | bytes 1572864 | tf_op jit(solution)/shard_map/all_to_all | solution.py:243
  78.5 0.1 convert_reduce_fusion
  78.6 0.6 mul.64
  (11 shorter events, 0.1 us)
Async XLA Ops:
  0.0 23.0 %collective-permute-start.2 = (bf16[4,128,1024]{2,1,0:T(8,128)(2,1)}, bf16[4,128,1024]{2,1,0:T(8,128)(2,1)S(1)}, u32[]{:S(2)}, u32[]{:S(2)}) collective-permute-start(bf16[4,128,1024]{2,1,0:T(8,128)(2,1)} %bitcast.5), channel_id=1, source_target_pairs={{64,0},{128,64},{192,128},{256,192},{320,256},{384,320},{448,384},... | collective-permute-start | bytes 3145736 | tf_op jit(solution)/shard_map/ppermute | solution.py:232
  4.1 1.2 %copy-start.3 = (bf16[1,4,128,1024]{3,2,1,0:T(8,128)(2,1)S(1)}, bf16[1,4,128,1024]{3,2,1,0:T(8,128)(2,1)}, u32[]{:S(2)}) copy-start(bf16[1,4,128,1024]{3,2,1,0:T(8,128)(2,1)} %param.2) | copy-start | bytes 3145732
  10.7 1.9 %copy-start = (bf16[1024,2048]{1,0:T(8,128)(2,1)}, bf16[1024,2048]{1,0:T(8,128)(2,1)S(1)}, u32[]{:S(2)}) copy-start(bf16[1024,2048]{1,0:T(8,128)(2,1)S(1)} %get-tuple-element.9.table_ref) | copy-start | bytes 12582916
  12.6 18.3 %collective-permute-start = (bf16[4,128,1024]{2,1,0:T(8,128)(2,1)}, bf16[4,128,1024]{2,1,0:T(8,128)(2,1)}, u32[]{:S(2)}, u32[]{:S(2)}) collective-permute-start(bf16[4,128,1024]{2,1,0:T(8,128)(2,1)} %get-tuple-element.8), channel_id=1, source_target_pairs={{448,0},{0,64},{64,128},{128,192},{192,256},{256,320},{320,384},{3... | collective-permute-start | bytes 3145736 | tf_op jit(solution)/shard_map/ppermute | solution.py:235
  18.3 12.6 %collective-permute-start.1 = (bf16[4,256,1024]{2,1,0:T(8,128)(2,1)}, bf16[4,256,1024]{2,1,0:T(8,128)(2,1)}, u32[]{:S(2)}, u32[]{:S(2)}) collective-permute-start(bf16[4,256,1024]{2,1,0:T(8,128)(2,1)} %get-tuple-element.10.own_ref), channel_id=1, source_target_pairs={{0,32},{32,0},{64,96},{96,64},{128,160},{160,128},{192,224},{224,1... | collective-permute-start | bytes 6291464 | tf_op jit(solution)/shard_map/ppermute | solution.py:234
  23.0 2.2 %copy-start.1 = (bf16[1024,2048]{1,0:T(8,128)(2,1)S(1)}, bf16[1024,2048]{1,0:T(8,128)(2,1)}, u32[]{:S(2)}) copy-start(bf16[1024,2048]{1,0:T(8,128)(2,1)} %copy-done) | copy-start | bytes 12582916
  27.9 6.2 %copy-start.4 = (s32[12,2]{0,1:T(2,128)S(1)}, s32[12,2]{0,1:T(2,128)}, u32[]{:S(2)}) copy-start(s32[12,2]{0,1:T(2,128)} %param.3) | copy-start | bytes 292
  28.0 6.2 %collective-permute-start.3 = (bf16[4,256,1024]{2,1,0:T(8,128)(2,1)S(1)}, bf16[4,256,1024]{2,1,0:T(8,128)(2,1)}, u32[]{:S(2)}, u32[]{:S(2)}) collective-permute-start(bf16[4,256,1024]{2,1,0:T(8,128)(2,1)S(1)} %near.1.near_ref), channel_id=1, source_target_pairs={{0,32},{32,0},{64,96},{96,64},{128,160},{160,128},{192,224},{224,1... | collective-permute-start | bytes 6291464 | tf_op jit(solution)/shard_map/ppermute | solution.py:238
  34.1 2.2 %copy-start.2 = (bf16[1024,2048]{1,0:T(8,128)(2,1)S(1)}, bf16[1024,2048]{1,0:T(8,128)(2,1)}, u32[]{:S(2)}) copy-start(bf16[1024,2048]{1,0:T(8,128)(2,1)} %copy-done) | copy-start | bytes 12582916

commit v5 on v4

--- a/solution.py
+++ b/solution.py
@@ -51,9 +51,10 @@
         out_ref[block, channels:, bins] = (imag * scale).astype(jnp.bfloat16)
 
 
-def first_kernel(cos_ref, sin_ref, x_ref, table_ref, out_ref, again_ref, low_cos_ref, low_sin_ref):
+def first_kernel(cos_ref, sin_ref, x_ref, table_ref, out_ref, again_ref, low_cos_ref, low_sin_ref, sem):
     samples = x_ref.shape[2]
-    again_ref[...] = x_ref[...]
+    fetch = pltpu.make_async_copy(x_ref, again_ref, sem)
+    fetch.start()
     rows = lambda ref, part: ref[part * SPLIT : (part + 1) * SPLIT, :]
     for at in range(samples // SPLIT):
         high = lambda ref, part: ref[part * SPLIT + at : part * SPLIT + at + 1, :]
@@ -76,7 +77,8 @@
         table_ref[:, columns] = real.reshape(samples, LANES).astype(jnp.bfloat16)
         columns = slice((2 * step + 1) * LANES, (2 * step + 2) * LANES)
         table_ref[:, columns] = imag.reshape(samples, LANES).astype(jnp.bfloat16)
-    whiten_all(x_ref, table_ref, out_ref)
+    fetch.wait()
+    whiten_all(again_ref, table_ref, out_ref)
 
 
 def whiten_all(x_ref, table_ref, out_ref):
@@ -101,18 +103,18 @@
     blocks, channels, samples = x.shape
     return pl.pallas_call(
         first_kernel,
-        in_specs=[HERE] * 3,
+        in_specs=[HERE, HERE, pl.BlockSpec(memory_space=pl.ANY)],
         out_specs=[HERE] * 3,
         out_shape=[
             pltpu.VMEM((samples, 2 * samples), jnp.bfloat16),
             pltpu.VMEM((blocks, 2 * channels, samples), jnp.bfloat16),
             pltpu.VMEM(x.shape, x.dtype),
         ],
-        scratch_shapes=[pltpu.VMEM((samples, LANES), jnp.float32)] * 2,
+        scratch_shapes=[pltpu.VMEM((samples, LANES), jnp.float32)] * 2 + [pltpu.SemaphoreType.DMA],
         compiler_params=pltpu.CompilerParams(vmem_limit_bytes=12 * MIB),
         cost_estimate=hint(blocks * channels * samples),
         name="table_and_own",
-    )(*pinned(*parts, x))
+    )(*pinned(*parts), pltpu.with_memory_space_constraint(x, pltpu.HBM))
 
 
 def whiten_next(x, table, name):
@@ -211,6 +213,7 @@
         out_specs=anywhere,
         out_shape=jax.ShapeDtypeStruct(x.shape, x.dtype),
         input_output_aliases={0: 0},
+        compiler_params=pltpu.CompilerParams(vmem_limit_bytes=MIB),
         cost_estimate=hint(work),
         name="far_arrived",
     )(x)

time: 79.8 us -> 78.2 us (0.980)
  waiting for transfers between devices: 6.94 us -> 11.2 us
  local copies, waits for them, and re-layouts: 8.19 us -> 4.77 us
  Pallas kernels: 17.6 us -> 15.3 us
    ppermute x1, waiting for transfers between devices: 2.69 us -> 7.15 us  [on_device(): near = lax.ppermute(x, 'chan', near_pairs)]
    unnamed x10 -> x8, local copies, waits for them, and re-layouts: 7.55 us -> 4.14 us
    pallas_call x1, Pallas kernels: 9.44 us -> 8.18 us  [far_and_pairs(): pl.pallas_call(last_kernel, grid_spec=pltpu.PrefetchScalarGridSpec(num_sc...]
    ppermute x1, waiting for transfers between devices: 1.06 us -> 0.01 us  [on_device(): far = lax.ppermute(again, 'chan', far_pairs)]
    pallas_call x1, Pallas kernels: 5.36 us -> 4.35 us  [whiten_first(): pl.pallas_call(first_kernel, in_specs=[HERE, HERE, pl.BlockSpec(memory_sp...]
    ppermute x1, waiting for transfers between devices: 3.19 us -> 4.08 us  [on_device(): passed = lax.ppermute(near, 'chan', sibling_pairs)]
  transfers between devices with their start and end apart: 4 -> 4, of which waited for: 3 -> 2; matrix products, arithmetic and copies ran while one was open for 1% -> 1% of each run, Pallas kernels for 10% -> 9%
where the time goes in v5:
time: 78.2 us; the launch traced here: 77.9 us
  blocking collectives  32.5 us (42%)
  Pallas kernels  15.3 us (20%)
  starting transfers between devices  12.8 us (16%)
  waiting for transfers between devices  11.2 us (14%)
  local copies, waits for them, and re-layouts  4.77 us (6%)
  other arithmetic  1.08 us (1%)
    all_to_all x1, blocking collectives, on_device(): arrived = lax.all_to_all(products, 'tm', 0, 0, tiled=True)  32.5 us
    pallas_call x1, Pallas kernels, far_and_pairs(): pl.pallas_call(last_kernel, grid_spec=pltpu.PrefetchScalarGridSpec(num_sc...  8.18 us
    ppermute x1, waiting for transfers between devices, on_device(): near = lax.ppermute(x, 'chan', near_pairs)  7.15 us
    ppermute x1, starting transfers between devices, on_device(): far = lax.ppermute(again, 'chan', far_pairs)  5.7 us
    pallas_call x1, Pallas kernels, whiten_first(): pl.pallas_call(first_kernel, in_specs=[HERE, HERE, pl.BlockSpec(memory_sp...  4.35 us
    unnamed x8, local copies, waits for them, and re-layouts  4.14 us
    ppermute x1, waiting for transfers between devices, on_device(): passed = lax.ppermute(near, 'chan', sibling_pairs)  4.08 us
    ppermute x1, starting transfers between devices, on_device(): near = lax.ppermute(x, 'chan', near_pairs)  3.25 us
  transfers between devices with their start and end apart: 4, of which 2 were waited for; matrix products, arithmetic and copies ran while one was open for 1% of the time, Pallas kernels for 9%

profile of v5, /device:TPU:56, one launch (start us, length us, event | category | flops | bytes accessed | tf_op | source)
XLA Modules:
  0.0 77.9 jit_solution(6862679363359185658)
XLA Ops:
  0.0 3.2 %collective-permute-start.2 = (bf16[4,128,1024]{2,1,0:T(8,128)(2,1)}, bf16[4,128,1024]{2,1,0:T(8,128)(2,1)S(1)}, u32[]{:S(2)}, u32[]{:S(2)}) collective-permute-start(bf16[4,128,1024]{2,1,0:T(8,128)(2,1)} %bitcast.7), channel_id=1, source_target_pairs={{64,0},{128,64},{192,128},{256,192},{320,256},{384,320},{448,384},... | collective-permute-start | bytes 3145736 | tf_op jit(solution)/shard_map/ppermute | solution.py:235
  3.3 0.7 fusion.8
  4.1 4.4 %table_and_own.1 = (bf16[1024,2048]{1,0:T(8,128)(2,1)S(1)}, bf16[4,256,1024]{2,1,0:T(8,128)(2,1)S(1)}, bf16[4,128,1024]{2,1,0:T(8,128)(2,1)}) custom-call(f32[256,128]{1,0:T(8,128)S(1)} %get-tuple-element.12.cos_ref, f32[256,128]{1,0:T(8,128)S(1)} %get-tuple-element.11.sin_ref, bf16[4,128,1024]{2,1,0:T(8,128)(2,1)} %bitcast.8), custom_call_target="tpu_custom_call" | custom-call | flops 524288 | bytes 65536 | tf_op jit(solution)/shard_map/table_and_own/pallas_call | solution.py:104
  8.4 0.0 copy-start
  8.5 1.9 %copy-done = bf16[1024,2048]{1,0:T(8,128)(2,1)} copy-done((bf16[1024,2048]{1,0:T(8,128)(2,1)}, bf16[1024,2048]{1,0:T(8,128)(2,1)S(1)}, u32[]{:S(2)}) %copy-start) | copy-done | bytes 4194328
  10.4 5.7 %collective-permute-start = (bf16[4,128,1024]{2,1,0:T(8,128)(2,1)}, bf16[4,128,1024]{2,1,0:T(8,128)(2,1)}, u32[]{:S(2)}, u32[]{:S(2)}) collective-permute-start(bf16[4,128,1024]{2,1,0:T(8,128)(2,1)} %get-tuple-element.8), channel_id=1, source_target_pairs={{448,0},{0,64},{64,128},{128,192},{192,256},{256,320},{320,384},{3... | collective-permute-start | bytes 3145736 | tf_op jit(solution)/shard_map/ppermute | solution.py:238
  16.1 1.9 %collective-permute-start.1 = (bf16[4,256,1024]{2,1,0:T(8,128)(2,1)S(1)}, bf16[4,256,1024]{2,1,0:T(8,128)(2,1)}, u32[]{:S(2)}, u32[]{:S(2)}) collective-permute-start(bf16[4,256,1024]{2,1,0:T(8,128)(2,1)S(1)} %get-tuple-element.10.own_ref), channel_id=1, source_target_pairs={{0,32},{32,0},{64,96},{96,64},{128,160},{160,128},{192,224},{224,1... | collective-permute-start | bytes 6291464 | tf_op jit(solution)/shard_map/ppermute | solution.py:237
  18.0 7.2 %collective-permute-done.2.x_ref = bf16[4,128,1024]{2,1,0:T(8,128)(2,1)S(1)} collective-permute-done((bf16[4,128,1024]{2,1,0:T(8,128)(2,1)}, bf16[4,128,1024]{2,1,0:T(8,128)(2,1)S(1)}, u32[]{:S(2)}, u32[]{:S(2)}) %collective-permute-start.2) | collective-permute-done | bytes 1048608 | tf_op jit(solution)/shard_map/ppermute | solution.py:235
  25.2 0.0 copy-start.1
  25.2 2.2 %copy-done.1 = bf16[1024,2048]{1,0:T(8,128)(2,1)S(1)} copy-done((bf16[1024,2048]{1,0:T(8,128)(2,1)S(1)}, bf16[1024,2048]{1,0:T(8,128)(2,1)}, u32[]{:S(2)}) %copy-start.1) | copy-done | bytes 4194328
  27.4 2.8 %near.1.near_ref = bf16[4,256,1024]{2,1,0:T(8,128)(2,1)S(1)} custom-call(bf16[4,128,1024]{2,1,0:T(8,128)(2,1)S(1)} %collective-permute-done.2.x_ref, bf16[1024,2048]{1,0:T(8,128)(2,1)S(1)} %copy-done.1), custom_call_target="tpu_custom_call" | custom-call | flops 524288 | bytes 65536 | tf_op jit(solution)/shard_map/near/pallas_call | solution.py:122
  30.2 0.0 copy-start.3
  30.2 1.9 %collective-permute-start.3 = (bf16[4,256,1024]{2,1,0:T(8,128)(2,1)S(1)}, bf16[4,256,1024]{2,1,0:T(8,128)(2,1)S(1)}, u32[]{:S(2)}, u32[]{:S(2)}) collective-permute-start(bf16[4,256,1024]{2,1,0:T(8,128)(2,1)S(1)} %near.1.near_ref), channel_id=1, source_target_pairs={{0,32},{32,0},{64,96},{96,64},{128,160},{160,128},{192,224},{224,1... | collective-permute-start | bytes 6291464 | tf_op jit(solution)/shard_map/ppermute | solution.py:241
  32.1 0.0 collective-permute-done.x_ref
  32.1 0.0 copy-start.2
  32.1 0.0 collective-permute-done.1.sibling_ref
  32.1 4.1 %collective-permute-done.3.passed_ref = bf16[4,256,1024]{2,1,0:T(8,128)(2,1)S(1)} collective-permute-done((bf16[4,256,1024]{2,1,0:T(8,128)(2,1)S(1)}, bf16[4,256,1024]{2,1,0:T(8,128)(2,1)S(1)}, u32[]{:S(2)}, u32[]{:S(2)}) %collective-permute-start.3) | collective-permute-done | bytes 2097184 | tf_op jit(solution)/shard_map/ppermute | solution.py:241
  36.2 0.0 copy-done.3
  36.2 0.0 copy-done.2
  36.2 8.2 %far_and_pairs.1 = f32[16,2,48,256]{3,2,1,0:T(8,128)S(1)} custom-call(s32[1]{0:T(128)} %bitcast.owner_ref, s32[2,12]{1,0:T(2,128)S(1)} %bitcast.5, bf16[4,128,1024]{2,1,0:T(8,128)(2,1)} %far_arrived.1.x_ref, bf16[1024,2048]{1,0:T(8,128)(2,1)S(1)} %copy-done.2, bf16[4,256,1024]{2,1,0:T(8,128)(2,1)S(1)} %get-tuple-element.10.own_ref, ...), custom_call_target="tpu_custom_call" | custom-call | flops 1572864 | bytes 65536 | tf_op jit(solution)/shard_map/far_and_pairs/pallas_call | solution.py:187
  44.4 0.2 convert_element_type.15
  44.6 32.5 %all_to_all.5 = f16[32,48,256]{2,1,0:T(8,128)(2,1)S(1)} all-to-all(f16[32,48,256]{2,1,0:T(8,128)(2,1)S(1)} %bitcast.6), channel_id=1, replica_groups=mesh['chan'=16,'tm'=32] {'tm'}, dimensions={0} | all-to-all | bytes 1572864 | tf_op jit(solution)/shard_map/all_to_all | solution.py:246
  77.2 0.1 convert_reduce_fusion
  77.3 0.6 mul.64
  (9 shorter events, 0.1 us)
Async XLA Ops:
  0.0 25.2 %collective-permute-start.2 = (bf16[4,128,1024]{2,1,0:T(8,128)(2,1)}, bf16[4,128,1024]{2,1,0:T(8,128)(2,1)S(1)}, u32[]{:S(2)}, u32[]{:S(2)}) collective-permute-start(bf16[4,128,1024]{2,1,0:T(8,128)(2,1)} %bitcast.7), channel_id=1, source_target_pairs={{64,0},{128,64},{192,128},{256,192},{320,256},{384,320},{448,384},... | collective-permute-start | bytes 3145736 | tf_op jit(solution)/shard_map/ppermute | solution.py:235
  8.4 1.9 %copy-start = (bf16[1024,2048]{1,0:T(8,128)(2,1)}, bf16[1024,2048]{1,0:T(8,128)(2,1)S(1)}, u32[]{:S(2)}) copy-start(bf16[1024,2048]{1,0:T(8,128)(2,1)S(1)} %get-tuple-element.9.table_ref) | copy-start | bytes 12582916
  10.4 21.7 %collective-permute-start = (bf16[4,128,1024]{2,1,0:T(8,128)(2,1)}, bf16[4,128,1024]{2,1,0:T(8,128)(2,1)}, u32[]{:S(2)}, u32[]{:S(2)}) collective-permute-start(bf16[4,128,1024]{2,1,0:T(8,128)(2,1)} %get-tuple-element.8), channel_id=1, source_target_pairs={{448,0},{0,64},{64,128},{128,192},{192,256},{256,320},{320,384},{3... | collective-permute-start | bytes 3145736 | tf_op jit(solution)/shard_map/ppermute | solution.py:238
  16.1 16.0 %collective-permute-start.1 = (bf16[4,256,1024]{2,1,0:T(8,128)(2,1)S(1)}, bf16[4,256,1024]{2,1,0:T(8,128)(2,1)}, u32[]{:S(2)}, u32[]{:S(2)}) collective-permute-start(bf16[4,256,1024]{2,1,0:T(8,128)(2,1)S(1)} %get-tuple-element.10.own_ref), channel_id=1, source_target_pairs={{0,32},{32,0},{64,96},{96,64},{128,160},{160,128},{192,224},{224,1... | collective-permute-start | bytes 6291464 | tf_op jit(solution)/shard_map/ppermute | solution.py:237
  25.2 2.2 %copy-start.1 = (bf16[1024,2048]{1,0:T(8,128)(2,1)S(1)}, bf16[1024,2048]{1,0:T(8,128)(2,1)}, u32[]{:S(2)}) copy-start(bf16[1024,2048]{1,0:T(8,128)(2,1)} %copy-done) | copy-start | bytes 12582916
  30.2 6.1 %copy-start.3 = (s32[12,2]{0,1:T(2,128)S(1)}, s32[12,2]{0,1:T(2,128)}, u32[]{:S(2)}) copy-start(s32[12,2]{0,1:T(2,128)} %param.3) | copy-start | bytes 292
  30.2 6.1 %collective-permute-start.3 = (bf16[4,256,1024]{2,1,0:T(8,128)(2,1)S(1)}, bf16[4,256,1024]{2,1,0:T(8,128)(2,1)S(1)}, u32[]{:S(2)}, u32[]{:S(2)}) collective-permute-start(bf16[4,256,1024]{2,1,0:T(8,128)(2,1)S(1)} %near.1.near_ref), channel_id=1, source_target_pairs={{0,32},{32,0},{64,96},{96,64},{128,160},{160,128},{192,224},{224,1... | collective-permute-start | bytes 6291464 | tf_op jit(solution)/shard_map/ppermute | solution.py:241
  32.1 4.1 %copy-start.2 = (bf16[1024,2048]{1,0:T(8,128)(2,1)S(1)}, bf16[1024,2048]{1,0:T(8,128)(2,1)}, u32[]{:S(2)}) copy-start(bf16[1024,2048]{1,0:T(8,128)(2,1)} %copy-done) | copy-start | bytes 12582916

commit v6 on v5

--- a/solution.py
+++ b/solution.py
@@ -131,7 +131,7 @@
 
 
 def last_kernel(
-    owner_ref, slots_ref, x_ref, table_ref, own_ref, sibling_ref, near_ref, passed_ref, out_ref, window_ref, sems
+    slots_ref, x_ref, table_ref, own_ref, sibling_ref, near_ref, passed_ref, out_ref, window_ref, sems
 ):
     step = pl.program_id(0)
     blocks, channels, samples = x_ref.shape
@@ -151,7 +151,7 @@
 
     @pl.when(step > 0)
     def _():
-        owner = owner_ref[0]
+        owner = lax.axis_index("chan")
 
         def place(block):
             block = jnp.where(block >= 0, block, owner * blocks)
@@ -181,13 +181,13 @@
             out_ref[:, 1, rows] = jnp.where(row < 4, pltpu.roll(first, 4, 1), second)
 
 
-def far_and_pairs(owner, slots, x, table, own, sibling, near, passed):
+def far_and_pairs(slots, x, table, own, sibling, near, passed):
     blocks, channels, samples = x.shape
     slot_count = slots.shape[0]
     return pl.pallas_call(
         last_kernel,
         grid_spec=pltpu.PrefetchScalarGridSpec(
-            num_scalar_prefetch=2,
+            num_scalar_prefetch=1,
             grid=(1 + slot_count // SLOTS_PER_STEP,),
             in_specs=[HERE] * 6,
             out_specs=pl.BlockSpec(
@@ -202,7 +202,7 @@
         compiler_params=pltpu.CompilerParams(vmem_limit_bytes=20 * MIB),
         cost_estimate=hint(slot_count * channels * samples),
         name="far_and_pairs",
-    )(owner, slots.T, *pinned(x, table, own, sibling, near, passed))
+    )(slots.T, *pinned(x, table, own, sibling, near, passed))
 
 
 def after_transfer(x, work):
@@ -225,7 +225,6 @@
     owners = lax.axis_size("chan")
     windows = lax.axis_size("tm")
     slot_count = pair_slots.shape[0]
-    owner = lax.axis_index("chan")
     even = range(0, owners, 2)
     odd = range(1, owners, 2)
     sibling_pairs = [(i, i ^ 1) for i in range(owners)]
@@ -239,7 +238,7 @@
     far = after_transfer(far, 100 * 10**9)
     near = whiten_next(near, table, "near")
     passed = lax.ppermute(near, "chan", sibling_pairs)
-    products = far_and_pairs(owner.reshape(1), pair_slots, far, table, own, sibling, near, passed)
+    products = far_and_pairs(pair_slots, far, table, own, sibling, near, passed)
 
     rows = channels // windows
     products = products.reshape(windows, slot_count * rows, 2 * channels).astype(jnp.float16)

time: 78.2 us -> 76.2 us (0.974)
  local copies, waits for them, and re-layouts: 4.77 us -> 0.64 us
  waiting for transfers between devices: 11.2 us -> 15.3 us
  Pallas kernels: 15.3 us -> 13.5 us
    unnamed x8 -> x2, local copies, waits for them, and re-layouts: 4.14 us -> 0.01 us
    ppermute x1, waiting for transfers between devices: 7.15 us -> 11.2 us  [on_device(): near = lax.ppermute(x, 'chan', near_pairs)]
    pallas_call x1, Pallas kernels: 8.18 us -> 6.28 us  [far_and_pairs(): pl.pallas_call(last_kernel, grid_spec=pltpu.PrefetchScalarGridSpec(num_sc...]
where the time goes in v6:
time: 76.2 us; the launch traced here: 76 us
  blocking collectives  32.6 us (43%)
  waiting for transfers between devices  15.3 us (20%)
  Pallas kernels  13.5 us (18%)
  starting transfers between devices  12.8 us (17%)
  other arithmetic  1.09 us (1%)
    all_to_all x1, blocking collectives, on_device(): arrived = lax.all_to_all(products, 'tm', 0, 0, tiled=True)  32.6 us
    ppermute x1, waiting for transfers between devices, on_device(): near = lax.ppermute(x, 'chan', near_pairs)  11.2 us
    pallas_call x1, Pallas kernels, far_and_pairs(): pl.pallas_call(last_kernel, grid_spec=pltpu.PrefetchScalarGridSpec(num_sc...  6.28 us
    ppermute x1, starting transfers between devices, on_device(): far = lax.ppermute(again, 'chan', far_pairs)  5.71 us
    pallas_call x1, Pallas kernels, whiten_first(): pl.pallas_call(first_kernel, in_specs=[HERE, HERE, pl.BlockSpec(memory_sp...  4.36 us
    ppermute x1, waiting for transfers between devices, on_device(): passed = lax.ppermute(near, 'chan', sibling_pairs)  4.09 us
    ppermute x1, starting transfers between devices, on_device(): near = lax.ppermute(x, 'chan', near_pairs)  3.25 us
    pallas_call x1, Pallas kernels, whiten_next(): pl.pallas_call(whiten_all, in_specs=[HERE] * 2, out_specs=HERE, out_shape...  2.81 us
  transfers between devices with their start and end apart: 4, of which 2 were waited for; matrix products, arithmetic and copies ran while one was open for 1% of the time, Pallas kernels for 9%

profile of v6, /device:TPU:56, one launch (start us, length us, event | category | flops | bytes accessed | tf_op | source)
XLA Modules:
  0.0 76.0 jit_solution(15399337904208285474)
XLA Ops:
  0.0 3.2 %collective-permute-start.2 = (bf16[4,128,1024]{2,1,0:T(8,128)(2,1)}, bf16[4,128,1024]{2,1,0:T(8,128)(2,1)S(1)}, u32[]{:S(2)}, u32[]{:S(2)}) collective-permute-start(bf16[4,128,1024]{2,1,0:T(8,128)(2,1)} %bitcast.6), channel_id=1, source_target_pairs={{64,0},{128,64},{192,128},{256,192},{320,256},{384,320},{448,384},... | collective-permute-start | bytes 3145736 | tf_op jit(solution)/shard_map/ppermute | solution.py:234
  3.3 0.7 fusion.8
  4.1 4.4 %table_and_own.1 = (bf16[1024,2048]{1,0:T(8,128)(2,1)S(1)}, bf16[4,256,1024]{2,1,0:T(8,128)(2,1)S(1)}, bf16[4,128,1024]{2,1,0:T(8,128)(2,1)S(1)}) custom-call(f32[256,128]{1,0:T(8,128)S(1)} %get-tuple-element.12.cos_ref, f32[256,128]{1,0:T(8,128)S(1)} %get-tuple-element.11.sin_ref, bf16[4,128,1024]{2,1,0:T(8,128)(2,1)} %bitcast.7), custom_call_target="tpu_custom_call" | custom-call | flops 524288 | bytes 65536 | tf_op jit(solution)/shard_map/table_and_own/pallas_call | solution.py:104
  8.5 5.7 %collective-permute-start = (bf16[4,128,1024]{2,1,0:T(8,128)(2,1)S(1)}, bf16[4,128,1024]{2,1,0:T(8,128)(2,1)S(1)}, u32[]{:S(2)}, u32[]{:S(2)}) collective-permute-start(bf16[4,128,1024]{2,1,0:T(8,128)(2,1)S(1)} %get-tuple-element.8), channel_id=1, source_target_pairs={{448,0},{0,64},{64,128},{128,192},{192,256},{256,320},{320,384},{3... | collective-permute-start | bytes 3145736 | tf_op jit(solution)/shard_map/ppermute | solution.py:237
  14.2 1.9 %collective-permute-start.1 = (bf16[4,256,1024]{2,1,0:T(8,128)(2,1)S(1)}, bf16[4,256,1024]{2,1,0:T(8,128)(2,1)S(1)}, u32[]{:S(2)}, u32[]{:S(2)}) collective-permute-start(bf16[4,256,1024]{2,1,0:T(8,128)(2,1)S(1)} %get-tuple-element.10.own_ref), channel_id=1, source_target_pairs={{0,32},{32,0},{64,96},{96,64},{128,160},{160,128},{192,224},{224,1... | collective-permute-start | bytes 6291464 | tf_op jit(solution)/shard_map/ppermute | solution.py:236
  16.1 11.2 %collective-permute-done.2.x_ref = bf16[4,128,1024]{2,1,0:T(8,128)(2,1)S(1)} collective-permute-done((bf16[4,128,1024]{2,1,0:T(8,128)(2,1)}, bf16[4,128,1024]{2,1,0:T(8,128)(2,1)S(1)}, u32[]{:S(2)}, u32[]{:S(2)}) %collective-permute-start.2) | collective-permute-done | bytes 1048608 | tf_op jit(solution)/shard_map/ppermute | solution.py:234
  27.3 2.8 %near.1.near_ref = bf16[4,256,1024]{2,1,0:T(8,128)(2,1)S(1)} custom-call(bf16[4,128,1024]{2,1,0:T(8,128)(2,1)S(1)} %collective-permute-done.2.x_ref, bf16[1024,2048]{1,0:T(8,128)(2,1)S(1)} %get-tuple-element.9.table_ref), custom_call_target="tpu_custom_call" | custom-call | flops 524288 | bytes 65536 | tf_op jit(solution)/shard_map/near/pallas_call | solution.py:122
  30.1 0.0 copy-start
  30.2 1.9 %collective-permute-start.3 = (bf16[4,256,1024]{2,1,0:T(8,128)(2,1)S(1)}, bf16[4,256,1024]{2,1,0:T(8,128)(2,1)S(1)}, u32[]{:S(2)}, u32[]{:S(2)}) collective-permute-start(bf16[4,256,1024]{2,1,0:T(8,128)(2,1)S(1)} %near.1.near_ref), channel_id=1, source_target_pairs={{0,32},{32,0},{64,96},{96,64},{128,160},{160,128},{192,224},{224,1... | collective-permute-start | bytes 6291464 | tf_op jit(solution)/shard_map/ppermute | solution.py:240
  32.1 0.0 collective-permute-done.x_ref
  32.1 0.0 collective-permute-done.1.sibling_ref
  32.1 4.1 %collective-permute-done.3.passed_ref = bf16[4,256,1024]{2,1,0:T(8,128)(2,1)S(1)} collective-permute-done((bf16[4,256,1024]{2,1,0:T(8,128)(2,1)S(1)}, bf16[4,256,1024]{2,1,0:T(8,128)(2,1)S(1)}, u32[]{:S(2)}, u32[]{:S(2)}) %collective-permute-start.3) | collective-permute-done | bytes 2097184 | tf_op jit(solution)/shard_map/ppermute | solution.py:240
  36.2 0.0 copy-done
  36.2 6.3 %far_and_pairs.1 = f32[16,2,48,256]{3,2,1,0:T(8,128)S(1)} custom-call(s32[2,12]{1,0:T(2,128)S(1)} %bitcast.4, bf16[4,128,1024]{2,1,0:T(8,128)(2,1)S(1)} %far_arrived.1.x_ref, bf16[1024,2048]{1,0:T(8,128)(2,1)S(1)} %get-tuple-element.9.table_ref, bf16[4,256,1024]{2,1,0:T(8,128)(2,1)S(1)} %get-tuple-element.10.own_ref, ...), custom_call_target="tpu_custom_call" | custom-call | flops 1572864 | bytes 65536 | tf_op jit(solution)/shard_map/far_and_pairs/pallas_call | solution.py:187
  42.5 0.2 convert_element_type.15
  42.7 32.6 %all_to_all.5 = f16[32,48,256]{2,1,0:T(8,128)(2,1)S(1)} all-to-all(f16[32,48,256]{2,1,0:T(8,128)(2,1)S(1)} %bitcast.5), channel_id=1, replica_groups=mesh['chan'=16,'tm'=32] {'tm'}, dimensions={0} | all-to-all | bytes 1572864 | tf_op jit(solution)/shard_map/all_to_all | solution.py:245
  75.2 0.1 convert_reduce_fusion
  75.4 0.6 mul.64
  (9 shorter events, 0.1 us)
Async XLA Ops:
  0.0 27.3 %collective-permute-start.2 = (bf16[4,128,1024]{2,1,0:T(8,128)(2,1)}, bf16[4,128,1024]{2,1,0:T(8,128)(2,1)S(1)}, u32[]{:S(2)}, u32[]{:S(2)}) collective-permute-start(bf16[4,128,1024]{2,1,0:T(8,128)(2,1)} %bitcast.6), channel_id=1, source_target_pairs={{64,0},{128,64},{192,128},{256,192},{320,256},{384,320},{448,384},... | collective-permute-start | bytes 3145736 | tf_op jit(solution)/shard_map/ppermute | solution.py:234
  8.5 23.6 %collective-permute-start = (bf16[4,128,1024]{2,1,0:T(8,128)(2,1)S(1)}, bf16[4,128,1024]{2,1,0:T(8,128)(2,1)S(1)}, u32[]{:S(2)}, u32[]{:S(2)}) collective-permute-start(bf16[4,128,1024]{2,1,0:T(8,128)(2,1)S(1)} %get-tuple-element.8), channel_id=1, source_target_pairs={{448,0},{0,64},{64,128},{128,192},{192,256},{256,320},{320,384},{3... | collective-permute-start | bytes 3145736 | tf_op jit(solution)/shard_map/ppermute | solution.py:237
  14.2 17.9 %collective-permute-start.1 = (bf16[4,256,1024]{2,1,0:T(8,128)(2,1)S(1)}, bf16[4,256,1024]{2,1,0:T(8,128)(2,1)S(1)}, u32[]{:S(2)}, u32[]{:S(2)}) collective-permute-start(bf16[4,256,1024]{2,1,0:T(8,128)(2,1)S(1)} %get-tuple-element.10.own_ref), channel_id=1, source_target_pairs={{0,32},{32,0},{64,96},{96,64},{128,160},{160,128},{192,224},{224,1... | collective-permute-start | bytes 6291464 | tf_op jit(solution)/shard_map/ppermute | solution.py:236
  30.1 6.1 %copy-start = (s32[12,2]{0,1:T(2,128)S(1)}, s32[12,2]{0,1:T(2,128)}, u32[]{:S(2)}) copy-start(s32[12,2]{0,1:T(2,128)} %param.3) | copy-start | bytes 292
  30.2 6.1 %collective-permute-start.3 = (bf16[4,256,1024]{2,1,0:T(8,128)(2,1)S(1)}, bf16[4,256,1024]{2,1,0:T(8,128)(2,1)S(1)}, u32[]{:S(2)}, u32[]{:S(2)}) collective-permute-start(bf16[4,256,1024]{2,1,0:T(8,128)(2,1)S(1)} %near.1.near_ref), channel_id=1, source_target_pairs={{0,32},{32,0},{64,96},{96,64},{128,160},{160,128},{192,224},{224,1... | collective-permute-start | bytes 6291464 | tf_op jit(solution)/shard_map/ppermute | solution.py:240

commit v7 on v6

--- a/solution.py
+++ b/solution.py
@@ -125,7 +125,7 @@
         out_specs=HERE,
         out_shape=pltpu.VMEM((blocks, 2 * channels, samples), jnp.bfloat16),
         compiler_params=pltpu.CompilerParams(vmem_limit_bytes=12 * MIB),
-        cost_estimate=hint(blocks * channels * samples),
+        cost_estimate=hint(17 * 10**9),
         name=name,
     )(*pinned(x, table))
 
@@ -205,18 +205,18 @@
     )(slots.T, *pinned(x, table, own, sibling, near, passed))
 
 
-def after_transfer(x, work):
+def after_transfer(x, work, *others):
     anywhere = pl.BlockSpec(memory_space=pl.ANY)
     return pl.pallas_call(
-        lambda x_ref, out_ref: None,
-        in_specs=[anywhere],
+        lambda x_ref, *refs: None,
+        in_specs=[anywhere] * (1 + len(others)),
         out_specs=anywhere,
         out_shape=jax.ShapeDtypeStruct(x.shape, x.dtype),
         input_output_aliases={0: 0},
         compiler_params=pltpu.CompilerParams(vmem_limit_bytes=MIB),
         cost_estimate=hint(work),
         name="far_arrived",
-    )(x)
+    )(x, *others)
 
 
 def on_device(strain, pair_slots):
@@ -235,7 +235,7 @@
     table, own, again = whiten_first(x, table_parts(samples))
     sibling = lax.ppermute(own, "chan", sibling_pairs)
     far = lax.ppermute(again, "chan", far_pairs)
-    far = after_transfer(far, 100 * 10**9)
+    far = after_transfer(far, 100 * 10**9, sibling)
     near = whiten_next(near, table, "near")
     passed = lax.ppermute(near, "chan", sibling_pairs)
     products = far_and_pairs(pair_slots, far, table, own, sibling, near, passed)

time: 76.2 us -> 72.6 us (0.953)
  waiting for transfers between devices: 15.3 us -> 10.5 us
  blocking collectives: 32.6 us -> 33.4 us
    ppermute x1, waiting for transfers between devices: 11.2 us -> 6.43 us  [on_device(): near = lax.ppermute(x, 'chan', near_pairs)]
    ppermute x1, waiting for transfers between devices: 0.01 us -> 1.11 us  [on_device(): far = lax.ppermute(again, 'chan', far_pairs)]
    ppermute x1, waiting for transfers between devices: 4.09 us -> 3.01 us  [on_device(): passed = lax.ppermute(near, 'chan', sibling_pairs)]
    all_to_all x1, blocking collectives: 32.6 us -> 33.4 us  [on_device(): arrived = lax.all_to_all(products, 'tm', 0, 0, tiled=True)]
  transfers between devices with their start and end apart: 4 -> 4, of which waited for: 2 -> 3; matrix products, arithmetic and copies ran while one was open for 1% -> 1% of each run, Pallas kernels for 9% -> 10%
where the time goes in v7:
time: 72.6 us; the launch traced here: 72.1 us
  blocking collectives  33.4 us (46%)
  Pallas kernels  13.5 us (19%)
  starting transfers between devices  12.8 us (18%)
  waiting for transfers between devices  10.5 us (14%)
  other arithmetic  1.09 us (2%)
    all_to_all x1, blocking collectives, on_device(): arrived = lax.all_to_all(products, 'tm', 0, 0, tiled=True)  33.4 us
    ppermute x1, waiting for transfers between devices, on_device(): near = lax.ppermute(x, 'chan', near_pairs)  6.43 us
    pallas_call x1, Pallas kernels, far_and_pairs(): pl.pallas_call(last_kernel, grid_spec=pltpu.PrefetchScalarGridSpec(num_sc...  6.3 us
    ppermute x1, starting transfers between devices, on_device(): far = lax.ppermute(again, 'chan', far_pairs)  5.71 us
    pallas_call x1, Pallas kernels, whiten_first(): pl.pallas_call(first_kernel, in_specs=[HERE, HERE, pl.BlockSpec(memory_sp...  4.36 us
    ppermute x1, starting transfers between devices, on_device(): near = lax.ppermute(x, 'chan', near_pairs)  3.25 us
    ppermute x1, waiting for transfers between devices, on_device(): passed = lax.ppermute(near, 'chan', sibling_pairs)  3.01 us
    pallas_call x1, Pallas kernels, whiten_next(): pl.pallas_call(whiten_all, in_specs=[HERE] * 2, out_specs=HERE, out_shape...  2.81 us
  transfers between devices with their start and end apart: 4, of which 3 were waited for; matrix products, arithmetic and copies ran while one was open for 1% of the time, Pallas kernels for 10%

profile of v7, /device:TPU:56, one launch (start us, length us, event | category | flops | bytes accessed | tf_op | source)
XLA Modules:
  0.0 72.1 jit_solution(8435876968612543228)
XLA Ops:
  0.0 3.2 %collective-permute-start.2 = (bf16[4,128,1024]{2,1,0:T(8,128)(2,1)}, bf16[4,128,1024]{2,1,0:T(8,128)(2,1)S(1)}, u32[]{:S(2)}, u32[]{:S(2)}) collective-permute-start(bf16[4,128,1024]{2,1,0:T(8,128)(2,1)} %bitcast.6), channel_id=1, source_target_pairs={{64,0},{128,64},{192,128},{256,192},{320,256},{384,320},{448,384},... | collective-permute-start | bytes 3145736 | tf_op jit(solution)/shard_map/ppermute | solution.py:234
  3.3 0.7 %fusion.8 = (f32[256,128]{1,0:T(8,128)S(1)}, f32[256,128]{1,0:T(8,128)S(1)}) fusion(s32[256]{0:T(256)S(1)} %get-tuple-element.20, s32[256]{0:T(256)S(1)} %get-tuple-element.22, pred[256]{0:T(512)(128)(4,1)S(1)} %get-tuple-element.15, s32[256]{0:T(256)S(1)} %get-tuple-element.19, s32[256]{0:T(256)S(1)} %get-tuple-element.23, ...), kind=kLoop, calls=%fused_computation.19 | loop fusion | flops 1015808 | bytes 271872 | tf_op jit(solution)/shard_map/sin | solution.py:39
  4.1 4.4 %table_and_own.1 = (bf16[1024,2048]{1,0:T(8,128)(2,1)S(1)}, bf16[4,256,1024]{2,1,0:T(8,128)(2,1)S(1)}, bf16[4,128,1024]{2,1,0:T(8,128)(2,1)S(1)}) custom-call(f32[256,128]{1,0:T(8,128)S(1)} %get-tuple-element.12.cos_ref, f32[256,128]{1,0:T(8,128)S(1)} %get-tuple-element.11.sin_ref, bf16[4,128,1024]{2,1,0:T(8,128)(2,1)} %bitcast.7), custom_call_target="tpu_custom_call" | custom-call | flops 524288 | bytes 65536 | tf_op jit(solution)/shard_map/table_and_own/pallas_call | solution.py:104
  8.5 1.9 %collective-permute-start.1 = (bf16[4,256,1024]{2,1,0:T(8,128)(2,1)S(1)}, bf16[4,256,1024]{2,1,0:T(8,128)(2,1)S(1)}, u32[]{:S(2)}, u32[]{:S(2)}) collective-permute-start(bf16[4,256,1024]{2,1,0:T(8,128)(2,1)S(1)} %get-tuple-element.9.own_ref), channel_id=1, source_target_pairs={{0,32},{32,0},{64,96},{96,64},{128,160},{160,128},{192,224},{224,1... | collective-permute-start | bytes 6291464 | tf_op jit(solution)/shard_map/ppermute | solution.py:236
  10.4 5.7 %collective-permute-start = (bf16[4,128,1024]{2,1,0:T(8,128)(2,1)S(1)}, bf16[4,128,1024]{2,1,0:T(8,128)(2,1)S(1)}, u32[]{:S(2)}, u32[]{:S(2)}) collective-permute-start(bf16[4,128,1024]{2,1,0:T(8,128)(2,1)S(1)} %get-tuple-element.8), channel_id=1, source_target_pairs={{448,0},{0,64},{64,128},{128,192},{192,256},{256,320},{320,384},{3... | collective-permute-start | bytes 3145736 | tf_op jit(solution)/shard_map/ppermute | solution.py:237
  16.1 6.4 %collective-permute-done.2.x_ref = bf16[4,128,1024]{2,1,0:T(8,128)(2,1)S(1)} collective-permute-done((bf16[4,128,1024]{2,1,0:T(8,128)(2,1)}, bf16[4,128,1024]{2,1,0:T(8,128)(2,1)S(1)}, u32[]{:S(2)}, u32[]{:S(2)}) %collective-permute-start.2) | collective-permute-done | bytes 1048608 | tf_op jit(solution)/shard_map/ppermute | solution.py:234
  22.5 2.8 %near.1.near_ref = bf16[4,256,1024]{2,1,0:T(8,128)(2,1)S(1)} custom-call(bf16[4,128,1024]{2,1,0:T(8,128)(2,1)S(1)} %collective-permute-done.2.x_ref, bf16[1024,2048]{1,0:T(8,128)(2,1)S(1)} %get-tuple-element.10.table_ref), custom_call_target="tpu_custom_call" | custom-call | flops 16999999488 | bytes 65536 | tf_op jit(solution)/shard_map/near/pallas_call | solution.py:122
  25.4 0.0 copy-start
  25.4 1.9 %collective-permute-start.3 = (bf16[4,256,1024]{2,1,0:T(8,128)(2,1)S(1)}, bf16[4,256,1024]{2,1,0:T(8,128)(2,1)S(1)}, u32[]{:S(2)}, u32[]{:S(2)}) collective-permute-start(bf16[4,256,1024]{2,1,0:T(8,128)(2,1)S(1)} %near.1.near_ref), channel_id=1, source_target_pairs={{0,32},{32,0},{64,96},{96,64},{128,160},{160,128},{192,224},{224,1... | collective-permute-start | bytes 6291464 | tf_op jit(solution)/shard_map/ppermute | solution.py:240
  27.3 1.1 %collective-permute-done.x_ref = bf16[4,128,1024]{2,1,0:T(8,128)(2,1)S(1)} collective-permute-done((bf16[4,128,1024]{2,1,0:T(8,128)(2,1)S(1)}, bf16[4,128,1024]{2,1,0:T(8,128)(2,1)S(1)}, u32[]{:S(2)}, u32[]{:S(2)}) %collective-permute-start) | collective-permute-done | bytes 1048608 | tf_op jit(solution)/shard_map/ppermute | solution.py:237
  28.4 0.0 collective-permute-done.1.refs_0_.sibling_ref
  28.4 3.0 %collective-permute-done.3.passed_ref = bf16[4,256,1024]{2,1,0:T(8,128)(2,1)S(1)} collective-permute-done((bf16[4,256,1024]{2,1,0:T(8,128)(2,1)S(1)}, bf16[4,256,1024]{2,1,0:T(8,128)(2,1)S(1)}, u32[]{:S(2)}, u32[]{:S(2)}) %collective-permute-start.3) | collective-permute-done | bytes 2097184 | tf_op jit(solution)/shard_map/ppermute | solution.py:240
  31.4 0.0 copy-done
  31.4 6.3 %far_and_pairs.1 = f32[16,2,48,256]{3,2,1,0:T(8,128)S(1)} custom-call(s32[2,12]{1,0:T(2,128)S(1)} %bitcast.4, bf16[4,128,1024]{2,1,0:T(8,128)(2,1)S(1)} %far_arrived.1.x_ref, bf16[1024,2048]{1,0:T(8,128)(2,1)S(1)} %get-tuple-element.10.table_ref, bf16[4,256,1024]{2,1,0:T(8,128)(2,1)S(1)} %get-tuple-element.9.own_ref, ...), custom_call_target="tpu_custom_call" | custom-call | flops 1572864 | bytes 65536 | tf_op jit(solution)/shard_map/far_and_pairs/pallas_call | solution.py:187
  37.7 0.2 convert_element_type.15
  37.9 33.4 %all_to_all.5 = f16[32,48,256]{2,1,0:T(8,128)(2,1)S(1)} all-to-all(f16[32,48,256]{2,1,0:T(8,128)(2,1)S(1)} %bitcast.5), channel_id=1, replica_groups=mesh['chan'=16,'tm'=32] {'tm'}, dimensions={0} | all-to-all | bytes 1572864 | tf_op jit(solution)/shard_map/all_to_all | solution.py:245
  71.3 0.1 convert_reduce_fusion
  71.4 0.6 mul.64
  (9 shorter events, 0.1 us)
Async XLA Ops:
  0.0 22.5 %collective-permute-start.2 = (bf16[4,128,1024]{2,1,0:T(8,128)(2,1)}, bf16[4,128,1024]{2,1,0:T(8,128)(2,1)S(1)}, u32[]{:S(2)}, u32[]{:S(2)}) collective-permute-start(bf16[4,128,1024]{2,1,0:T(8,128)(2,1)} %bitcast.6), channel_id=1, source_target_pairs={{64,0},{128,64},{192,128},{256,192},{320,256},{384,320},{448,384},... | collective-permute-start | bytes 3145736 | tf_op jit(solution)/shard_map/ppermute | solution.py:234
  8.5 19.9 %collective-permute-start.1 = (bf16[4,256,1024]{2,1,0:T(8,128)(2,1)S(1)}, bf16[4,256,1024]{2,1,0:T(8,128)(2,1)S(1)}, u32[]{:S(2)}, u32[]{:S(2)}) collective-permute-start(bf16[4,256,1024]{2,1,0:T(8,128)(2,1)S(1)} %get-tuple-element.9.own_ref), channel_id=1, source_target_pairs={{0,32},{32,0},{64,96},{96,64},{128,160},{160,128},{192,224},{224,1... | collective-permute-start | bytes 6291464 | tf_op jit(solution)/shard_map/ppermute | solution.py:236
  10.4 18.0 %collective-permute-start = (bf16[4,128,1024]{2,1,0:T(8,128)(2,1)S(1)}, bf16[4,128,1024]{2,1,0:T(8,128)(2,1)S(1)}, u32[]{:S(2)}, u32[]{:S(2)}) collective-permute-start(bf16[4,128,1024]{2,1,0:T(8,128)(2,1)S(1)} %get-tuple-element.8), channel_id=1, source_target_pairs={{448,0},{0,64},{64,128},{128,192},{192,256},{256,320},{320,384},{3... | collective-permute-start | bytes 3145736 | tf_op jit(solution)/shard_map/ppermute | solution.py:237
  25.4 6.1 %copy-start = (s32[12,2]{0,1:T(2,128)S(1)}, s32[12,2]{0,1:T(2,128)}, u32[]{:S(2)}) copy-start(s32[12,2]{0,1:T(2,128)} %param.3) | copy-start | bytes 292
  25.4 6.1 %collective-permute-start.3 = (bf16[4,256,1024]{2,1,0:T(8,128)(2,1)S(1)}, bf16[4,256,1024]{2,1,0:T(8,128)(2,1)S(1)}, u32[]{:S(2)}, u32[]{:S(2)}) collective-permute-start(bf16[4,256,1024]{2,1,0:T(8,128)(2,1)S(1)} %near.1.near_ref), channel_id=1, source_target_pairs={{0,32},{32,0},{64,96},{96,64},{128,160},{160,128},{192,224},{224,1... | collective-permute-start | bytes 6291464 | tf_op jit(solution)/shard_map/ppermute | solution.py:240

commit v8 on v7

--- a/solution.py
+++ b/solution.py
@@ -51,10 +51,15 @@
         out_ref[block, channels:, bins] = (imag * scale).astype(jnp.bfloat16)
 
 
-def first_kernel(cos_ref, sin_ref, x_ref, table_ref, out_ref, again_ref, low_cos_ref, low_sin_ref, sem):
-    samples = x_ref.shape[2]
-    fetch = pltpu.make_async_copy(x_ref, again_ref, sem)
-    fetch.start()
+def first_kernel(cos_ref, sin_ref, x_ref, table_ref, out_ref, low_ref, high_ref, low_cos_ref, low_sin_ref, sems):
+    blocks, _, samples = x_ref.shape
+    half = blocks // 2
+    fetches = [
+        pltpu.make_async_copy(x_ref.at[:half], low_ref, sems.at[0]),
+        pltpu.make_async_copy(x_ref.at[half:], high_ref, sems.at[1]),
+    ]
+    for fetch in fetches:
+        fetch.start()
     rows = lambda ref, part: ref[part * SPLIT : (part + 1) * SPLIT, :]
     for at in range(samples // SPLIT):
         high = lambda ref, part: ref[part * SPLIT + at : part * SPLIT + at + 1, :]
@@ -77,12 +82,13 @@
         table_ref[:, columns] = real.reshape(samples, LANES).astype(jnp.bfloat16)
         columns = slice((2 * step + 1) * LANES, (2 * step + 2) * LANES)
         table_ref[:, columns] = imag.reshape(samples, LANES).astype(jnp.bfloat16)
-    fetch.wait()
-    whiten_all(again_ref, table_ref, out_ref)
-
-
-def whiten_all(x_ref, table_ref, out_ref):
-    x = x_ref[...]
+    for fetch in fetches:
+        fetch.wait()
+    whiten_all((low_ref, high_ref), table_ref, out_ref)
+
+
+def whiten_all(x_refs, table_ref, out_ref):
+    x = jnp.concatenate([x_ref[...] for x_ref in x_refs], axis=0)
     for step in range(x.shape[2] // LANES):
         table = table_ref[:, 2 * step * LANES : 2 * (step + 1) * LANES]
         whiten_bins(x, table, out_ref, slice(step * LANES, (step + 1) * LANES))
@@ -104,13 +110,14 @@
     return pl.pallas_call(
         first_kernel,
         in_specs=[HERE, HERE, pl.BlockSpec(memory_space=pl.ANY)],
-        out_specs=[HERE] * 3,
+        out_specs=[HERE] * 4,
         out_shape=[
             pltpu.VMEM((samples, 2 * samples), jnp.bfloat16),
             pltpu.VMEM((blocks, 2 * channels, samples), jnp.bfloat16),
-            pltpu.VMEM(x.shape, x.dtype),
+            pltpu.VMEM((blocks // 2, channels, samples), x.dtype),
+            pltpu.VMEM((blocks // 2, channels, samples), x.dtype),
         ],
-        scratch_shapes=[pltpu.VMEM((samples, LANES), jnp.float32)] * 2 + [pltpu.SemaphoreType.DMA],
+        scratch_shapes=[pltpu.VMEM((samples, LANES), jnp.float32)] * 2 + [pltpu.SemaphoreType.DMA((2,))],
         compiler_params=pltpu.CompilerParams(vmem_limit_bytes=12 * MIB),
         cost_estimate=hint(blocks * channels * samples),
         name="table_and_own",
@@ -120,7 +127,7 @@
 def whiten_next(x, table, name):
     blocks, channels, samples = x.shape
     return pl.pallas_call(
-        whiten_all,
+        lambda x_ref, table_ref, out_ref: whiten_all((x_ref,), table_ref, out_ref),
         in_specs=[HERE] * 2,
         out_specs=HERE,
         out_shape=pltpu.VMEM((blocks, 2 * channels, samples), jnp.bfloat16),
@@ -131,10 +138,11 @@
 
 
 def last_kernel(
-    slots_ref, x_ref, table_ref, own_ref, sibling_ref, near_ref, passed_ref, out_ref, window_ref, sems
+    slots_ref, low_ref, high_ref, table_ref, own_ref, sibling_ref, near_ref, passed_ref, out_ref, window_ref, sems
 ):
     step = pl.program_id(0)
-    blocks, channels, samples = x_ref.shape
+    blocks, stacked, samples = own_ref.shape
+    channels = stacked // 2
 
     @pl.when(step == 0)
     def _():
@@ -145,7 +153,7 @@
         ]
         for copy in copies:
             copy.start()
-        whiten_all(x_ref, table_ref, window_ref.at[pl.ds(3 * blocks, blocks)])
+        whiten_all((low_ref, high_ref), table_ref, window_ref.at[pl.ds(3 * blocks, blocks)])
         for copy in copies:
             copy.wait()
 
@@ -181,15 +189,16 @@
             out_ref[:, 1, rows] = jnp.where(row < 4, pltpu.roll(first, 4, 1), second)
 
 
-def far_and_pairs(slots, x, table, own, sibling, near, passed):
-    blocks, channels, samples = x.shape
+def far_and_pairs(slots, low, high, table, own, sibling, near, passed):
+    blocks, stacked, samples = own.shape
+    channels = stacked // 2
     slot_count = slots.shape[0]
     return pl.pallas_call(
         last_kernel,
         grid_spec=pltpu.PrefetchScalarGridSpec(
             num_scalar_prefetch=1,
             grid=(1 + slot_count // SLOTS_PER_STEP,),
-            in_specs=[HERE] * 6,
+            in_specs=[HERE] * 7,
             out_specs=pl.BlockSpec(
                 (channels // 8, 2, 4 * SLOTS_PER_STEP, 2 * channels), lambda i, *_: (0, 0, jnp.maximum(i - 1, 0), 0)
             ),
@@ -202,7 +211,7 @@
         compiler_params=pltpu.CompilerParams(vmem_limit_bytes=20 * MIB),
         cost_estimate=hint(slot_count * channels * samples),
         name="far_and_pairs",
-    )(slots.T, *pinned(x, table, own, sibling, near, passed))
+    )(slots.T, *pinned(low, high, table, own, sibling, near, passed))
 
 
 def after_transfer(x, work, *others):
@@ -232,13 +241,13 @@
     far_pairs = [((i - 2) % owners, i) for i in even] + [((i + 2) % owners, i) for i in odd]
 
     near = lax.ppermute(x, "chan", near_pairs)
-    table, own, again = whiten_first(x, table_parts(samples))
+    table, own, low, high = whiten_first(x, table_parts(samples))
     sibling = lax.ppermute(own, "chan", sibling_pairs)
-    far = lax.ppermute(again, "chan", far_pairs)
-    far = after_transfer(far, 100 * 10**9, sibling)
+    low, high = [lax.ppermute(part, "chan", far_pairs) for part in (low, high)]
+    low = after_transfer(low, 100 * 10**9, high, sibling)
     near = whiten_next(near, table, "near")
     passed = lax.ppermute(near, "chan", sibling_pairs)
-    products = far_and_pairs(pair_slots, far, table, own, sibling, near, passed)
+    products = far_and_pairs(pair_slots, low, high, table, own, sibling, near, passed)
 
     rows = channels // windows
     products = products.reshape(windows, slot_count * rows, 2 * channels).astype(jnp.float16)

time: 72.6 us -> 72.6 us (level)
  waiting for transfers between devices: 10.5 us -> 6.59 us
  starting transfers between devices: 12.8 us -> 16.7 us
    ppermute x1, waiting for transfers between devices: 6.43 us -> 2.47 us  [on_device(): near = lax.ppermute(x, 'chan', near_pairs)]
    ppermute x1 -> x2, starting transfers between devices: 5.71 us -> 9.63 us  [on_device(): low, high = [lax.ppermute(part, 'chan', far_pairs) for part in (low, high)]]
  transfers between devices with their start and end apart: 4 -> 5, of which waited for: 3 -> 3; matrix products, arithmetic and copies ran while one was open for 1% -> 1% of each run, Pallas kernels for 10% -> 10%
where the time goes in v8:
time: 72.6 us; the launch traced here: 72.1 us
  blocking collectives  33.4 us (46%)
  starting transfers between devices  16.7 us (23%)
  Pallas kernels  13.5 us (19%)
  waiting for transfers between devices  6.59 us (9%)
  other arithmetic  1.09 us (2%)
    all_to_all x1, blocking collectives, on_device(): arrived = lax.all_to_all(products, 'tm', 0, 0, tiled=True)  33.4 us
    ppermute x2, starting transfers between devices, on_device(): low, high = [lax.ppermute(part, 'chan', far_pairs) for part in (low, high)]  9.63 us
    pallas_call x1, Pallas kernels, far_and_pairs(): pl.pallas_call(last_kernel, grid_spec=pltpu.PrefetchScalarGridSpec(num_sc...  6.29 us
    pallas_call x1, Pallas kernels, whiten_first(): pl.pallas_call(first_kernel, in_specs=[HERE, HERE, pl.BlockSpec(memory_sp...  4.38 us
    ppermute x1, starting transfers between devices, on_device(): near = lax.ppermute(x, 'chan', near_pairs)  3.25 us
    ppermute x1, waiting for transfers between devices, on_device(): passed = lax.ppermute(near, 'chan', sibling_pairs)  2.99 us
    pallas_call x1, Pallas kernels, whiten_next(): pl.pallas_call(lambda x_ref, table_ref, out_ref: whiten_all((x_ref,), tab...  2.81 us
    ppermute x1, waiting for transfers between devices, on_device(): near = lax.ppermute(x, 'chan', near_pairs)  2.47 us
  transfers between devices with their start and end apart: 5, of which 3 were waited for; matrix products, arithmetic and copies ran while one was open for 1% of the time, Pallas kernels for 10%

profile of v8, /device:TPU:56, one launch (start us, length us, event | category | flops | bytes accessed | tf_op | source)
XLA Modules:
  0.0 72.1 jit_solution(11091759586381362915)
XLA Ops:
  0.0 3.2 %collective-permute-start.3 = (bf16[4,128,1024]{2,1,0:T(8,128)(2,1)}, bf16[4,128,1024]{2,1,0:T(8,128)(2,1)S(1)}, u32[]{:S(2)}, u32[]{:S(2)}) collective-permute-start(bf16[4,128,1024]{2,1,0:T(8,128)(2,1)} %bitcast.6), channel_id=1, source_target_pairs={{64,0},{128,64},{192,128},{256,192},{320,256},{384,320},{448,384},... | collective-permute-start | bytes 3145736 | tf_op jit(solution)/shard_map/ppermute | solution.py:243
  3.3 0.7 %fusion.8 = (f32[256,128]{1,0:T(8,128)S(1)}, f32[256,128]{1,0:T(8,128)S(1)}) fusion(s32[256]{0:T(256)S(1)} %get-tuple-element.22, s32[256]{0:T(256)S(1)} %get-tuple-element.24, pred[256]{0:T(512)(128)(4,1)S(1)} %get-tuple-element.17, s32[256]{0:T(256)S(1)} %get-tuple-element.21, s32[256]{0:T(256)S(1)} %get-tuple-element.25, ...), kind=kLoop, calls=%fused_computation.19 | loop fusion | flops 1015808 | bytes 271872 | tf_op jit(solution)/shard_map/sin | solution.py:39
  4.1 4.4 %table_and_own.1 = (bf16[1024,2048]{1,0:T(8,128)(2,1)S(1)}, bf16[4,256,1024]{2,1,0:T(8,128)(2,1)S(1)}, bf16[2,128,1024]{2,1,0:T(8,128)(2,1)S(1)}, bf16[2,128,1024]{2,1,0:T(8,128)(2,1)S(1)}) custom-call(f32[256,128]{1,0:T(8,128)S(1)} %get-tuple-element.14.cos_ref, f32[256,128]{1,0:T(8,128)S(1)} %get-tuple-element.13.sin_ref, bf16[4,128,1024]{2,1,0:T(8,128)(2,1)} %bitcast.7), custom_call_target="tpu_custom_call" | custom-call | flops 524288 | bytes 65536 | tf_op jit(solution)/shard_map/table_and_own/pallas_call | solution.py:110
  8.5 1.9 %collective-permute-start.2 = (bf16[4,256,1024]{2,1,0:T(8,128)(2,1)S(1)}, bf16[4,256,1024]{2,1,0:T(8,128)(2,1)S(1)}, u32[]{:S(2)}, u32[]{:S(2)}) collective-permute-start(bf16[4,256,1024]{2,1,0:T(8,128)(2,1)S(1)} %get-tuple-element.11.own_ref), channel_id=1, source_target_pairs={{0,32},{32,0},{64,96},{96,64},{128,160},{160,128},{192,224},{224,1... | collective-permute-start | bytes 6291464 | tf_op jit(solution)/shard_map/ppermute | solution.py:245
  10.4 5.7 %collective-permute-start = (bf16[2,128,1024]{2,1,0:T(8,128)(2,1)S(1)}, bf16[2,128,1024]{2,1,0:T(8,128)(2,1)S(1)}, u32[]{:S(2)}, u32[]{:S(2)}) collective-permute-start(bf16[2,128,1024]{2,1,0:T(8,128)(2,1)S(1)} %get-tuple-element.9), channel_id=1, source_target_pairs={{448,0},{0,64},{64,128},{128,192},{192,256},{256,320},{320,384},{3... | collective-permute-start | bytes 1572872 | tf_op jit(solution)/shard_map/ppermute | solution.py:246
  16.1 3.9 %collective-permute-start.1 = (bf16[2,128,1024]{2,1,0:T(8,128)(2,1)S(1)}, bf16[2,128,1024]{2,1,0:T(8,128)(2,1)S(1)}, u32[]{:S(2)}, u32[]{:S(2)}) collective-permute-start(bf16[2,128,1024]{2,1,0:T(8,128)(2,1)S(1)} %get-tuple-element.10), channel_id=1, source_target_pairs={{448,0},{0,64},{64,128},{128,192},{192,256},{256,320},{320,384},{3... | collective-permute-start | bytes 1572872 | tf_op jit(solution)/shard_map/ppermute | solution.py:246
  20.0 2.5 %collective-permute-done.3.x_ref = bf16[4,128,1024]{2,1,0:T(8,128)(2,1)S(1)} collective-permute-done((bf16[4,128,1024]{2,1,0:T(8,128)(2,1)}, bf16[4,128,1024]{2,1,0:T(8,128)(2,1)S(1)}, u32[]{:S(2)}, u32[]{:S(2)}) %collective-permute-start.3) | collective-permute-done | bytes 1048608 | tf_op jit(solution)/shard_map/ppermute | solution.py:243
  22.5 2.8 %near.1.near_ref = bf16[4,256,1024]{2,1,0:T(8,128)(2,1)S(1)} custom-call(bf16[4,128,1024]{2,1,0:T(8,128)(2,1)S(1)} %collective-permute-done.3.x_ref, bf16[1024,2048]{1,0:T(8,128)(2,1)S(1)} %get-tuple-element.12.table_ref), custom_call_target="tpu_custom_call" | custom-call | flops 16999999488 | bytes 65536 | tf_op jit(solution)/shard_map/near/pallas_call | solution.py:129
  25.3 0.0 copy-start
  25.4 1.9 %collective-permute-start.4 = (bf16[4,256,1024]{2,1,0:T(8,128)(2,1)S(1)}, bf16[4,256,1024]{2,1,0:T(8,128)(2,1)S(1)}, u32[]{:S(2)}, u32[]{:S(2)}) collective-permute-start(bf16[4,256,1024]{2,1,0:T(8,128)(2,1)S(1)} %near.1.near_ref), channel_id=1, source_target_pairs={{0,32},{32,0},{64,96},{96,64},{128,160},{160,128},{192,224},{224,1... | collective-permute-start | bytes 6291464 | tf_op jit(solution)/shard_map/ppermute | solution.py:249
  27.3 0.0 collective-permute-done.x_ref
  27.3 1.1 %collective-permute-done.1.refs_0_.high_ref = bf16[2,128,1024]{2,1,0:T(8,128)(2,1)S(1)} collective-permute-done((bf16[2,128,1024]{2,1,0:T(8,128)(2,1)S(1)}, bf16[2,128,1024]{2,1,0:T(8,128)(2,1)S(1)}, u32[]{:S(2)}, u32[]{:S(2)}) %collective-permute-start.1) | collective-permute-done | bytes 524320 | tf_op jit(solution)/shard_map/ppermute | solution.py:246
  28.4 0.0 collective-permute-done.2.refs_1_.sibling_ref
  28.4 3.0 %collective-permute-done.4.passed_ref = bf16[4,256,1024]{2,1,0:T(8,128)(2,1)S(1)} collective-permute-done((bf16[4,256,1024]{2,1,0:T(8,128)(2,1)S(1)}, bf16[4,256,1024]{2,1,0:T(8,128)(2,1)S(1)}, u32[]{:S(2)}, u32[]{:S(2)}) %collective-permute-start.4) | collective-permute-done | bytes 2097184 | tf_op jit(solution)/shard_map/ppermute | solution.py:249
  31.4 0.0 copy-done
  31.4 6.3 %far_and_pairs.1 = f32[16,2,48,256]{3,2,1,0:T(8,128)S(1)} custom-call(s32[2,12]{1,0:T(2,128)S(1)} %bitcast.4, bf16[2,128,1024]{2,1,0:T(8,128)(2,1)S(1)} %far_arrived.1.low_ref, bf16[2,128,1024]{2,1,0:T(8,128)(2,1)S(1)} %collective-permute-done.1.refs_0_.high_ref, bf16[1024,2048]{1,0:T(8,128)(2,1)S(1)} %get-tuple-element.12.table_ref, ...), custom_call_target="tpu_custom_call" | custom-call | flops 1572864 | bytes 65536 | tf_op jit(solution)/shard_map/far_and_pairs/pallas_call | solution.py:196
  37.7 0.2 convert_element_type.15
  37.9 33.4 %all_to_all.5 = f16[32,48,256]{2,1,0:T(8,128)(2,1)S(1)} all-to-all(f16[32,48,256]{2,1,0:T(8,128)(2,1)S(1)} %bitcast.5), channel_id=1, replica_groups=mesh['chan'=16,'tm'=32] {'tm'}, dimensions={0} | all-to-all | bytes 1572864 | tf_op jit(solution)/shard_map/all_to_all | solution.py:254
  71.3 0.1 convert_reduce_fusion
  71.4 0.6 mul.64
  (9 shorter events, 0.1 us)
Async XLA Ops:
  0.0 22.5 %collective-permute-start.3 = (bf16[4,128,1024]{2,1,0:T(8,128)(2,1)}, bf16[4,128,1024]{2,1,0:T(8,128)(2,1)S(1)}, u32[]{:S(2)}, u32[]{:S(2)}) collective-permute-start(bf16[4,128,1024]{2,1,0:T(8,128)(2,1)} %bitcast.6), channel_id=1, source_target_pairs={{64,0},{128,64},{192,128},{256,192},{320,256},{384,320},{448,384},... | collective-permute-start | bytes 3145736 | tf_op jit(solution)/shard_map/ppermute | solution.py:243
  8.5 19.9 %collective-permute-start.2 = (bf16[4,256,1024]{2,1,0:T(8,128)(2,1)S(1)}, bf16[4,256,1024]{2,1,0:T(8,128)(2,1)S(1)}, u32[]{:S(2)}, u32[]{:S(2)}) collective-permute-start(bf16[4,256,1024]{2,1,0:T(8,128)(2,1)S(1)} %get-tuple-element.11.own_ref), channel_id=1, source_target_pairs={{0,32},{32,0},{64,96},{96,64},{128,160},{160,128},{192,224},{224,1... | collective-permute-start | bytes 6291464 | tf_op jit(solution)/shard_map/ppermute | solution.py:245
  10.4 16.9 %collective-permute-start = (bf16[2,128,1024]{2,1,0:T(8,128)(2,1)S(1)}, bf16[2,128,1024]{2,1,0:T(8,128)(2,1)S(1)}, u32[]{:S(2)}, u32[]{:S(2)}) collective-permute-start(bf16[2,128,1024]{2,1,0:T(8,128)(2,1)S(1)} %get-tuple-element.9), channel_id=1, source_target_pairs={{448,0},{0,64},{64,128},{128,192},{192,256},{256,320},{320,384},{3... | collective-permute-start | bytes 1572872 | tf_op jit(solution)/shard_map/ppermute | solution.py:246
  16.1 12.3 %collective-permute-start.1 = (bf16[2,128,1024]{2,1,0:T(8,128)(2,1)S(1)}, bf16[2,128,1024]{2,1,0:T(8,128)(2,1)S(1)}, u32[]{:S(2)}, u32[]{:S(2)}) collective-permute-start(bf16[2,128,1024]{2,1,0:T(8,128)(2,1)S(1)} %get-tuple-element.10), channel_id=1, source_target_pairs={{448,0},{0,64},{64,128},{128,192},{192,256},{256,320},{320,384},{3... | collective-permute-start | bytes 1572872 | tf_op jit(solution)/shard_map/ppermute | solution.py:246
  25.3 6.1 %copy-start = (s32[12,2]{0,1:T(2,128)S(1)}, s32[12,2]{0,1:T(2,128)}, u32[]{:S(2)}) copy-start(s32[12,2]{0,1:T(2,128)} %param.3) | copy-start | bytes 292
  25.4 6.1 %collective-permute-start.4 = (bf16[4,256,1024]{2,1,0:T(8,128)(2,1)S(1)}, bf16[4,256,1024]{2,1,0:T(8,128)(2,1)S(1)}, u32[]{:S(2)}, u32[]{:S(2)}) collective-permute-start(bf16[4,256,1024]{2,1,0:T(8,128)(2,1)S(1)} %near.1.near_ref), channel_id=1, source_target_pairs={{0,32},{32,0},{64,96},{96,64},{128,160},{160,128},{192,224},{224,1... | collective-permute-start | bytes 6291464 | tf_op jit(solution)/shard_map/ppermute | solution.py:249

commit v9 on v7

--- a/solution.py
+++ b/solution.py
@@ -1,3 +1,4 @@
+import functools
 import math
 
 import jax
@@ -12,6 +13,7 @@
 SPLIT = 32
 GROUPS = 5
 SLOTS_PER_STEP = 6
+SLOTS_PER_GROUP = 2
 MIB = 1024 * 1024
 
 
@@ -131,7 +133,7 @@
 
 
 def last_kernel(
-    slots_ref, x_ref, table_ref, own_ref, sibling_ref, near_ref, passed_ref, out_ref, window_ref, sems
+    slots_ref, x_ref, table_ref, own_ref, sibling_ref, near_ref, passed_ref, out_ref, group_ref, window_ref, sems
 ):
     step = pl.program_id(0)
     blocks, channels, samples = x_ref.shape
@@ -149,7 +151,11 @@
         for copy in copies:
             copy.wait()
 
-    @pl.when(step > 0)
+    group_ref[0] = sum(
+        (slots_ref[0, slot] >= 0).astype(jnp.int32) for slot in range(SLOTS_PER_GROUP, slots_ref.shape[1], SLOTS_PER_GROUP)
+    )
+
+    @pl.when((step > 0) & (slots_ref[0, jnp.maximum(step - 1, 0) * SLOTS_PER_STEP] >= 0))
     def _():
         owner = lax.axis_index("chan")
 
@@ -190,15 +196,22 @@
             num_scalar_prefetch=1,
             grid=(1 + slot_count // SLOTS_PER_STEP,),
             in_specs=[HERE] * 6,
-            out_specs=pl.BlockSpec(
-                (channels // 8, 2, 4 * SLOTS_PER_STEP, 2 * channels), lambda i, *_: (0, 0, jnp.maximum(i - 1, 0), 0)
-            ),
+            out_specs=[
+                pl.BlockSpec(
+                    (channels // 8, 2, 4 * SLOTS_PER_STEP, 2 * channels),
+                    lambda i, *_: (0, 0, jnp.maximum(i - 1, 0), 0),
+                ),
+                pl.BlockSpec(memory_space=pltpu.SMEM),
+            ],
             scratch_shapes=[
                 pltpu.VMEM((GROUPS * blocks, 2 * channels, samples), jnp.bfloat16),
                 pltpu.SemaphoreType.DMA((4,)),
             ],
         ),
-        out_shape=pltpu.VMEM((channels // 8, 2, slot_count * 4, 2 * channels), jnp.float32),
+        out_shape=[
+            jax.ShapeDtypeStruct((channels // 8, 2, slot_count * 4, 2 * channels), jnp.float32),
+            jax.ShapeDtypeStruct((1,), jnp.int32),
+        ],
         compiler_params=pltpu.CompilerParams(vmem_limit_bytes=20 * MIB),
         cost_estimate=hint(slot_count * channels * samples),
         name="far_and_pairs",
@@ -238,12 +251,22 @@
     far = after_transfer(far, 100 * 10**9, sibling)
     near = whiten_next(near, table, "near")
     passed = lax.ppermute(near, "chan", sibling_pairs)
-    products = far_and_pairs(pair_slots, far, table, own, sibling, near, passed)
+    products, group = far_and_pairs(pair_slots, far, table, own, sibling, near, passed)
 
     rows = channels // windows
-    products = products.reshape(windows, slot_count * rows, 2 * channels).astype(jnp.float16)
-    arrived = lax.all_to_all(products, "tm", 0, 0, tiled=True)
-    total = jnp.sum(arrived.astype(jnp.float32), axis=0) * (4.0 / (samples * windows))
+    products = products.reshape(windows, slot_count * rows, 2 * channels)
+
+    def summed(slots, products):
+        sent = products[:, : slots * rows].astype(jnp.float16)
+        arrived = lax.all_to_all(sent, "tm", 0, 0, tiled=True)
+        total = jnp.sum(arrived.astype(jnp.float32), axis=0) * (4.0 / (samples * windows))
+        return jnp.pad(total, ((0, (slot_count - slots) * rows), (0, 0)))
+
+    total = lax.switch(
+        group[0],
+        [functools.partial(summed, slots) for slots in range(SLOTS_PER_GROUP, slot_count + 1, SLOTS_PER_GROUP)],
+        products,
+    )
     return jnp.transpose(total.reshape(slot_count, rows, 2 * channels), (1, 0, 2))
 
 

time: 72.6 us -> 71.4 us (0.983)
  the two profiles are of different devices: /device:TPU:56 before, /device:TPU:25 now
where the time goes in v9:
time: 71.4 us; the launch traced here: 71.1 us
  blocking collectives  33.3 us (47%)
  Pallas kernels  14 us (20%)
  starting transfers between devices  12.7 us (18%)
  waiting for transfers between devices  8.57 us (12%)
  other arithmetic  1.06 us (1%)
  between operations  0.77 us (1%)
    all_to_all x1, blocking collectives, summed(): arrived = lax.all_to_all(sent, 'tm', 0, 0, tiled=True)  33.3 us
    pallas_call x1, Pallas kernels, far_and_pairs(): pl.pallas_call(last_kernel, grid_spec=pltpu.PrefetchScalarGridSpec(num_sc...  6.87 us
    ppermute x1, waiting for transfers between devices, on_device(): far = lax.ppermute(again, 'chan', far_pairs)  4.85 us
    ppermute x1, starting transfers between devices, on_device(): passed = lax.ppermute(near, 'chan', sibling_pairs)  4.45 us
    ppermute x1, starting transfers between devices, on_device(): near = lax.ppermute(x, 'chan', near_pairs)  4.41 us
    pallas_call x1, Pallas kernels, whiten_first(): pl.pallas_call(first_kernel, in_specs=[HERE, HERE, pl.BlockSpec(memory_sp...  4.37 us
    ppermute x1, waiting for transfers between devices, on_device(): near = lax.ppermute(x, 'chan', near_pairs)  3.71 us
    pallas_call x1, Pallas kernels, whiten_next(): pl.pallas_call(whiten_all, in_specs=[HERE] * 2, out_specs=HERE, out_shape...  2.8 us
  transfers between devices with their start and end apart: 4, of which 2 were waited for; matrix products, arithmetic and copies ran while one was open for 1% of the time, Pallas kernels for 10%

profile of v9, /device:TPU:25, one launch (start us, length us, event | category | flops | bytes accessed | tf_op | source)
XLA Modules:
  0.0 71.1 jit_solution(17865856494105923968)
XLA Ops:
  0.0 4.4 %collective-permute-start.2 = (bf16[4,128,1024]{2,1,0:T(8,128)(2,1)}, bf16[4,128,1024]{2,1,0:T(8,128)(2,1)S(1)}, u32[]{:S(2)}, u32[]{:S(2)}) collective-permute-start(bf16[4,128,1024]{2,1,0:T(8,128)(2,1)} %bitcast.12), channel_id=1, source_target_pairs={{64,0},{128,64},{192,128},{256,192},{320,256},{384,320},{448,384},... | collective-permute-start | bytes 3145736 | tf_op jit(solution)/shard_map/ppermute | solution.py:247
  4.5 0.7 %fusion.8 = (f32[256,128]{1,0:T(8,128)S(1)}, f32[256,128]{1,0:T(8,128)S(1)}) fusion(s32[256]{0:T(256)S(1)} %get-tuple-element.37, s32[256]{0:T(256)S(1)} %get-tuple-element.39, pred[256]{0:T(512)(128)(4,1)S(1)} %get-tuple-element.32, s32[256]{0:T(256)S(1)} %get-tuple-element.36, s32[256]{0:T(256)S(1)} %get-tuple-element.40, ...), kind=kLoop, calls=%fused_computation.35 | loop fusion | flops 1015808 | bytes 271872 | tf_op jit(solution)/shard_map/sin | solution.py:41
  5.2 4.4 %table_and_own.1 = (bf16[1024,2048]{1,0:T(8,128)(2,1)S(1)}, bf16[4,256,1024]{2,1,0:T(8,128)(2,1)S(1)}, bf16[4,128,1024]{2,1,0:T(8,128)(2,1)S(1)}) custom-call(f32[256,128]{1,0:T(8,128)S(1)} %get-tuple-element.29.cos_ref, f32[256,128]{1,0:T(8,128)S(1)} %get-tuple-element.28.sin_ref, bf16[4,128,1024]{2,1,0:T(8,128)(2,1)} %bitcast.13), custom_call_target="tpu_custom_call" | custom-call | flops 524288 | bytes 65536 | tf_op jit(solution)/shard_map/table_and_own/pallas_call | solution.py:106
  9.6 1.9 %collective-permute-start.1 = (bf16[4,256,1024]{2,1,0:T(8,128)(2,1)S(1)}, bf16[4,256,1024]{2,1,0:T(8,128)(2,1)S(1)}, u32[]{:S(2)}, u32[]{:S(2)}) collective-permute-start(bf16[4,256,1024]{2,1,0:T(8,128)(2,1)S(1)} %get-tuple-element.24.own_ref), channel_id=1, source_target_pairs={{0,32},{32,0},{64,96},{96,64},{128,160},{160,128},{192,224},{224,1... | collective-permute-start | bytes 6291464 | tf_op jit(solution)/shard_map/ppermute | solution.py:249
  11.5 1.9 %collective-permute-start = (bf16[4,128,1024]{2,1,0:T(8,128)(2,1)S(1)}, bf16[4,128,1024]{2,1,0:T(8,128)(2,1)S(1)}, u32[]{:S(2)}, u32[]{:S(2)}) collective-permute-start(bf16[4,128,1024]{2,1,0:T(8,128)(2,1)S(1)} %get-tuple-element.23), channel_id=1, source_target_pairs={{448,0},{0,64},{64,128},{128,192},{192,256},{256,320},{320,384},{3... | collective-permute-start | bytes 3145736 | tf_op jit(solution)/shard_map/ppermute | solution.py:250
  13.5 3.7 %collective-permute-done.2.x_ref = bf16[4,128,1024]{2,1,0:T(8,128)(2,1)S(1)} collective-permute-done((bf16[4,128,1024]{2,1,0:T(8,128)(2,1)}, bf16[4,128,1024]{2,1,0:T(8,128)(2,1)S(1)}, u32[]{:S(2)}, u32[]{:S(2)}) %collective-permute-start.2) | collective-permute-done | bytes 1048608 | tf_op jit(solution)/shard_map/ppermute | solution.py:247
  17.2 2.8 %near.1.near_ref = bf16[4,256,1024]{2,1,0:T(8,128)(2,1)S(1)} custom-call(bf16[4,128,1024]{2,1,0:T(8,128)(2,1)S(1)} %collective-permute-done.2.x_ref, bf16[1024,2048]{1,0:T(8,128)(2,1)S(1)} %get-tuple-element.25.table_ref), custom_call_target="tpu_custom_call" | custom-call | flops 16999999488 | bytes 65536 | tf_op jit(solution)/shard_map/near/pallas_call | solution.py:124
  20.0 0.0 copy-start
  20.0 4.5 %collective-permute-start.3 = (bf16[4,256,1024]{2,1,0:T(8,128)(2,1)S(1)}, bf16[4,256,1024]{2,1,0:T(8,128)(2,1)S(1)}, u32[]{:S(2)}, u32[]{:S(2)}) collective-permute-start(bf16[4,256,1024]{2,1,0:T(8,128)(2,1)S(1)} %near.1.near_ref), channel_id=1, source_target_pairs={{0,32},{32,0},{64,96},{96,64},{128,160},{160,128},{192,224},{224,1... | collective-permute-start | bytes 6291464 | tf_op jit(solution)/shard_map/ppermute | solution.py:253
  24.5 4.8 %collective-permute-done.x_ref = bf16[4,128,1024]{2,1,0:T(8,128)(2,1)S(1)} collective-permute-done((bf16[4,128,1024]{2,1,0:T(8,128)(2,1)S(1)}, bf16[4,128,1024]{2,1,0:T(8,128)(2,1)S(1)}, u32[]{:S(2)}, u32[]{:S(2)}) %collective-permute-start) | collective-permute-done | bytes 1048608 | tf_op jit(solution)/shard_map/ppermute | solution.py:250
  29.3 0.0 collective-permute-done.1.refs_0_.sibling_ref
  29.3 0.0 collective-permute-done.3.passed_ref
  29.3 0.0 copy-done
  29.3 6.9 %far_and_pairs.1 = (f32[16,2,48,256]{3,2,1,0:T(8,128)S(1)}, s32[1]{0:T(128)}) custom-call(s32[2,12]{1,0:T(2,128)S(1)} %bitcast.5, bf16[4,128,1024]{2,1,0:T(8,128)(2,1)S(1)} %far_arrived.1.x_ref, bf16[1024,2048]{1,0:T(8,128)(2,1)S(1)} %get-tuple-element.25.table_ref, bf16[4,256,1024]{2,1,0:T(8,128)(2,1)S(1)} %get-tuple-element.24.own_ref, ...), custom_call_target="tpu_custom_call" | custom-call | flops 1572864 | bytes 65536 | tf_op jit(solution)/shard_map/far_and_pairs/pallas_call | solution.py:193
  36.9 33.6 %conditional.1 = (f32[48,256]{1,0:T(8,128)S(1)}) conditional(s32[]{:T(128)} %bitcast.2, f32[32,48,256]{2,1,0:T(8,128)S(1)} %bitcast.6, f32[32,48,256]{2,1,0:T(8,128)S(1)} %bitcast.7, f32[32,48,256]{2,1,0:T(8,128)S(1)} %bitcast.8, f32[32,48,256]{2,1,0:T(8,128)S(1)} %bitcast.9, ...), branch_computations={%region_0.2_spmd, %region_2.4_spmd, %region_4.6_spmd, %region_6.8_... | conditional | flops 1179648 | bytes 4866056 | solution.py:265
  36.9 0.1 convert_element_type.37
  37.1 33.3 %all_to_all.29 = f16[32,48,256]{2,1,0:T(8,128)(2,1)S(1)} all-to-all(f16[32,48,256]{2,1,0:T(8,128)(2,1)S(1)} %convert_element_type.37), channel_id=1, replica_groups=mesh['chan'=16,'tm'=32] {'tm'}, dimensions={0} | all-to-all | bytes 1572864 | tf_op jit(solution)/shard_map/cond/branch_5_fun/all_to_all | solution.py:261
  70.4 0.1 convert_reduce_fusion.5
  70.5 0.6 reshape.28
  (9 shorter events, 0.1 us)
Async XLA Ops:
  0.0 17.2 %collective-permute-start.2 = (bf16[4,128,1024]{2,1,0:T(8,128)(2,1)}, bf16[4,128,1024]{2,1,0:T(8,128)(2,1)S(1)}, u32[]{:S(2)}, u32[]{:S(2)}) collective-permute-start(bf16[4,128,1024]{2,1,0:T(8,128)(2,1)} %bitcast.12), channel_id=1, source_target_pairs={{64,0},{128,64},{192,128},{256,192},{320,256},{384,320},{448,384},... | collective-permute-start | bytes 3145736 | tf_op jit(solution)/shard_map/ppermute | solution.py:247
  9.6 19.7 %collective-permute-start.1 = (bf16[4,256,1024]{2,1,0:T(8,128)(2,1)S(1)}, bf16[4,256,1024]{2,1,0:T(8,128)(2,1)S(1)}, u32[]{:S(2)}, u32[]{:S(2)}) collective-permute-start(bf16[4,256,1024]{2,1,0:T(8,128)(2,1)S(1)} %get-tuple-element.24.own_ref), channel_id=1, source_target_pairs={{0,32},{32,0},{64,96},{96,64},{128,160},{160,128},{192,224},{224,1... | collective-permute-start | bytes 6291464 | tf_op jit(solution)/shard_map/ppermute | solution.py:249
  11.5 17.8 %collective-permute-start = (bf16[4,128,1024]{2,1,0:T(8,128)(2,1)S(1)}, bf16[4,128,1024]{2,1,0:T(8,128)(2,1)S(1)}, u32[]{:S(2)}, u32[]{:S(2)}) collective-permute-start(bf16[4,128,1024]{2,1,0:T(8,128)(2,1)S(1)} %get-tuple-element.23), channel_id=1, source_target_pairs={{448,0},{0,64},{64,128},{128,192},{192,256},{256,320},{320,384},{3... | collective-permute-start | bytes 3145736 | tf_op jit(solution)/shard_map/ppermute | solution.py:250
  20.0 9.3 %copy-start = (s32[12,2]{0,1:T(2,128)S(1)}, s32[12,2]{0,1:T(2,128)}, u32[]{:S(2)}) copy-start(s32[12,2]{0,1:T(2,128)} %param.9) | copy-start | bytes 292
  20.0 9.3 %collective-permute-start.3 = (bf16[4,256,1024]{2,1,0:T(8,128)(2,1)S(1)}, bf16[4,256,1024]{2,1,0:T(8,128)(2,1)S(1)}, u32[]{:S(2)}, u32[]{:S(2)}) collective-permute-start(bf16[4,256,1024]{2,1,0:T(8,128)(2,1)S(1)} %near.1.near_ref), channel_id=1, source_target_pairs={{0,32},{32,0},{64,96},{96,64},{128,160},{160,128},{192,224},{224,1... | collective-permute-start | bytes 6291464 | tf_op jit(solution)/shard_map/ppermute | solution.py:253

commit v10 on v9

--- a/solution.py
+++ b/solution.py
@@ -241,8 +241,9 @@
     even = range(0, owners, 2)
     odd = range(1, owners, 2)
     sibling_pairs = [(i, i ^ 1) for i in range(owners)]
-    near_pairs = [((i + 2) % owners, i) for i in even] + [((i - 2) % owners, i) for i in odd]
-    far_pairs = [((i - 2) % owners, i) for i in even] + [((i + 2) % owners, i) for i in odd]
+    inside = lambda pairs: [(source, target) for source, target in pairs if 0 <= source < owners]
+    near_pairs = inside([(i + 2, i) for i in even] + [(i - 2, i) for i in odd])
+    far_pairs = inside([(i - 2, i) for i in even] + [(i + 2, i) for i in odd])
 
     near = lax.ppermute(x, "chan", near_pairs)
     table, own, again = whiten_first(x, table_parts(samples))

time: 71.4 us -> 66.9 us (0.937)
  the two profiles are of different devices: /device:TPU:25 before, /device:TPU:41 now
where the time goes in v10:
time: 66.9 us; the launch traced here: 66.6 us
  blocking collectives  30.1 us (45%)
  Pallas kernels  14 us (21%)
  starting transfers between devices  12.8 us (19%)
  waiting for transfers between devices  7.26 us (11%)
  other arithmetic  1.02 us (2%)
  between operations  0.77 us (1%)
    all_to_all x1, blocking collectives, summed(): arrived = lax.all_to_all(sent, 'tm', 0, 0, tiled=True)  30.1 us
    pallas_call x1, Pallas kernels, far_and_pairs(): pl.pallas_call(last_kernel, grid_spec=pltpu.PrefetchScalarGridSpec(num_sc...  6.87 us
    ppermute x1, starting transfers between devices, on_device(): passed = lax.ppermute(near, 'chan', sibling_pairs)  4.89 us
    pallas_call x1, Pallas kernels, whiten_first(): pl.pallas_call(first_kernel, in_specs=[HERE, HERE, pl.BlockSpec(memory_sp...  4.37 us
    ppermute x1, waiting for transfers between devices, on_device(): far = lax.ppermute(again, 'chan', far_pairs)  4.36 us
    ppermute x1, starting transfers between devices, on_device(): sibling = lax.ppermute(own, 'chan', sibling_pairs)  3.53 us
    ppermute x1, waiting for transfers between devices, on_device(): near = lax.ppermute(x, 'chan', near_pairs)  2.9 us
    pallas_call x1, Pallas kernels, whiten_next(): pl.pallas_call(whiten_all, in_specs=[HERE] * 2, out_specs=HERE, out_shape...  2.8 us
  transfers between devices with their start and end apart: 4, of which 2 were waited for; matrix products, arithmetic and copies ran while one was open for 1% of the time, Pallas kernels for 11%

profile of v10, /device:TPU:41, one launch (start us, length us, event | category | flops | bytes accessed | tf_op | source)
XLA Modules:
  0.0 66.6 jit_solution(14258022339744292080)
XLA Ops:
  0.0 2.3 %collective-permute-start.2 = (bf16[4,128,1024]{2,1,0:T(8,128)(2,1)}, bf16[4,128,1024]{2,1,0:T(8,128)(2,1)S(1)}, u32[]{:S(2)}, u32[]{:S(2)}) collective-permute-start(bf16[4,128,1024]{2,1,0:T(8,128)(2,1)} %bitcast.12), channel_id=1, source_target_pairs={{64,0},{128,64},{192,128},{256,192},{320,256},{384,320},{448,384},... | collective-permute-start | bytes 3145736 | tf_op jit(solution)/shard_map/ppermute | solution.py:248
  2.4 0.7 %fusion.8 = (f32[256,128]{1,0:T(8,128)S(1)}, f32[256,128]{1,0:T(8,128)S(1)}) fusion(s32[256]{0:T(256)S(1)} %get-tuple-element.37, s32[256]{0:T(256)S(1)} %get-tuple-element.39, pred[256]{0:T(512)(128)(4,1)S(1)} %get-tuple-element.32, s32[256]{0:T(256)S(1)} %get-tuple-element.36, s32[256]{0:T(256)S(1)} %get-tuple-element.40, ...), kind=kLoop, calls=%fused_computation.35 | loop fusion | flops 1015808 | bytes 271872 | tf_op jit(solution)/shard_map/sin | solution.py:41
  3.1 4.4 %table_and_own.1 = (bf16[1024,2048]{1,0:T(8,128)(2,1)S(1)}, bf16[4,256,1024]{2,1,0:T(8,128)(2,1)S(1)}, bf16[4,128,1024]{2,1,0:T(8,128)(2,1)S(1)}) custom-call(f32[256,128]{1,0:T(8,128)S(1)} %get-tuple-element.29.cos_ref, f32[256,128]{1,0:T(8,128)S(1)} %get-tuple-element.28.sin_ref, bf16[4,128,1024]{2,1,0:T(8,128)(2,1)} %bitcast.13), custom_call_target="tpu_custom_call" | custom-call | flops 524288 | bytes 65536 | tf_op jit(solution)/shard_map/table_and_own/pallas_call | solution.py:106
  7.5 3.5 %collective-permute-start.1 = (bf16[4,256,1024]{2,1,0:T(8,128)(2,1)S(1)}, bf16[4,256,1024]{2,1,0:T(8,128)(2,1)S(1)}, u32[]{:S(2)}, u32[]{:S(2)}) collective-permute-start(bf16[4,256,1024]{2,1,0:T(8,128)(2,1)S(1)} %get-tuple-element.24.own_ref), channel_id=1, source_target_pairs={{0,32},{32,0},{64,96},{96,64},{128,160},{160,128},{192,224},{224,1... | collective-permute-start | bytes 6291464 | tf_op jit(solution)/shard_map/ppermute | solution.py:250
  11.1 2.1 %collective-permute-start = (bf16[4,128,1024]{2,1,0:T(8,128)(2,1)S(1)}, bf16[4,128,1024]{2,1,0:T(8,128)(2,1)S(1)}, u32[]{:S(2)}, u32[]{:S(2)}) collective-permute-start(bf16[4,128,1024]{2,1,0:T(8,128)(2,1)S(1)} %get-tuple-element.23), channel_id=1, source_target_pairs={{0,64},{64,128},{128,192},{192,256},{256,320},{320,384},{384,448},... | collective-permute-start | bytes 3145736 | tf_op jit(solution)/shard_map/ppermute | solution.py:251
  13.1 2.9 %collective-permute-done.2.x_ref = bf16[4,128,1024]{2,1,0:T(8,128)(2,1)S(1)} collective-permute-done((bf16[4,128,1024]{2,1,0:T(8,128)(2,1)}, bf16[4,128,1024]{2,1,0:T(8,128)(2,1)S(1)}, u32[]{:S(2)}, u32[]{:S(2)}) %collective-permute-start.2) | collective-permute-done | bytes 1048608 | tf_op jit(solution)/shard_map/ppermute | solution.py:248
  16.0 2.8 %near.1.near_ref = bf16[4,256,1024]{2,1,0:T(8,128)(2,1)S(1)} custom-call(bf16[4,128,1024]{2,1,0:T(8,128)(2,1)S(1)} %collective-permute-done.2.x_ref, bf16[1024,2048]{1,0:T(8,128)(2,1)S(1)} %get-tuple-element.25.table_ref), custom_call_target="tpu_custom_call" | custom-call | flops 16999999488 | bytes 65536 | tf_op jit(solution)/shard_map/near/pallas_call | solution.py:124
  18.9 0.0 copy-start
  18.9 4.9 %collective-permute-start.3 = (bf16[4,256,1024]{2,1,0:T(8,128)(2,1)S(1)}, bf16[4,256,1024]{2,1,0:T(8,128)(2,1)S(1)}, u32[]{:S(2)}, u32[]{:S(2)}) collective-permute-start(bf16[4,256,1024]{2,1,0:T(8,128)(2,1)S(1)} %near.1.near_ref), channel_id=1, source_target_pairs={{0,32},{32,0},{64,96},{96,64},{128,160},{160,128},{192,224},{224,1... | collective-permute-start | bytes 6291464 | tf_op jit(solution)/shard_map/ppermute | solution.py:254
  23.8 4.4 %collective-permute-done.x_ref = bf16[4,128,1024]{2,1,0:T(8,128)(2,1)S(1)} collective-permute-done((bf16[4,128,1024]{2,1,0:T(8,128)(2,1)S(1)}, bf16[4,128,1024]{2,1,0:T(8,128)(2,1)S(1)}, u32[]{:S(2)}, u32[]{:S(2)}) %collective-permute-start) | collective-permute-done | bytes 1048608 | tf_op jit(solution)/shard_map/ppermute | solution.py:251
  28.1 0.0 collective-permute-done.1.refs_0_.sibling_ref
  28.1 0.0 collective-permute-done.3.passed_ref
  28.1 0.0 copy-done
  28.1 6.9 %far_and_pairs.1 = (f32[16,2,48,256]{3,2,1,0:T(8,128)S(1)}, s32[1]{0:T(128)}) custom-call(s32[2,12]{1,0:T(2,128)S(1)} %bitcast.5, bf16[4,128,1024]{2,1,0:T(8,128)(2,1)S(1)} %far_arrived.1.x_ref, bf16[1024,2048]{1,0:T(8,128)(2,1)S(1)} %get-tuple-element.25.table_ref, bf16[4,256,1024]{2,1,0:T(8,128)(2,1)S(1)} %get-tuple-element.24.own_ref, ...), custom_call_target="tpu_custom_call" | custom-call | flops 1572864 | bytes 65536 | tf_op jit(solution)/shard_map/far_and_pairs/pallas_call | solution.py:193
  35.7 30.4 %conditional.1 = (f32[48,256]{1,0:T(8,128)S(1)}) conditional(s32[]{:T(128)} %bitcast.2, f32[32,48,256]{2,1,0:T(8,128)S(1)} %bitcast.6, f32[32,48,256]{2,1,0:T(8,128)S(1)} %bitcast.7, f32[32,48,256]{2,1,0:T(8,128)S(1)} %bitcast.8, f32[32,48,256]{2,1,0:T(8,128)S(1)} %bitcast.9, ...), branch_computations={%region_0.2_spmd, %region_2.4_spmd, %region_4.6_spmd, %region_6.8_... | conditional | flops 1179648 | bytes 4866056 | solution.py:266
  35.7 0.1 slice_convert_fusion.4
  35.8 30.1 %all_to_all.28 = f16[32,40,256]{2,1,0:T(8,128)(2,1)S(1)} all-to-all(f16[32,40,256]{2,1,0:T(8,128)(2,1)S(1)} %slice_convert_fusion.4), channel_id=1, replica_groups=mesh['chan'=16,'tm'=32] {'tm'}, dimensions={0} | all-to-all | bytes 1310720 | tf_op jit(solution)/shard_map/cond/branch_4_fun/all_to_all | solution.py:262
  65.9 0.1 convert_reduce_fusion.4
  66.0 0.6 reshape.28
  (10 shorter events, 0.1 us)
Async XLA Ops:
  0.0 16.0 %collective-permute-start.2 = (bf16[4,128,1024]{2,1,0:T(8,128)(2,1)}, bf16[4,128,1024]{2,1,0:T(8,128)(2,1)S(1)}, u32[]{:S(2)}, u32[]{:S(2)}) collective-permute-start(bf16[4,128,1024]{2,1,0:T(8,128)(2,1)} %bitcast.12), channel_id=1, source_target_pairs={{64,0},{128,64},{192,128},{256,192},{320,256},{384,320},{448,384},... | collective-permute-start | bytes 3145736 | tf_op jit(solution)/shard_map/ppermute | solution.py:248
  7.5 20.6 %collective-permute-start.1 = (bf16[4,256,1024]{2,1,0:T(8,128)(2,1)S(1)}, bf16[4,256,1024]{2,1,0:T(8,128)(2,1)S(1)}, u32[]{:S(2)}, u32[]{:S(2)}) collective-permute-start(bf16[4,256,1024]{2,1,0:T(8,128)(2,1)S(1)} %get-tuple-element.24.own_ref), channel_id=1, source_target_pairs={{0,32},{32,0},{64,96},{96,64},{128,160},{160,128},{192,224},{224,1... | collective-permute-start | bytes 6291464 | tf_op jit(solution)/shard_map/ppermute | solution.py:250
  11.1 17.1 %collective-permute-start = (bf16[4,128,1024]{2,1,0:T(8,128)(2,1)S(1)}, bf16[4,128,1024]{2,1,0:T(8,128)(2,1)S(1)}, u32[]{:S(2)}, u32[]{:S(2)}) collective-permute-start(bf16[4,128,1024]{2,1,0:T(8,128)(2,1)S(1)} %get-tuple-element.23), channel_id=1, source_target_pairs={{0,64},{64,128},{128,192},{192,256},{256,320},{320,384},{384,448},... | collective-permute-start | bytes 3145736 | tf_op jit(solution)/shard_map/ppermute | solution.py:251
  18.9 9.3 %copy-start = (s32[12,2]{0,1:T(2,128)S(1)}, s32[12,2]{0,1:T(2,128)}, u32[]{:S(2)}) copy-start(s32[12,2]{0,1:T(2,128)} %param.9) | copy-start | bytes 292
  18.9 9.3 %collective-permute-start.3 = (bf16[4,256,1024]{2,1,0:T(8,128)(2,1)S(1)}, bf16[4,256,1024]{2,1,0:T(8,128)(2,1)S(1)}, u32[]{:S(2)}, u32[]{:S(2)}) collective-permute-start(bf16[4,256,1024]{2,1,0:T(8,128)(2,1)S(1)} %near.1.near_ref), channel_id=1, source_target_pairs={{0,32},{32,0},{64,96},{96,64},{128,160},{160,128},{192,224},{224,1... | collective-permute-start | bytes 6291464 | tf_op jit(solution)/shard_map/ppermute | solution.py:254

commit v11 on v10

--- a/solution.py
+++ b/solution.py
@@ -12,7 +12,7 @@
 ROWS_PERIOD = 16
 SPLIT = 32
 GROUPS = 5
-SLOTS_PER_STEP = 6
+SLOTS_PER_STEP = 4
 SLOTS_PER_GROUP = 2
 MIB = 1024 * 1024
 
@@ -135,38 +135,30 @@
 def last_kernel(
     slots_ref, x_ref, table_ref, own_ref, sibling_ref, near_ref, passed_ref, out_ref, group_ref, window_ref, sems
 ):
-    step = pl.program_id(0)
     blocks, channels, samples = x_ref.shape
-
-    @pl.when(step == 0)
-    def _():
-        parts = ((own_ref, 0), (sibling_ref, 1), (near_ref, 2), (passed_ref, 4))
-        copies = [
-            pltpu.make_async_copy(ref, window_ref.at[pl.ds(place * blocks, blocks)], sems.at[at])
-            for at, (ref, place) in enumerate(parts)
-        ]
-        for copy in copies:
-            copy.start()
-        whiten_all(x_ref, table_ref, window_ref.at[pl.ds(3 * blocks, blocks)])
-        for copy in copies:
-            copy.wait()
-
+    parts = ((own_ref, 0), (sibling_ref, 1), (near_ref, 2), (passed_ref, 4))
+    copies = [
+        pltpu.make_async_copy(ref, window_ref.at[pl.ds(place * blocks, blocks)], sems.at[at])
+        for at, (ref, place) in enumerate(parts)
+    ]
+    for copy in copies:
+        copy.start()
     group_ref[0] = sum(
         (slots_ref[0, slot] >= 0).astype(jnp.int32) for slot in range(SLOTS_PER_GROUP, slots_ref.shape[1], SLOTS_PER_GROUP)
     )
-
-    @pl.when((step > 0) & (slots_ref[0, jnp.maximum(step - 1, 0) * SLOTS_PER_STEP] >= 0))
-    def _():
-        owner = lax.axis_index("chan")
-
-        def place(block):
-            block = jnp.where(block >= 0, block, owner * blocks)
-            away = (lax.div(block, blocks) - owner) * (1 - 2 * lax.rem(owner, 2))
-            return lax.rem(away + GROUPS, GROUPS) * blocks + lax.rem(block, blocks)
-
+    whiten_all(x_ref, table_ref, window_ref.at[pl.ds(3 * blocks, blocks)])
+    for copy in copies:
+        copy.wait()
+    owner = lax.axis_index("chan")
+
+    def place(block):
+        block = jnp.where(block >= 0, block, owner * blocks)
+        away = (lax.div(block, blocks) - owner) * (1 - 2 * lax.rem(owner, 2))
+        return lax.rem(away + GROUPS, GROUPS) * blocks + lax.rem(block, blocks)
+
+    def pairs(start):
         found = []
-        for at in range(SLOTS_PER_STEP):
-            slot = (step - 1) * SLOTS_PER_STEP + at
+        for slot in range(start, start + SLOTS_PER_STEP):
             first, second = slots_ref[0, slot], slots_ref[1, slot]
             product = lax.dot_general(
                 window_ref[place(first)],
@@ -182,34 +174,28 @@
         for pair in range(SLOTS_PER_STEP // 2):
             first, second = found[2 * pair], found[2 * pair + 1]
             row = lax.broadcasted_iota(jnp.int32, first.shape, 1)
-            rows = slice(8 * pair, 8 * (pair + 1))
+            rows = slice(4 * start + 8 * pair, 4 * start + 8 * (pair + 1))
             out_ref[:, 0, rows] = jnp.where(row < 4, first, pltpu.roll(second, 4, 1))
             out_ref[:, 1, rows] = jnp.where(row < 4, pltpu.roll(first, 4, 1), second)
 
+    pairs(0)
+    for start in range(SLOTS_PER_STEP, slots_ref.shape[1], SLOTS_PER_STEP):
+        pl.when(slots_ref[0, start] >= 0)(functools.partial(pairs, start))
+
 
 def far_and_pairs(slots, x, table, own, sibling, near, passed):
     blocks, channels, samples = x.shape
     slot_count = slots.shape[0]
     return pl.pallas_call(
         last_kernel,
-        grid_spec=pltpu.PrefetchScalarGridSpec(
-            num_scalar_prefetch=1,
-            grid=(1 + slot_count // SLOTS_PER_STEP,),
-            in_specs=[HERE] * 6,
-            out_specs=[
-                pl.BlockSpec(
-                    (channels // 8, 2, 4 * SLOTS_PER_STEP, 2 * channels),
-                    lambda i, *_: (0, 0, jnp.maximum(i - 1, 0), 0),
-                ),
-                pl.BlockSpec(memory_space=pltpu.SMEM),
-            ],
-            scratch_shapes=[
-                pltpu.VMEM((GROUPS * blocks, 2 * channels, samples), jnp.bfloat16),
-                pltpu.SemaphoreType.DMA((4,)),
-            ],
-        ),
+        in_specs=[pl.BlockSpec(memory_space=pltpu.SMEM)] + [HERE] * 6,
+        out_specs=[HERE, pl.BlockSpec(memory_space=pltpu.SMEM)],
+        scratch_shapes=[
+            pltpu.VMEM((GROUPS * blocks, 2 * channels, samples), jnp.bfloat16),
+            pltpu.SemaphoreType.DMA((4,)),
+        ],
         out_shape=[
-            jax.ShapeDtypeStruct((channels // 8, 2, slot_count * 4, 2 * channels), jnp.float32),
+            pltpu.VMEM((channels // 8, 2, slot_count * 4, 2 * channels), jnp.float32),
             jax.ShapeDtypeStruct((1,), jnp.int32),
         ],
         compiler_params=pltpu.CompilerParams(vmem_limit_bytes=20 * MIB),

time: 66.9 us -> 69.3 us (1.036)
  the two profiles are of different devices: /device:TPU:41 before, /device:TPU:49 now
where the time goes in v11:
time: 69.3 us; the launch traced here: 68.1 us
  blocking collectives  31.6 us (46%)
  Pallas kernels  14 us (20%)
  starting transfers between devices  13.7 us (20%)
  waiting for transfers between devices  6.36 us (9%)
  other arithmetic  1.02 us (1%)
  between operations  0.77 us (1%)
    all_to_all x1, blocking collectives, summed(): arrived = lax.all_to_all(sent, 'tm', 0, 0, tiled=True)  31.6 us
    pallas_call x1, Pallas kernels, far_and_pairs(): pl.pallas_call(last_kernel, in_specs=[pl.BlockSpec(memory_space=pltpu.SME...  6.81 us
    ppermute x1, starting transfers between devices, on_device(): passed = lax.ppermute(near, 'chan', sibling_pairs)  4.89 us
    pallas_call x1, Pallas kernels, whiten_first(): pl.pallas_call(first_kernel, in_specs=[HERE, HERE, pl.BlockSpec(memory_sp...  4.37 us
    ppermute x1, waiting for transfers between devices, on_device(): far = lax.ppermute(again, 'chan', far_pairs)  4.36 us
    ppermute x1, starting transfers between devices, on_device(): sibling = lax.ppermute(own, 'chan', sibling_pairs)  3.53 us
    ppermute x1, starting transfers between devices, on_device(): far = lax.ppermute(again, 'chan', far_pairs)  2.98 us
    pallas_call x1, Pallas kernels, whiten_next(): pl.pallas_call(whiten_all, in_specs=[HERE] * 2, out_specs=HERE, out_shape...  2.8 us
  transfers between devices with their start and end apart: 4, of which 2 were waited for; matrix products, arithmetic and copies ran while one was open for 1% of the time, Pallas kernels for 11%

profile of v11, /device:TPU:49, one launch (start us, length us, event | category | flops | bytes accessed | tf_op | source)
XLA Modules:
  0.0 68.1 jit_solution(3211256691995784511)
XLA Ops:
  0.0 2.3 %collective-permute-start.2 = (bf16[4,128,1024]{2,1,0:T(8,128)(2,1)}, bf16[4,128,1024]{2,1,0:T(8,128)(2,1)S(1)}, u32[]{:S(2)}, u32[]{:S(2)}) collective-permute-start(bf16[4,128,1024]{2,1,0:T(8,128)(2,1)} %bitcast.12), channel_id=1, source_target_pairs={{64,0},{128,64},{192,128},{256,192},{320,256},{384,320},{448,384},... | collective-permute-start | bytes 3145736 | tf_op jit(solution)/shard_map/ppermute | solution.py:234
  2.4 0.7 %fusion.8 = (f32[256,128]{1,0:T(8,128)S(1)}, f32[256,128]{1,0:T(8,128)S(1)}) fusion(s32[256]{0:T(256)S(1)} %get-tuple-element.37, s32[256]{0:T(256)S(1)} %get-tuple-element.39, pred[256]{0:T(512)(128)(4,1)S(1)} %get-tuple-element.32, s32[256]{0:T(256)S(1)} %get-tuple-element.36, s32[256]{0:T(256)S(1)} %get-tuple-element.40, ...), kind=kLoop, calls=%fused_computation.35 | loop fusion | flops 1015808 | bytes 271872 | tf_op jit(solution)/shard_map/sin | solution.py:41
  3.1 4.4 %table_and_own.1 = (bf16[1024,2048]{1,0:T(8,128)(2,1)S(1)}, bf16[4,256,1024]{2,1,0:T(8,128)(2,1)S(1)}, bf16[4,128,1024]{2,1,0:T(8,128)(2,1)S(1)}) custom-call(f32[256,128]{1,0:T(8,128)S(1)} %get-tuple-element.29.cos_ref, f32[256,128]{1,0:T(8,128)S(1)} %get-tuple-element.28.sin_ref, bf16[4,128,1024]{2,1,0:T(8,128)(2,1)} %bitcast.13), custom_call_target="tpu_custom_call" | custom-call | flops 524288 | bytes 65536 | tf_op jit(solution)/shard_map/table_and_own/pallas_call | solution.py:106
  7.5 3.5 %collective-permute-start.1 = (bf16[4,256,1024]{2,1,0:T(8,128)(2,1)S(1)}, bf16[4,256,1024]{2,1,0:T(8,128)(2,1)S(1)}, u32[]{:S(2)}, u32[]{:S(2)}) collective-permute-start(bf16[4,256,1024]{2,1,0:T(8,128)(2,1)S(1)} %get-tuple-element.24.own_ref), channel_id=1, source_target_pairs={{0,32},{32,0},{64,96},{96,64},{128,160},{160,128},{192,224},{224,1... | collective-permute-start | bytes 6291464 | tf_op jit(solution)/shard_map/ppermute | solution.py:236
  11.1 3.0 %collective-permute-start = (bf16[4,128,1024]{2,1,0:T(8,128)(2,1)S(1)}, bf16[4,128,1024]{2,1,0:T(8,128)(2,1)S(1)}, u32[]{:S(2)}, u32[]{:S(2)}) collective-permute-start(bf16[4,128,1024]{2,1,0:T(8,128)(2,1)S(1)} %get-tuple-element.23), channel_id=1, source_target_pairs={{0,64},{64,128},{128,192},{192,256},{256,320},{320,384},{384,448},... | collective-permute-start | bytes 3145736 | tf_op jit(solution)/shard_map/ppermute | solution.py:237
  14.0 2.0 %collective-permute-done.2.x_ref = bf16[4,128,1024]{2,1,0:T(8,128)(2,1)S(1)} collective-permute-done((bf16[4,128,1024]{2,1,0:T(8,128)(2,1)}, bf16[4,128,1024]{2,1,0:T(8,128)(2,1)S(1)}, u32[]{:S(2)}, u32[]{:S(2)}) %collective-permute-start.2) | collective-permute-done | bytes 1048608 | tf_op jit(solution)/shard_map/ppermute | solution.py:234
  16.0 2.8 %near.1.near_ref = bf16[4,256,1024]{2,1,0:T(8,128)(2,1)S(1)} custom-call(bf16[4,128,1024]{2,1,0:T(8,128)(2,1)S(1)} %collective-permute-done.2.x_ref, bf16[1024,2048]{1,0:T(8,128)(2,1)S(1)} %get-tuple-element.25.table_ref), custom_call_target="tpu_custom_call" | custom-call | flops 16999999488 | bytes 65536 | tf_op jit(solution)/shard_map/near/pallas_call | solution.py:124
  18.9 0.0 copy-start
  18.9 4.9 %collective-permute-start.3 = (bf16[4,256,1024]{2,1,0:T(8,128)(2,1)S(1)}, bf16[4,256,1024]{2,1,0:T(8,128)(2,1)S(1)}, u32[]{:S(2)}, u32[]{:S(2)}) collective-permute-start(bf16[4,256,1024]{2,1,0:T(8,128)(2,1)S(1)} %near.1.near_ref), channel_id=1, source_target_pairs={{0,32},{32,0},{64,96},{96,64},{128,160},{160,128},{192,224},{224,1... | collective-permute-start | bytes 6291464 | tf_op jit(solution)/shard_map/ppermute | solution.py:240
  23.8 4.4 %collective-permute-done.x_ref = bf16[4,128,1024]{2,1,0:T(8,128)(2,1)S(1)} collective-permute-done((bf16[4,128,1024]{2,1,0:T(8,128)(2,1)S(1)}, bf16[4,128,1024]{2,1,0:T(8,128)(2,1)S(1)}, u32[]{:S(2)}, u32[]{:S(2)}) %collective-permute-start) | collective-permute-done | bytes 1048608 | tf_op jit(solution)/shard_map/ppermute | solution.py:237
  28.1 0.0 collective-permute-done.1.refs_0_.sibling_ref
  28.1 0.0 collective-permute-done.3.passed_ref
  28.1 0.0 copy-done
  28.1 6.8 %far_and_pairs.1 = (f32[16,2,48,256]{3,2,1,0:T(8,128)S(1)}, s32[1]{0:T(128)}) custom-call(s32[2,12]{1,0:T(2,128)S(1)} %bitcast.11, bf16[4,128,1024]{2,1,0:T(8,128)(2,1)S(1)} %far_arrived.1.x_ref, bf16[1024,2048]{1,0:T(8,128)(2,1)S(1)} %get-tuple-element.25.table_ref, bf16[4,256,1024]{2,1,0:T(8,128)(2,1)S(1)} %get-tuple-element.24.own_ref, ...), custom_call_target="tpu_custom_call" | custom-call | flops 1572864 | bytes 65536 | tf_op jit(solution)/shard_map/far_and_pairs/pallas_call | solution.py:189
  35.6 31.9 %conditional.1 = (f32[48,256]{1,0:T(8,128)S(1)}) conditional(s32[]{:T(128)} %bitcast.2, f32[32,48,256]{2,1,0:T(8,128)S(1)} %bitcast.5, f32[32,48,256]{2,1,0:T(8,128)S(1)} %bitcast.6, f32[32,48,256]{2,1,0:T(8,128)S(1)} %bitcast.7, f32[32,48,256]{2,1,0:T(8,128)S(1)} %bitcast.8, f32[32,48,256]{2,1,0:T(8,128)S(1)} %bitcast.9, ...), branch_computations={%region_0.2_spmd, %region_2.4_spmd, %region_4.6_spmd, %region_6.8_... | conditional | flops 1179648 | bytes 4866056 | solution.py:252
  35.6 0.1 slice_convert_fusion.4
  35.8 31.6 %all_to_all.28 = f16[32,40,256]{2,1,0:T(8,128)(2,1)S(1)} all-to-all(f16[32,40,256]{2,1,0:T(8,128)(2,1)S(1)} %slice_convert_fusion.4), channel_id=1, replica_groups=mesh['chan'=16,'tm'=32] {'tm'}, dimensions={0} | all-to-all | bytes 1310720 | tf_op jit(solution)/shard_map/cond/branch_4_fun/all_to_all | solution.py:248
  67.4 0.1 convert_reduce_fusion.4
  67.5 0.6 reshape.28
  (10 shorter events, 0.1 us)
Async XLA Ops:
  0.0 16.0 %collective-permute-start.2 = (bf16[4,128,1024]{2,1,0:T(8,128)(2,1)}, bf16[4,128,1024]{2,1,0:T(8,128)(2,1)S(1)}, u32[]{:S(2)}, u32[]{:S(2)}) collective-permute-start(bf16[4,128,1024]{2,1,0:T(8,128)(2,1)} %bitcast.12), channel_id=1, source_target_pairs={{64,0},{128,64},{192,128},{256,192},{320,256},{384,320},{448,384},... | collective-permute-start | bytes 3145736 | tf_op jit(solution)/shard_map/ppermute | solution.py:234
  7.5 20.6 %collective-permute-start.1 = (bf16[4,256,1024]{2,1,0:T(8,128)(2,1)S(1)}, bf16[4,256,1024]{2,1,0:T(8,128)(2,1)S(1)}, u32[]{:S(2)}, u32[]{:S(2)}) collective-permute-start(bf16[4,256,1024]{2,1,0:T(8,128)(2,1)S(1)} %get-tuple-element.24.own_ref), channel_id=1, source_target_pairs={{0,32},{32,0},{64,96},{96,64},{128,160},{160,128},{192,224},{224,1... | collective-permute-start | bytes 6291464 | tf_op jit(solution)/shard_map/ppermute | solution.py:236
  11.1 17.1 %collective-permute-start = (bf16[4,128,1024]{2,1,0:T(8,128)(2,1)S(1)}, bf16[4,128,1024]{2,1,0:T(8,128)(2,1)S(1)}, u32[]{:S(2)}, u32[]{:S(2)}) collective-permute-start(bf16[4,128,1024]{2,1,0:T(8,128)(2,1)S(1)} %get-tuple-element.23), channel_id=1, source_target_pairs={{0,64},{64,128},{128,192},{192,256},{256,320},{320,384},{384,448},... | collective-permute-start | bytes 3145736 | tf_op jit(solution)/shard_map/ppermute | solution.py:237
  18.9 9.3 %copy-start = (s32[12,2]{0,1:T(2,128)S(1)}, s32[12,2]{0,1:T(2,128)}, u32[]{:S(2)}) copy-start(s32[12,2]{0,1:T(2,128)} %param.9) | copy-start | bytes 292
  18.9 9.3 %collective-permute-start.3 = (bf16[4,256,1024]{2,1,0:T(8,128)(2,1)S(1)}, bf16[4,256,1024]{2,1,0:T(8,128)(2,1)S(1)}, u32[]{:S(2)}, u32[]{:S(2)}) collective-permute-start(bf16[4,256,1024]{2,1,0:T(8,128)(2,1)S(1)} %near.1.near_ref), channel_id=1, source_target_pairs={{0,32},{32,0},{64,96},{96,64},{128,160},{160,128},{192,224},{224,1... | collective-permute-start | bytes 6291464 | tf_op jit(solution)/shard_map/ppermute | solution.py:240

commit v12 on v11

--- a/solution.py
+++ b/solution.py
@@ -246,7 +246,7 @@
     def summed(slots, products):
         sent = products[:, : slots * rows].astype(jnp.float16)
         arrived = lax.all_to_all(sent, "tm", 0, 0, tiled=True)
-        total = jnp.sum(arrived.astype(jnp.float32), axis=0) * (4.0 / (samples * windows))
+        total = jnp.sum(arrived.astype(jnp.float32) * (4.0 / (samples * windows)), axis=0)
         return jnp.pad(total, ((0, (slot_count - slots) * rows), (0, 0)))
 
     total = lax.switch(

time: 69.3 us -> 69.2 us (level)
  the two profiles are of different devices: /device:TPU:49 before, /device:TPU:9 now
where the time goes in v12:
time: 69.2 us; the launch traced here: 68.9 us
  blocking collectives  28.5 us (41%)
  starting transfers between devices  20.2 us (29%)
  Pallas kernels  14 us (20%)
  waiting for transfers between devices  3.76 us (5%)
  other arithmetic  1.05 us (2%)
  between operations  0.77 us (1%)
    all_to_all x1, blocking collectives, summed(): arrived = lax.all_to_all(sent, 'tm', 0, 0, tiled=True)  28.5 us
    ppermute x1, starting transfers between devices, on_device(): passed = lax.ppermute(near, 'chan', sibling_pairs)  7.97 us
    ppermute x1, starting transfers between devices, on_device(): sibling = lax.ppermute(own, 'chan', sibling_pairs)  7.11 us
    pallas_call x1, Pallas kernels, far_and_pairs(): pl.pallas_call(last_kernel, in_specs=[pl.BlockSpec(memory_space=pltpu.SME...  6.81 us
    pallas_call x1, Pallas kernels, whiten_first(): pl.pallas_call(first_kernel, in_specs=[HERE, HERE, pl.BlockSpec(memory_sp...  4.37 us
    ppermute x1, waiting for transfers between devices, on_device(): far = lax.ppermute(again, 'chan', far_pairs)  3.49 us
    ppermute x1, starting transfers between devices, on_device(): near = lax.ppermute(x, 'chan', near_pairs)  3.19 us
    pallas_call x1, Pallas kernels, whiten_next(): pl.pallas_call(whiten_all, in_specs=[HERE] * 2, out_specs=HERE, out_shape...  2.8 us
  transfers between devices with their start and end apart: 4, of which 2 were waited for; matrix products, arithmetic and copies ran while one was open for 1% of the time, Pallas kernels for 10%

profile of v12, /device:TPU:9, one launch (start us, length us, event | category | flops | bytes accessed | tf_op | source)
XLA Modules:
  0.0 68.9 jit_solution(1583651959368395023)
XLA Ops:
  0.0 3.2 %collective-permute-start.2 = (bf16[4,128,1024]{2,1,0:T(8,128)(2,1)}, bf16[4,128,1024]{2,1,0:T(8,128)(2,1)S(1)}, u32[]{:S(2)}, u32[]{:S(2)}) collective-permute-start(bf16[4,128,1024]{2,1,0:T(8,128)(2,1)} %bitcast.12), channel_id=1, source_target_pairs={{64,0},{128,64},{192,128},{256,192},{320,256},{384,320},{448,384},... | collective-permute-start | bytes 3145736 | tf_op jit(solution)/shard_map/ppermute | solution.py:234
  3.3 0.7 %fusion.8 = (f32[256,128]{1,0:T(8,128)S(1)}, f32[256,128]{1,0:T(8,128)S(1)}) fusion(s32[256]{0:T(256)S(1)} %get-tuple-element.37, s32[256]{0:T(256)S(1)} %get-tuple-element.39, pred[256]{0:T(512)(128)(4,1)S(1)} %get-tuple-element.32, s32[256]{0:T(256)S(1)} %get-tuple-element.36, s32[256]{0:T(256)S(1)} %get-tuple-element.40, ...), kind=kLoop, calls=%fused_computation.29 | loop fusion | flops 1015808 | bytes 271872 | tf_op jit(solution)/shard_map/sin | solution.py:41
  4.0 4.4 %table_and_own.1 = (bf16[1024,2048]{1,0:T(8,128)(2,1)S(1)}, bf16[4,256,1024]{2,1,0:T(8,128)(2,1)S(1)}, bf16[4,128,1024]{2,1,0:T(8,128)(2,1)S(1)}) custom-call(f32[256,128]{1,0:T(8,128)S(1)} %get-tuple-element.29.cos_ref, f32[256,128]{1,0:T(8,128)S(1)} %get-tuple-element.28.sin_ref, bf16[4,128,1024]{2,1,0:T(8,128)(2,1)} %bitcast.13), custom_call_target="tpu_custom_call" | custom-call | flops 524288 | bytes 65536 | tf_op jit(solution)/shard_map/table_and_own/pallas_call | solution.py:106
  8.4 7.1 %collective-permute-start.1 = (bf16[4,256,1024]{2,1,0:T(8,128)(2,1)S(1)}, bf16[4,256,1024]{2,1,0:T(8,128)(2,1)S(1)}, u32[]{:S(2)}, u32[]{:S(2)}) collective-permute-start(bf16[4,256,1024]{2,1,0:T(8,128)(2,1)S(1)} %get-tuple-element.24.own_ref), channel_id=1, source_target_pairs={{0,32},{32,0},{64,96},{96,64},{128,160},{160,128},{192,224},{224,1... | collective-permute-start | bytes 6291464 | tf_op jit(solution)/shard_map/ppermute | solution.py:236
  15.5 1.9 %collective-permute-start = (bf16[4,128,1024]{2,1,0:T(8,128)(2,1)S(1)}, bf16[4,128,1024]{2,1,0:T(8,128)(2,1)S(1)}, u32[]{:S(2)}, u32[]{:S(2)}) collective-permute-start(bf16[4,128,1024]{2,1,0:T(8,128)(2,1)S(1)} %get-tuple-element.23), channel_id=1, source_target_pairs={{0,64},{64,128},{128,192},{192,256},{256,320},{320,384},{384,448},... | collective-permute-start | bytes 3145736 | tf_op jit(solution)/shard_map/ppermute | solution.py:237
  17.5 0.0 collective-permute-done.2.x_ref
  17.5 2.8 %near.1.near_ref = bf16[4,256,1024]{2,1,0:T(8,128)(2,1)S(1)} custom-call(bf16[4,128,1024]{2,1,0:T(8,128)(2,1)S(1)} %collective-permute-done.2.x_ref, bf16[1024,2048]{1,0:T(8,128)(2,1)S(1)} %get-tuple-element.25.table_ref), custom_call_target="tpu_custom_call" | custom-call | flops 16999999488 | bytes 65536 | tf_op jit(solution)/shard_map/near/pallas_call | solution.py:124
  20.3 0.0 copy-start
  20.3 8.0 %collective-permute-start.3 = (bf16[4,256,1024]{2,1,0:T(8,128)(2,1)S(1)}, bf16[4,256,1024]{2,1,0:T(8,128)(2,1)S(1)}, u32[]{:S(2)}, u32[]{:S(2)}) collective-permute-start(bf16[4,256,1024]{2,1,0:T(8,128)(2,1)S(1)} %near.1.near_ref), channel_id=1, source_target_pairs={{0,32},{32,0},{64,96},{96,64},{128,160},{160,128},{192,224},{224,1... | collective-permute-start | bytes 6291464 | tf_op jit(solution)/shard_map/ppermute | solution.py:240
  28.3 3.5 %collective-permute-done.x_ref = bf16[4,128,1024]{2,1,0:T(8,128)(2,1)S(1)} collective-permute-done((bf16[4,128,1024]{2,1,0:T(8,128)(2,1)S(1)}, bf16[4,128,1024]{2,1,0:T(8,128)(2,1)S(1)}, u32[]{:S(2)}, u32[]{:S(2)}) %collective-permute-start) | collective-permute-done | bytes 1048608 | tf_op jit(solution)/shard_map/ppermute | solution.py:237
  31.8 0.0 collective-permute-done.1.refs_0_.sibling_ref
  31.8 0.3 collective-permute-done.3.passed_ref
  32.0 0.0 copy-done
  32.0 6.8 %far_and_pairs.1 = (f32[16,2,48,256]{3,2,1,0:T(8,128)S(1)}, s32[1]{0:T(128)}) custom-call(s32[2,12]{1,0:T(2,128)S(1)} %bitcast.11, bf16[4,128,1024]{2,1,0:T(8,128)(2,1)S(1)} %far_arrived.1.x_ref, bf16[1024,2048]{1,0:T(8,128)(2,1)S(1)} %get-tuple-element.25.table_ref, bf16[4,256,1024]{2,1,0:T(8,128)(2,1)S(1)} %get-tuple-element.24.own_ref, ...), custom_call_target="tpu_custom_call" | custom-call | flops 1572864 | bytes 65536 | tf_op jit(solution)/shard_map/far_and_pairs/pallas_call | solution.py:189
  39.5 28.8 %conditional.1 = (f32[48,256]{1,0:T(8,128)S(1)}) conditional(s32[]{:T(128)} %bitcast.2, f32[32,48,256]{2,1,0:T(8,128)S(1)} %bitcast.5, f32[32,48,256]{2,1,0:T(8,128)S(1)} %bitcast.6, f32[32,48,256]{2,1,0:T(8,128)S(1)} %bitcast.7, f32[32,48,256]{2,1,0:T(8,128)S(1)} %bitcast.8, f32[32,48,256]{2,1,0:T(8,128)S(1)} %bitcast.9, ...), branch_computations={%region_0.2_spmd, %region_2.4_spmd, %region_4.6_spmd, %region_6.8_... | conditional | flops 1560576 | bytes 4767752 | solution.py:252
  39.5 0.1 slice_convert_fusion.4
  39.7 28.5 %all_to_all.28 = f16[32,40,256]{2,1,0:T(8,128)(2,1)S(1)} all-to-all(f16[32,40,256]{2,1,0:T(8,128)(2,1)S(1)} %slice_convert_fusion.4), channel_id=1, replica_groups=mesh['chan'=16,'tm'=32] {'tm'}, dimensions={0} | all-to-all | bytes 1310720 | tf_op jit(solution)/shard_map/cond/branch_4_fun/all_to_all | solution.py:248
  68.1 0.1 multiply_reduce_fusion.4
  68.3 0.6 reshape.28
  (9 shorter events, 0.1 us)
Async XLA Ops:
  0.0 17.5 %collective-permute-start.2 = (bf16[4,128,1024]{2,1,0:T(8,128)(2,1)}, bf16[4,128,1024]{2,1,0:T(8,128)(2,1)S(1)}, u32[]{:S(2)}, u32[]{:S(2)}) collective-permute-start(bf16[4,128,1024]{2,1,0:T(8,128)(2,1)} %bitcast.12), channel_id=1, source_target_pairs={{64,0},{128,64},{192,128},{256,192},{320,256},{384,320},{448,384},... | collective-permute-start | bytes 3145736 | tf_op jit(solution)/shard_map/ppermute | solution.py:234
  8.4 23.3 %collective-permute-start.1 = (bf16[4,256,1024]{2,1,0:T(8,128)(2,1)S(1)}, bf16[4,256,1024]{2,1,0:T(8,128)(2,1)S(1)}, u32[]{:S(2)}, u32[]{:S(2)}) collective-permute-start(bf16[4,256,1024]{2,1,0:T(8,128)(2,1)S(1)} %get-tuple-element.24.own_ref), channel_id=1, source_target_pairs={{0,32},{32,0},{64,96},{96,64},{128,160},{160,128},{192,224},{224,1... | collective-permute-start | bytes 6291464 | tf_op jit(solution)/shard_map/ppermute | solution.py:236
  15.5 16.2 %collective-permute-start = (bf16[4,128,1024]{2,1,0:T(8,128)(2,1)S(1)}, bf16[4,128,1024]{2,1,0:T(8,128)(2,1)S(1)}, u32[]{:S(2)}, u32[]{:S(2)}) collective-permute-start(bf16[4,128,1024]{2,1,0:T(8,128)(2,1)S(1)} %get-tuple-element.23), channel_id=1, source_target_pairs={{0,64},{64,128},{128,192},{192,256},{256,320},{320,384},{384,448},... | collective-permute-start | bytes 3145736 | tf_op jit(solution)/shard_map/ppermute | solution.py:237
  20.3 11.8 %copy-start = (s32[12,2]{0,1:T(2,128)S(1)}, s32[12,2]{0,1:T(2,128)}, u32[]{:S(2)}) copy-start(s32[12,2]{0,1:T(2,128)} %param.9) | copy-start | bytes 292
  20.3 11.7 %collective-permute-start.3 = (bf16[4,256,1024]{2,1,0:T(8,128)(2,1)S(1)}, bf16[4,256,1024]{2,1,0:T(8,128)(2,1)S(1)}, u32[]{:S(2)}, u32[]{:S(2)}) collective-permute-start(bf16[4,256,1024]{2,1,0:T(8,128)(2,1)S(1)} %near.1.near_ref), channel_id=1, source_target_pairs={{0,32},{32,0},{64,96},{96,64},{128,160},{160,128},{192,224},{224,1... | collective-permute-start | bytes 6291464 | tf_op jit(solution)/shard_map/ppermute | solution.py:240
